TPU v7x, 32 devices: a whole 2x2x4 slice. The times are simulated.
32 devices in a mesh: grp: 4 (over x, core), wide: 8 (over z, y).
Axes of the slice: x: 2, y: 2, z: 4, core: 2. Of those that a mesh axis runs over, the one named last changes fastest.
Arguments:
- byte_ids: int32 [16384], P(('grp', 'wide')), may hold values from 0 to 255
- item_lengths: int32 [32], P(('grp', 'wide')), may hold values from 113 to 512, as said below
- embed_table: bfloat16 [256, 768], P('grp'), may hold values from -6 to 6
- patch_weight: bfloat16 [6144, 768], P('grp'), may hold values from -0.078125 to 0.078125
- patch_bias: float32 [768], replicated, may hold values from -3 to 3
- norm_gain: float32 [2, 2, 768], replicated, may hold values from 0.1 to 1.9
- norm_bias: float32 [2, 2, 768], replicated, may hold values from -3 to 3
- qkv_weight: bfloat16 [2, 3, 768, 768], P(None, None, 'grp'), may hold values from -0.21875 to 0.21875
- out_weight: bfloat16 [2, 768, 768], P(None, 'grp'), may hold values from -0.625 to 0.625
- up_weight: bfloat16 [2, 768, 3072], P(None, 'grp'), may hold values from -0.21875 to 0.21875
- up_bias: float32 [2, 3072], replicated, may hold values from -3 to 3
- down_weight: bfloat16 [2, 3072, 768], P(None, 'grp'), may hold values from -0.109375 to 0.109375
- down_bias: float32 [2, 768], replicated, may hold values from -3 to 3
- out_cot: bfloat16 [16384, 768], P(('grp', 'wide')), may hold values from -6 to 6
Outputs:
- local_out: bfloat16 [16384, 768], P(('grp', 'wide'))
- embed_rows_grad: bfloat16 [16384, 768], P(('grp', 'wide'))
- embed_table_grad: float32 [256, 768], P('grp', 'wide')
- patch_weight_grad: float32 [6144, 768], P('grp', 'wide')
- patch_bias_grad: float32 [768], replicated
- norm_gain_grad: float32 [2, 2, 768], replicated
- norm_bias_grad: float32 [2, 2, 768], replicated
- qkv_weight_grad: float32 [2, 3, 768, 768], P(None, None, 'grp', 'wide')
- out_weight_grad: float32 [2, 768, 768], P(None, 'grp', 'wide')
- up_weight_grad: float32 [2, 768, 3072], P(None, 'grp', 'wide')
- up_bias_grad: float32 [2, 3072], replicated
- down_weight_grad: float32 [2, 3072, 768], P(None, 'grp', 'wide')
- down_bias_grad: float32 [2, 768], replicated
Inputs may be any that keep to these rules, and one draw needn't show every extreme that they name: `item_lengths`: A tile is 16 consecutive bytes of an item; an item of length L has ceil(L / 16) tiles that hold valid bytes. The 8 items with one grp index have exactly 160 such tiles together, and among them some item is full, in every draw.
All inputs are finite; a program needn't handle non-finite values.
Results may differ from a plain program's by a relative error of at most 0.019.
Values may be sent and summed in bfloat16 or wider, within the bound.
No kernel may reach another device: no remote copies, remote signals or barrier semaphores. Data moves between devices by JAX's collectives and lax.ppermute only.
A program may use at most 384 MiB of HBM per device.

v0:
```python
import jax
import jax.numpy as jnp
from jax import lax
from jax.sharding import PartitionSpec as P

HEADS = 12
HEAD_DIM = 64
PATCH = 8
TILE = 2
RECV_TILES = 20


NORM_EPS = 1e-05
MASK_FILL = -1e30


def product(left, right):
    return jnp.dot(left, right, preferred_element_type=jnp.float32)


def weight_term(left, right):
    return lax.dot_general(
        left, right, (((0,), (0,)), ((), ())), preferred_element_type=jnp.float32
    )


def back_product(left, right):
    return lax.dot_general(
        left, right, (((1,), (1,)), ((), ())), preferred_element_type=jnp.float32
    )


def layer_norm(hidden, gain, bias):
    centered = hidden - jnp.mean(hidden, axis=-1, keepdims=True)
    spread = jnp.mean(centered * centered, axis=-1, keepdims=True)
    return centered * lax.rsqrt(spread + NORM_EPS) * gain + bias


def masked_softmax(scores):
    span = scores.shape[-1]
    rows_index = lax.broadcasted_iota(jnp.int32, (span, span), 0)
    cols_index = lax.broadcasted_iota(jnp.int32, (span, span), 1)
    return jax.nn.softmax(jnp.where(cols_index <= rows_index, scores, MASK_FILL), axis=-1)


def gelu_tanh(upper):
    return jax.nn.gelu(upper, approximate=True)


def split_heads(hidden, span):
    return hidden.reshape(hidden.shape[0] // span, span, HEADS, HEAD_DIM)


def to_blocks(term, groups, shards):
    lead = term.shape[:-2]
    rows, cols = (term.shape[-2], term.shape[-1])
    split = term.reshape(lead + (groups, rows // groups, shards, cols // shards))
    count = len(lead)
    moved = jnp.moveaxis(split, (count, count + 2), (0, 1))
    return moved.reshape(-1)


def from_blocks(flat, shape, groups, shards):
    return flat.reshape(tuple(shape[:-2]) + (shape[-2] // groups, shape[-1] // shards))


def block_forward(hidden, weights, span):
    gains, biases, w_qkv, w_out, w_up, b_up, w_down, b_down = weights
    rows_total = hidden.shape[0]
    normed_one = layer_norm(hidden, gains[0], biases[0]).astype(jnp.bfloat16)
    query = split_heads(product(normed_one, w_qkv[0]).astype(jnp.bfloat16), span)
    keyed = split_heads(product(normed_one, w_qkv[1]).astype(jnp.bfloat16), span)
    valued = split_heads(product(normed_one, w_qkv[2]).astype(jnp.bfloat16), span)
    score_scale = HEAD_DIM ** (-0.5)
    scores = (
        jnp.einsum("glhd,gmhd->ghlm", query, keyed, preferred_element_type=jnp.float32)
        * score_scale
    )
    probs = masked_softmax(scores).astype(jnp.bfloat16)
    mixed = jnp.einsum("ghlm,gmhd->glhd", probs, valued, preferred_element_type=jnp.float32)
    mixed = mixed.reshape(rows_total, -1).astype(jnp.bfloat16)
    middle = hidden + product(mixed, w_out)
    normed_two = layer_norm(middle, gains[1], biases[1]).astype(jnp.bfloat16)
    upper = product(normed_two, w_up) + b_up
    active = gelu_tanh(upper).astype(jnp.bfloat16)
    return middle + (product(active, w_down) + b_down)


def block_backward(hidden, grad_out, weights, span):
    gains, biases, w_qkv, w_out, w_up, b_up, w_down, b_down = weights
    rows_total = hidden.shape[0]
    norm_one_value, norm_one_back = jax.vjp(layer_norm, hidden, gains[0], biases[0])
    normed_one = norm_one_value.astype(jnp.bfloat16)
    query = split_heads(product(normed_one, w_qkv[0]).astype(jnp.bfloat16), span)
    keyed = split_heads(product(normed_one, w_qkv[1]).astype(jnp.bfloat16), span)
    valued = split_heads(product(normed_one, w_qkv[2]).astype(jnp.bfloat16), span)
    score_scale = HEAD_DIM ** (-0.5)
    scores = (
        jnp.einsum("glhd,gmhd->ghlm", query, keyed, preferred_element_type=jnp.float32)
        * score_scale
    )
    probs_value, soft_back = jax.vjp(masked_softmax, scores)
    probs = probs_value.astype(jnp.bfloat16)
    mixed = jnp.einsum("ghlm,gmhd->glhd", probs, valued, preferred_element_type=jnp.float32)
    mixed = mixed.reshape(rows_total, -1).astype(jnp.bfloat16)
    middle = hidden + product(mixed, w_out)
    norm_two_value, norm_two_back = jax.vjp(layer_norm, middle, gains[1], biases[1])
    normed_two = norm_two_value.astype(jnp.bfloat16)
    upper = product(normed_two, w_up) + b_up
    active_value, gelu_back = jax.vjp(gelu_tanh, upper)
    active = active_value.astype(jnp.bfloat16)
    grad_down = grad_out.astype(jnp.bfloat16)
    down_bias_term = jnp.sum(grad_down.astype(jnp.float32), axis=0)
    down_term = weight_term(active, grad_down)
    grad_upper = gelu_back(back_product(grad_down, w_down))[0].astype(jnp.bfloat16)
    up_bias_term = jnp.sum(grad_upper.astype(jnp.float32), axis=0)
    up_term = weight_term(normed_two, grad_upper)
    grad_norm_two, gain_two_term, bias_two_term = norm_two_back(back_product(grad_upper, w_up))
    grad_middle = grad_out + grad_norm_two
    grad_branch = grad_middle.astype(jnp.bfloat16)
    out_term = weight_term(mixed, grad_branch)
    grad_mixed = back_product(grad_branch, w_out).astype(jnp.bfloat16)
    grad_heads = split_heads(grad_mixed, span)
    grad_probs = jnp.einsum(
        "glhd,gmhd->ghlm", grad_heads, valued, preferred_element_type=jnp.float32
    )
    grad_value = jnp.einsum(
        "ghlm,glhd->gmhd", probs, grad_heads, preferred_element_type=jnp.float32
    )
    grad_value = grad_value.reshape(rows_total, -1).astype(jnp.bfloat16)
    grad_scores = soft_back(grad_probs)[0].astype(jnp.bfloat16)
    grad_query = (
        jnp.einsum("ghlm,gmhd->glhd", grad_scores, keyed, preferred_element_type=jnp.float32)
        * score_scale
    )
    grad_query = grad_query.reshape(rows_total, -1).astype(jnp.bfloat16)
    grad_key = (
        jnp.einsum("ghlm,glhd->gmhd", grad_scores, query, preferred_element_type=jnp.float32)
        * score_scale
    )
    grad_key = grad_key.reshape(rows_total, -1).astype(jnp.bfloat16)
    qkv_term = jnp.stack(
        [
            weight_term(normed_one, grad_query),
            weight_term(normed_one, grad_key),
            weight_term(normed_one, grad_value),
        ]
    )
    grad_normed = (
        back_product(grad_query, w_qkv[0])
        + back_product(grad_key, w_qkv[1])
        + back_product(grad_value, w_qkv[2])
    )
    grad_norm_one, gain_one_term, bias_one_term = norm_one_back(grad_normed)
    grad_hidden = grad_middle + grad_norm_one
    gain_term = jnp.stack([gain_one_term, gain_two_term])
    bias_term = jnp.stack([bias_one_term, bias_two_term])
    return (
        grad_hidden,
        (
            gain_term,
            bias_term,
            qkv_term,
            out_term,
            up_term,
            up_bias_term,
            down_term,
            down_bias_term,
        ),
    )


def body(
    byte_ids,
    item_lengths,
    embed_table,
    patch_weight,
    patch_bias,
    norm_gain,
    norm_bias,
    qkv_weight,
    out_weight,
    up_weight,
    up_bias,
    down_weight,
    down_bias,
    out_cot,
):
    gathered = (
        lax.all_gather(embed_table, "grp", axis=0, tiled=True),
        lax.all_gather(patch_weight, "grp", axis=0, tiled=True),
        lax.all_gather(qkv_weight, "grp", axis=2, tiled=True),
        lax.all_gather(out_weight, "grp", axis=1, tiled=True),
        lax.all_gather(up_weight, "grp", axis=1, tiled=True),
        lax.all_gather(down_weight, "grp", axis=1, tiled=True),
    )
    embed_full, patch_full, qkv_full, out_full, up_full, down_full = gathered
    byte_count = byte_ids.shape[0]
    model_width = embed_full.shape[1]
    patch_count = byte_count // PATCH
    positions = lax.broadcasted_iota(jnp.int32, (byte_count, 1), 0)
    byte_keep = (positions < item_lengths[0]).astype(jnp.float32)
    vocab_index = lax.broadcasted_iota(jnp.int32, (1, embed_full.shape[0]), 1)
    one_hot = ((byte_ids[:, None] == vocab_index).astype(jnp.float32) * byte_keep).astype(
        jnp.bfloat16
    )
    embedded = product(one_hot, embed_full)
    patches = embedded.astype(jnp.bfloat16).reshape(patch_count, PATCH * model_width)
    summary = product(patches, patch_full) + patch_bias
    global_weights = (
        norm_gain[0],
        norm_bias[0],
        qkv_full[0],
        out_full[0],
        up_full[0],
        up_bias[0],
        down_full[0],
        down_bias[0],
    )
    local_weights = (
        norm_gain[1],
        norm_bias[1],
        qkv_full[1],
        out_full[1],
        up_full[1],
        up_bias[1],
        down_full[1],
        down_bias[1],
    )
    global_out = block_forward(summary, global_weights, patch_count)
    local_in = (
        (embedded.reshape(patch_count, PATCH, model_width) + global_out[:, None, :])
        .reshape(byte_count, model_width)
        .astype(jnp.bfloat16)
    )
    cot_masked = (out_cot.astype(jnp.float32) * byte_keep).astype(jnp.bfloat16)
    shards = lax.axis_size("wide")
    groups = lax.axis_size("grp")
    tile_height = TILE * PATCH
    tile_slots = byte_count // tile_height
    depth = tile_slots // shards
    tile_total = (item_lengths + tile_height - 1) // tile_height
    all_counts = lax.all_gather(tile_total, "wide", axis=0, tiled=True)
    starts = jnp.cumsum(all_counts) - all_counts
    my_index = lax.axis_index("wide")
    my_start = starts[my_index] % shards
    depth_index = lax.broadcasted_iota(jnp.int32, (depth, shards), 0)
    first_tile = (my_index - starts[None, :]) % shards
    tile_number = first_tile + shards * depth_index
    live = tile_number < all_counts[None, :]
    slot_number = (starts[None, :] + tile_number) // shards
    recv_index = lax.broadcasted_iota(jnp.int32, (RECV_TILES, 1, 1), 0)
    selector = (
        ((slot_number[None] == recv_index) & live[None])
        .astype(jnp.bfloat16)
        .reshape(RECV_TILES, depth * shards)
    )

    def spread_tiles(rows):
        return jnp.roll(rows.reshape(depth, shards, tile_height, model_width), my_start, axis=1)

    def unspread_tiles(tiles):
        return jnp.roll(tiles, -my_start, axis=1).reshape(byte_count, model_width)

    def compact_tiles(received):
        packed = product(selector, received.reshape(depth * shards, tile_height * model_width))
        return packed.astype(jnp.bfloat16).reshape(RECV_TILES * tile_height, model_width)

    def expand_tiles(rows):
        spread_back = weight_term(selector, rows.reshape(RECV_TILES, tile_height * model_width))
        return spread_back.astype(jnp.bfloat16).reshape(depth, shards, tile_height, model_width)

    sent_in = spread_tiles(local_in)
    arrived_in = lax.all_to_all(sent_in, "wide", split_axis=1, concat_axis=1, tiled=True)
    decoded = block_forward(
        compact_tiles(arrived_in).astype(jnp.float32), local_weights, PATCH
    ).astype(jnp.bfloat16)
    returned = lax.all_to_all(
        expand_tiles(decoded), "wide", split_axis=1, concat_axis=1, tiled=True
    )
    local_low = unspread_tiles(returned)
    local_out = (local_low.astype(jnp.float32) * byte_keep).astype(jnp.bfloat16)
    arrived = (
        lax.all_to_all(sent_in, "wide", split_axis=1, concat_axis=1, tiled=True),
        lax.all_to_all(spread_tiles(cot_masked), "wide", split_axis=1, concat_axis=1, tiled=True),
    )
    grad_rows, local_grads = block_backward(
        compact_tiles(arrived[0]).astype(jnp.float32),
        compact_tiles(arrived[1]).astype(jnp.float32),
        local_weights,
        PATCH,
    )
    grad_back = expand_tiles(grad_rows.astype(jnp.bfloat16))
    grad_local = unspread_tiles(
        lax.all_to_all(grad_back, "wide", split_axis=1, concat_axis=1, tiled=True)
    )
    grad_global = jnp.sum(
        grad_local.astype(jnp.float32).reshape(patch_count, PATCH, model_width), axis=1
    )
    grad_summary, global_grads = block_backward(summary, grad_global, global_weights, patch_count)
    grad_summary_low = grad_summary.astype(jnp.bfloat16)
    patch_bias_term = jnp.sum(grad_summary_low.astype(jnp.float32), axis=0)
    patch_weight_term = weight_term(patches, grad_summary_low)
    grad_patches = back_product(grad_summary_low, patch_full).reshape(byte_count, model_width)
    embed_rows_grad = (grad_local.astype(jnp.float32) + grad_patches).astype(jnp.bfloat16)
    table_term = weight_term(one_hot, embed_rows_grad)
    stacked = [
        jnp.stack([global_part, local_part])
        for global_part, local_part in zip(global_grads, local_grads)
    ]
    gain_term, bias_term, qkv_term, out_term, up_term, up_bias_term, down_term, down_bias_term = (
        stacked
    )
    matrices = (table_term, patch_weight_term, qkv_term, out_term, up_term, down_term)
    blocked = tuple((to_blocks(entry, groups, shards) for entry in matrices))
    shares = (
        lax.psum_scatter(blocked[0], ("grp", "wide"), scatter_dimension=0, tiled=True),
        lax.psum_scatter(blocked[1], ("grp", "wide"), scatter_dimension=0, tiled=True),
        lax.psum_scatter(blocked[2], ("grp", "wide"), scatter_dimension=0, tiled=True),
        lax.psum_scatter(blocked[3], ("grp", "wide"), scatter_dimension=0, tiled=True),
        lax.psum_scatter(blocked[4], ("grp", "wide"), scatter_dimension=0, tiled=True),
        lax.psum_scatter(blocked[5], ("grp", "wide"), scatter_dimension=0, tiled=True),
    )
    vectors = lax.psum(
        (patch_bias_term, gain_term, bias_term, up_bias_term, down_bias_term), ("grp", "wide")
    )
    embed_table_grad = from_blocks(shares[0], table_term.shape, groups, shards)
    patch_weight_grad = from_blocks(shares[1], patch_weight_term.shape, groups, shards)
    qkv_weight_grad = from_blocks(shares[2], qkv_term.shape, groups, shards)
    out_weight_grad = from_blocks(shares[3], out_term.shape, groups, shards)
    up_weight_grad = from_blocks(shares[4], up_term.shape, groups, shards)
    down_weight_grad = from_blocks(shares[5], down_term.shape, groups, shards)
    return (
        local_out,
        embed_rows_grad,
        embed_table_grad,
        patch_weight_grad,
        vectors[0],
        vectors[1],
        vectors[2],
        qkv_weight_grad,
        out_weight_grad,
        up_weight_grad,
        vectors[3],
        down_weight_grad,
        vectors[4],
    )


def solution(mesh):
    placed = (
        P(("grp", "wide")),
        P(("grp", "wide")),
        P("grp", None),
        P("grp", None),
        P(),
        P(),
        P(),
        P(None, None, "grp", None),
        P(None, "grp", None),
        P(None, "grp", None),
        P(),
        P(None, "grp", None),
        P(),
        P(("grp", "wide"), None),
    )
    return jax.shard_map(
        body,
        mesh=mesh,
        in_specs=placed,
        out_specs=(
            P(("grp", "wide"), None),
            P(("grp", "wide"), None),
            P("grp", "wide"),
            P("grp", "wide"),
            P(),
            P(),
            P(),
            P(None, None, "grp", "wide"),
            P(None, "grp", "wide"),
            P(None, "grp", "wide"),
            P(),
            P(None, "grp", "wide"),
            P(),
        ),
        check_vma=False,
    )
```

profile of v0, /device:TPU:0, one launch (start us, length us, event | category | flops | bytes accessed | tf_op | source)
XLA Modules:
  0.0 1924.4 jit_solution(14012076969192270796)
XLA Ops:
  12.6 13.1 all-reduce
  28.9 9.0 all_gather.22
  43.7 34.9 %all-gather.6.cloned.1.call-done = bf16[6144,768]{1,0:T(8,128)(2,1)} async-done(((bf16[1536,768]{1,0:T(8,128)(2,1)}), bf16[6144,768]{1,0:T(8,128)(2,1)}) %all-gather.6.cloned.1.call-update) | async-done | bytes 9437200 | tf_op jit(solution)/shard_map/all_gather | solution.py:191
  84.4 46.7 %all-gather.8.cloned.1.call-done = bf16[2,3,768,768]{3,2,1,0:T(8,128)(2,1)} async-done(((bf16[2,3,192,768]{3,2,1,0:T(8,128)(2,1)}), bf16[2,3,768,768]{3,2,1,0:T(8,128)(2,1)}) %all-gather.8.cloned.1.call-update) | async-done | bytes 7077904 | tf_op jit(solution)/shard_map/all_gather | solution.py:192
  140.6 16.2 all-gather.10.cloned.1.call-done
  158.9 63.6 %all-gather.12.cloned.1.call-done = bf16[2,768,3072]{2,1,0:T(8,128)(2,1)} async-done(((bf16[2,192,3072]{2,1,0:T(8,128)(2,1)}), bf16[2,768,3072]{2,1,0:T(8,128)(2,1)}) %all-gather.12.cloned.1.call-update) | async-done | bytes 9437200 | tf_op jit(solution)/shard_map/all_gather | solution.py:194
  226.7 61.5 %all-gather.14.cloned.1.call-done = bf16[2,3072,768]{2,1,0:T(8,128)(2,1)} async-done(((bf16[2,768,768]{2,1,0:T(8,128)(2,1)}), bf16[2,3072,768]{2,1,0:T(8,128)(2,1)}) %all-gather.14.cloned.1.call-update) | async-done | bytes 9437200 | tf_op jit(solution)/shard_map/all_gather | solution.py:195
  299.6 19.9 %all-to-all-done = bf16[4,8,16,768]{3,2,0,1:T(8,128)(2,1)S(1)} async-done(((bf16[4,8,16,768]{3,2,0,1:T(8,128)(2,1)}), bf16[4,8,16,768]{3,2,0,1:T(8,128)(2,1)S(1)}, u32[]{:S(2)}, u32[]{:S(2)}) %all-to-all-start) | async-done | bytes 786464 | tf_op jit(solution)/shard_map/all_to_all | solution.py:274
  373.5 19.9 %all-to-all-done.1 = bf16[4,8,16,768]{3,2,0,1:T(8,128)(2,1)} async-done(((bf16[4,8,16,768]{3,2,0,1:T(8,128)(2,1)}), bf16[4,8,16,768]{3,2,0,1:T(8,128)(2,1)}, u32[]{:S(2)}, u32[]{:S(2)}) %all-to-all-start.1) | async-done | bytes 786464 | tf_op jit(solution)/shard_map/all_to_all | solution.py:278
  424.1 8.1 convert_reduce_fusion
  566.5 10.7 maximum_bitcast_fusion.1
  577.2 19.7 %reshape.780 = f32[4718592]{0:T(1024)} reshape(f32[4,8,2,192,384]{4,3,2,1,0:T(8,128)} %maximum_bitcast_fusion.1) | data formatting | bytes 37748736 | tf_op jit(solution)/shard_map/reshape | solution.py:60
  596.9 12.5 stack.114
  614.9 10.7 maximum_bitcast_fusion.2
  625.6 22.2 %copy.333 = f32[4,8,2,768,96]{4,3,2,1,0:T(8,128)} copy(f32[4,8,2,768,96]{3,4,1,0,2:T(8,128)} %maximum_bitcast_fusion.2) | data formatting | bytes 37748736 | tf_op jit(solution)/shard_map/transpose | solution.py:59
  647.8 27.2 %reshape.783 = f32[4718592]{0:T(1024)} reshape(f32[4,8,2,768,96]{4,3,2,1,0:T(8,128)} %copy.333) | data formatting | bytes 37748736 | tf_op jit(solution)/shard_map/reshape | solution.py:60
  690.5 7.0 copy.320
  697.5 20.6 %reshape.774 = f32[3538944]{0:T(1024)} reshape(f32[4,8,2,3,192,96]{5,4,3,2,1,0:T(8,128)} %copy.320) | data formatting | bytes 28311552 | tf_op jit(solution)/shard_map/reshape | solution.py:60
  725.2 8.4 reshape.778
  734.1 7.9 convolution_bitcast_fusion
  742.0 22.1 %copy.308 = f32[4,8,1536,96]{3,2,1,0:T(8,128)} copy(f32[4,8,1536,96]{2,3,1,0:T(8,128)} %convolution_bitcast_fusion) | data formatting | bytes 37748736 | tf_op jit(solution)/shard_map/transpose | solution.py:59
  764.1 27.2 %reshape.762 = f32[4718592]{0:T(1024)} reshape(f32[4,8,1536,96]{3,2,1,0:T(8,128)} %copy.308) | data formatting | bytes 37748736 | tf_op jit(solution)/shard_map/reshape | solution.py:60
  808.7 43.2 %all-reduce.7 = (f32[768]{0:T(1024)}, f32[2,2,768]{2,1,0:T(2,128)}, f32[2,2,768]{2,1,0:T(2,128)}, f32[2,3072]{1,0:T(2,128)}, f32[2,768]{1,0:T(2,128)}) all-reduce(f32[768]{0:T(1024)S(1)} %get-tuple-element.99, f32[2,2,768]{2,1,0:T(2,128)S(1)} %pad_maximum_fusion.1, ...), channel_id=1, replica_groups=mesh['grp'=4,'wide'=8] {'grp','wide'}, use_global_device_ids=true, to_apply=%region_27.29 | all-reduce | flops 14592 | bytes 116736 | tf_op jit(solution)/shard_map/psum | solution.py:324
  851.8 1053.5 %all-reduce.11.cloned.1.call-done = (f32[196608]{0:T(1024)}, f32[4718592]{0:T(1024)}, f32[3538944]{0:T(1024)}, f32[1179648]{0:T(1024)}, f32[4718592]{0:T(1024)}, /*index=5*/f32[4718592]{0:T(1024)}) async-done(((f32[196608]{0:T(1024)}, f32[4718592]{0:T(1024)}, f32[3538944]{0:T(1024)}, f32[1179648]{0:T(1024)}, f32[4718592]{0:T(1024)}, /*index=5*/f32[4718592]{0:T(1024)}), (f32[196608]{0:T(1024)}, ...) | async-done | bytes 76283920
  (527 shorter events, 319.6 us)
Async XLA Ops:
  7.2 71.5 %all-gather.6.cloned.1.call-start = ((), (), s32[]{:S(2)}) async-start(), calls=%async_computation.4 | async-start | bytes 11796480 | tf_op jit(solution)/shard_map/all_gather | solution.py:191
  7.9 123.2 %all-gather.8.cloned.1.call-start = ((), (), s32[]{:S(2)}) async-start(), calls=%async_computation.5 | async-start | bytes 8847360 | tf_op jit(solution)/shard_map/all_gather | solution.py:192
  8.7 29.3 %copy-start.101 = (s32[512]{0:T(512)S(1)}, s32[512]{0:T(512)}, u32[]{:S(2)}) copy-start(s32[512]{0:T(512)} %param.16) | copy-start | bytes 6148
  8.7 148.1 %all-gather.10.cloned.1.call-start = ((), (), s32[]{:S(2)}) async-start(), calls=%async_computation.6 | async-start | bytes 2949120 | tf_op jit(solution)/shard_map/all_gather | solution.py:193
  9.4 213.0 %all-gather.12.cloned.1.call-start = ((), (), s32[]{:S(2)}) async-start(), calls=%async_computation.7 | async-start | bytes 11796480 | tf_op jit(solution)/shard_map/all_gather | solution.py:194
  10.0 278.1 %all-gather.14.cloned.1.call-start = ((), (), s32[]{:S(2)}) async-start(), calls=%async_computation.8 | async-start | bytes 11796480 | tf_op jit(solution)/shard_map/all_gather | solution.py:195
  38.9 98.5 %copy-start.60 = (pred[64,64]{0,1:T(8,128)(4,1)}, pred[64,64]{0,1:T(8,128)(4,1)S(1)}, u32[]{:S(2)}) copy-start(pred[64,64]{0,1:T(8,128)(4,1)S(1)} %iota_compare_fusion.1) | copy-start | bytes 12292
  42.3 92.5 %copy-start.81 = (f32[768]{0:T(1024)}, f32[768]{0:T(1024)S(1)}, u32[]{:S(2)}) copy-start(f32[768]{0:T(1024)S(1)} %get-tuple-element.84) | copy-start | bytes 9220
  84.2 53.5 %copy-start.92 = (f32[64]{0:T(128)}, f32[64]{0:T(128)S(1)}, u32[]{:S(2)}) copy-start(f32[64]{0:T(128)S(1)} %broadcast_multiply_fusion.3) | copy-start | bytes 772
  84.4 53.3 %copy-start.124 = (f32[64]{0:T(128)}, f32[64]{0:T(128)S(1)}, u32[]{:S(2)}) copy-start(f32[64]{0:T(128)S(1)} %multiply_reduce_fusion.13) | copy-start | bytes 772
  84.4 53.3 %copy-start.103 = (f32[64]{0:T(128)}, f32[64]{0:T(128)S(1)}, u32[]{:S(2)}) copy-start(f32[64]{0:T(128)S(1)} %fusion.131) | copy-start | bytes 772
  137.7 89.0 %copy-start.42 = (f32[12,64,64]{1,2,0:T(8,128)}, f32[12,64,64]{1,2,0:T(8,128)S(1)}, u32[]{:S(2)}) copy-start(f32[12,64,64]{1,2,0:T(8,128)S(1)} %fusion.45) | copy-start | bytes 589828
  158.6 129.5 %copy-start.110 = (f32[768]{0:T(1024)S(1)}, f32[768]{0:T(1024)}, u32[]{:S(2)}) copy-start(f32[768]{0:T(1024)} %get-tuple-element.87) | copy-start | bytes 9220
  158.7 129.5 %copy-start.86 = (f32[64]{0:T(128)}, f32[64]{0:T(128)S(1)}, u32[]{:S(2)}) copy-start(f32[64]{0:T(128)S(1)} %broadcast_multiply_fusion.2) | copy-start | bytes 772
  158.8 129.3 %copy-start.126 = (f32[64]{0:T(128)}, f32[64]{0:T(128)S(1)}, u32[]{:S(2)}) copy-start(f32[64]{0:T(128)S(1)} %multiply_reduce_fusion.12) | copy-start | bytes 772
  158.9 129.3 %copy-start.97 = (f32[64]{0:T(128)}, f32[64]{0:T(128)S(1)}, u32[]{:S(2)}) copy-start(f32[64]{0:T(128)S(1)} %fusion.132) | copy-start | bytes 772
  293.2 26.2 %all-to-all-start = ((bf16[4,8,16,768]{3,2,0,1:T(8,128)(2,1)}), bf16[4,8,16,768]{3,2,0,1:T(8,128)(2,1)S(1)}, u32[]{:S(2)}, u32[]{:S(2)}) async-start(bf16[4,8,16,768]{3,2,0,1:T(8,128)(2,1)} %copy.370), calls=%async_computation | async-start | bytes 1572864 | tf_op jit(solution)/shard_map/all_to_all | solution.py:274
  299.5 39.1 %copy-start.122 = (pred[8,8]{0,1:T(8,128)(4,1)}, pred[8,8]{0,1:T(8,128)(4,1)S(1)}, u32[]{:S(2)}) copy-start(pred[8,8]{0,1:T(8,128)(4,1)S(1)} %iota_compare_fusion.3) | copy-start | bytes 196
  299.5 67.3 %copy-start.88 = (s32[32]{0:T(128)}, s32[32]{0:T(128)S(1)}, u32[]{:S(2)}) copy-start(s32[32]{0:T(128)S(1)} %and_select_fusion) | copy-start | bytes 388
  299.5 67.2 %copy-start.90 = (pred[32]{0:T(512)(128)(4,1)}, pred[32]{0:T(512)(128)(4,1)S(1)}, u32[]{:S(2)}) copy-start(pred[32]{0:T(512)(128)(4,1)S(1)} %add_compare_fusion) | copy-start | bytes 100
  369.3 24.2 %all-to-all-start.1 = ((bf16[4,8,16,768]{3,2,0,1:T(8,128)(2,1)}), bf16[4,8,16,768]{3,2,0,1:T(8,128)(2,1)}, u32[]{:S(2)}, u32[]{:S(2)}) async-start(bf16[4,8,16,768]{3,2,0,1:T(8,128)(2,1)} %copy.275), calls=%async_computation.1 | async-start | bytes 1572864 | tf_op jit(solution)/shard_map/all_to_all | solution.py:278
  397.6 24.4 %all-to-all-start.2 = ((bf16[4,8,16,768]{3,2,0,1:T(8,128)(2,1)}), bf16[4,8,16,768]{3,2,0,1:T(8,128)(2,1)}, u32[]{:S(2)}, u32[]{:S(2)}) async-start(bf16[4,8,16,768]{3,2,0,1:T(8,128)(2,1)} %copy.278), calls=%async_computation.2 | async-start | bytes 1572864 | tf_op jit(solution)/shard_map/all_to_all | solution.py:285
  480.1 40.0 %all-to-all-start.3 = ((bf16[4,8,16,768]{3,2,0,1:T(8,128)(2,1)}), bf16[4,8,16,768]{3,2,0,1:T(8,128)(2,1)}, u32[]{:S(2)}, u32[]{:S(2)}) async-start(bf16[4,8,16,768]{3,2,0,1:T(8,128)(2,1)} %copy.289), calls=%async_computation.3 | async-start | bytes 1572864 | tf_op jit(solution)/shard_map/all_to_all | solution.py:295
  484.3 1421.1 %all-reduce.11.cloned.1.call-start = ((), (), s32[]{:S(2)}) async-start(), calls=%async_computation.9 | async-start | bytes 152567808
  (122 other events, 775.3 us)
Sparse Core Ops, SparseCore 0:
  9.6 69.0 all-gather.5
  80.2 50.8 all-gather.7
  132.7 24.0 all-gather.9
  158.2 64.2 all-gather.11
  223.9 64.2 all-gather.13
  806.8 1098.5 all-reduce.10
where the time goes:
time: 1940 us; the launch traced here: 1920 us
  waiting for transfers between devices  1320 us (68%)
  local copies, waits for them, and re-layouts  297 us (15%)
  matrix products  152 us (8%)
  blocking collectives  65.2 us (3%)
  other arithmetic  48.5 us (2%)
    unnamed x7, waiting for transfers between devices  1060 us
    reshape x6, local copies, waits for them, and re-layouts, to_blocks(): return moved.reshape(-1)  105 us
    all_gather x1, waiting for transfers between devices, body(): lax.all_gather(up_weight, 'grp', axis=1, tiled=True)  63.6 us
    all_gather x1, waiting for transfers between devices, body(): lax.all_gather(down_weight, 'grp', axis=1, tiled=True)  61.5 us
    transpose x4, local copies, waits for them, and re-layouts, to_blocks(): moved = jnp.moveaxis(split, (count, count + 2), (0, 1))  54.4 us
    dot_general x16, matrix products, weight_term(): lax.dot_general(left, right, (((0,), (0,)), ((), ())), preferred_element_...  48.8 us
    all_gather x1, waiting for transfers between devices, body(): lax.all_gather(qkv_weight, 'grp', axis=2, tiled=True)  46.7 us
    dot_general x13, matrix products, back_product(): lax.dot_general(left, right, (((1,), (1,)), ((), ())), preferred_element_...  44.4 us
  transfers between devices with their start and end apart: 10, of which 9 were waited for; matrix products, arithmetic and copies ran while one was open for 4% of the time, Pallas kernels for 0%

commit v1 on v0

v1 whole, which is shorter than its diff:
```python
import jax
import jax.numpy as jnp
from jax import lax
from jax.sharding import PartitionSpec as P

HEADS = 12
HEAD_DIM = 64
PATCH = 8

NORM_EPS = 1e-05
MASK_FILL = -1e30
BF = jnp.bfloat16
F32 = jnp.float32


def product(left, right):
    return jnp.dot(left, right, preferred_element_type=F32)


def weight_term(left, right):
    return lax.dot_general(left, right, (((0,), (0,)), ((), ())), preferred_element_type=F32)


def back_product(left, right):
    return lax.dot_general(left, right, (((1,), (1,)), ((), ())), preferred_element_type=F32)


def bits_of(count):
    return count.bit_length() - 1


def swap(value, axis, mask):
    return lax.ppermute(value, axis, [(i, i ^ mask) for i in range(lax.axis_size(axis))])


def bit_at(axis, bit):
    return (lax.axis_index(axis) >> bit) & 1


def pick(value, index, axis):
    return lax.dynamic_index_in_dim(value, index, axis, keepdims=False)


def gather_butterfly(value, axis, bits):
    for bit in bits:
        value = jnp.concatenate([value, swap(value, axis, 1 << bit)], axis=0)
    return value


def gather_weight(shard, dim):
    groups = lax.axis_size("grp")
    me = lax.axis_index("grp")
    side = bit_at("wide", 0)
    rows = shard.shape[dim]
    half = rows // 2
    pieces = {0: (lax.dynamic_slice_in_dim(shard, side * half, half, dim), None)}
    for bit in reversed(range(1, bits_of(groups))):
        for rel in list(pieces):
            first = swap(pieces[rel][0], "grp", 1 << bit)
            pieces[rel ^ (1 << bit)] = (first, swap(first, "wide", 1))
    whole = {0: (shard, None)}
    whole[1] = (swap(shard, "grp", 1), None)
    for rel in list(pieces):
        if rel:
            whole[rel] = pieces[rel]
            whole[rel ^ 1] = tuple(swap(p, "grp", 1) for p in pieces[rel])
    shape = list(shard.shape)
    shape[dim] = rows * groups
    out = jnp.zeros(shape, shard.dtype)
    for rel, (first, second) in whole.items():
        base = (me ^ rel) * rows
        if second is None:
            out = lax.dynamic_update_slice_in_dim(out, first, base, dim)
        else:
            out = lax.dynamic_update_slice_in_dim(out, first, base + side * half, dim)
            out = lax.dynamic_update_slice_in_dim(out, second, base + (1 - side) * half, dim)
    return out


def reduce_blocks(terms, order):
    chips, wides, rows, lanes = terms.shape
    core = bit_at("grp", 0)
    split = terms.reshape((chips, wides, 2, rows // 2, lanes))
    acc = (pick(split, core, 2).astype(F32) + swap(pick(split, 1 - core, 2), "grp", 1).astype(F32)).astype(BF)
    left = [("grp", b) for b in reversed(range(1, bits_of(lax.axis_size("grp"))))]
    left += [("wide", b) for b in reversed(range(bits_of(wides)))]
    acc = acc.reshape((2,) * len(left) + (rows // 2, lanes))
    for number, step in enumerate(order):
        axis, bit = step
        at = left.index(step)
        mine = bit_at(axis, bit)
        got = swap(pick(acc, 1 - mine, at), axis, 1 << bit)
        acc = pick(acc, mine, at).astype(F32) + got.astype(F32)
        if number + 1 < len(order):
            acc = acc.astype(BF)
        left.remove(step)
    return acc


def join_cores(half, by_lanes):
    core = bit_at("grp", 0)
    rows, lanes = half.shape
    low, high = half[:, : lanes // 2], half[:, lanes // 2 :]
    mine = jnp.where(core == 0, low, high)
    other = swap(jnp.where(core == 0, high, low), "grp", 1)
    return jnp.where(core == 0, jnp.concatenate([mine, other]), jnp.concatenate([other, mine]))


def layer_norm(hidden, gain, bias):
    centered = hidden - jnp.mean(hidden, axis=-1, keepdims=True)
    spread = jnp.mean(centered * centered, axis=-1, keepdims=True)
    return centered * lax.rsqrt(spread + NORM_EPS) * gain + bias


def masked_softmax(scores):
    span = scores.shape[-1]
    rows_index = lax.broadcasted_iota(jnp.int32, (span, span), 0)
    cols_index = lax.broadcasted_iota(jnp.int32, (span, span), 1)
    return jax.nn.softmax(jnp.where(cols_index <= rows_index, scores, MASK_FILL), axis=-1)


def gelu_tanh(upper):
    return jax.nn.gelu(upper, approximate=True)


def split_heads(hidden, span):
    return hidden.reshape(hidden.shape[0] // span, span, HEADS, HEAD_DIM)


def block_forward(hidden, weights, span):
    gains, biases, w_qkv, w_out, w_up, b_up, w_down, b_down = weights
    rows_total = hidden.shape[0]
    norm_one, norm_one_back = jax.vjp(layer_norm, hidden, gains[0], biases[0])
    normed_one = norm_one.astype(BF)
    query = split_heads(product(normed_one, w_qkv[0]).astype(BF), span)
    keyed = split_heads(product(normed_one, w_qkv[1]).astype(BF), span)
    valued = split_heads(product(normed_one, w_qkv[2]).astype(BF), span)
    scale = HEAD_DIM ** (-0.5)
    scores = jnp.einsum("glhd,gmhd->ghlm", query, keyed, preferred_element_type=F32) * scale
    probs_value, soft_back = jax.vjp(masked_softmax, scores)
    probs = probs_value.astype(BF)
    mixed = jnp.einsum("ghlm,gmhd->glhd", probs, valued, preferred_element_type=F32)
    mixed = mixed.reshape(rows_total, -1).astype(BF)
    middle = hidden + product(mixed, w_out)
    norm_two, norm_two_back = jax.vjp(layer_norm, middle, gains[1], biases[1])
    normed_two = norm_two.astype(BF)
    upper = product(normed_two, w_up) + b_up
    active_value, gelu_back = jax.vjp(gelu_tanh, upper)
    active = active_value.astype(BF)
    out = middle + (product(active, w_down) + b_down)
    kept = (norm_one_back, normed_one, query, keyed, valued, soft_back, probs, mixed, norm_two_back, normed_two, gelu_back, active)
    return out, kept


def by_chips(left, right, chips, wides, pieces=1):
    lanes = left.shape[1] // chips // pieces
    parts = []
    for at in range(chips):
        rows = []
        for piece in range(pieces):
            base = (at * pieces + piece) * lanes
            term = weight_term(right, left[:, base : base + lanes]).astype(BF)
            rows.append(term.reshape(wides, -1, lanes))
        parts.append(jnp.concatenate(rows, axis=1))
    return jnp.stack(parts)


def block_backward(grad_out, weights, kept, span, chips, wides):
    gains, biases, w_qkv, w_out, w_up, b_up, w_down, b_down = weights
    norm_one_back, normed_one, query, keyed, valued, soft_back, probs, mixed, norm_two_back, normed_two, gelu_back, active = kept
    rows_total = grad_out.shape[0]
    scale = HEAD_DIM ** (-0.5)
    grad_down = grad_out.astype(BF)
    down_bias_term = jnp.sum(grad_down.astype(F32), axis=0)
    grad_upper = gelu_back(back_product(grad_down, w_down))[0].astype(BF)
    up_bias_term = jnp.sum(grad_upper.astype(F32), axis=0)
    grad_norm_two, gain_two_term, bias_two_term = norm_two_back(back_product(grad_upper, w_up))
    up_term = by_chips(normed_two, grad_upper, chips, wides)
    down_term = by_chips(active, grad_down, chips, wides, active.shape[1] // normed_two.shape[1])
    grad_middle = grad_out + grad_norm_two
    grad_branch = grad_middle.astype(BF)
    out_term = by_chips(mixed, grad_branch, chips, wides)
    grad_mixed = back_product(grad_branch, w_out).astype(BF)
    grad_heads = split_heads(grad_mixed, span)
    grad_probs = jnp.einsum("glhd,gmhd->ghlm", grad_heads, valued, preferred_element_type=F32)
    grad_value = jnp.einsum("ghlm,glhd->gmhd", probs, grad_heads, preferred_element_type=F32)
    grad_value = grad_value.reshape(rows_total, -1).astype(BF)
    grad_scores = soft_back(grad_probs)[0].astype(BF)
    grad_query = jnp.einsum("ghlm,gmhd->glhd", grad_scores, keyed, preferred_element_type=F32) * scale
    grad_query = grad_query.reshape(rows_total, -1).astype(BF)
    grad_key = jnp.einsum("ghlm,glhd->gmhd", grad_scores, query, preferred_element_type=F32) * scale
    grad_key = grad_key.reshape(rows_total, -1).astype(BF)
    grads = (grad_query, grad_key, grad_value)
    attend_term = jnp.concatenate(
        [by_chips(normed_one, entry, chips, wides) for entry in grads] + [out_term], axis=2
    )
    grad_normed = (
        back_product(grad_query, w_qkv[0])
        + back_product(grad_key, w_qkv[1])
        + back_product(grad_value, w_qkv[2])
    )
    grad_norm_one, gain_one_term, bias_one_term = norm_one_back(grad_normed)
    grad_hidden = grad_middle + grad_norm_one
    vectors = (
        jnp.stack([gain_one_term, gain_two_term]),
        jnp.stack([bias_one_term, bias_two_term]),
        up_bias_term,
        down_bias_term,
    )
    return grad_hidden, up_term, down_term, attend_term, vectors


def body(
    byte_ids,
    item_lengths,
    embed_table,
    patch_weight,
    patch_bias,
    norm_gain,
    norm_bias,
    qkv_weight,
    out_weight,
    up_weight,
    up_bias,
    down_weight,
    down_bias,
    out_cot,
):
    groups = lax.axis_size("grp")
    wides = lax.axis_size("wide")
    chips = groups // 2
    grp_bits = bits_of(groups)
    wide_bits = bits_of(wides)
    me = lax.axis_index("grp")
    width = embed_table.shape[1]
    vocab_rows = embed_table.shape[0]
    vocab = vocab_rows * groups
    byte_count = byte_ids.shape[0]
    patch_count = byte_count // PATCH
    own_spots = PATCH // groups

    positions = lax.broadcasted_iota(jnp.int32, (byte_count, 1), 0)
    valid = positions < item_lengths[0]
    byte_keep = valid.astype(F32)
    ids = jnp.where(valid[:, 0], byte_ids, -1)
    ids_grp = gather_butterfly(ids.reshape(1, patch_count, PATCH), "grp", range(grp_bits))
    table = gather_butterfly(embed_table[None], "grp", range(grp_bits)).reshape(vocab, width)

    def one_hot_rel(numbers):
        moved = jnp.where(numbers < 0, -1, numbers ^ (me * vocab_rows))
        return (moved[..., None] == jnp.arange(vocab)).astype(BF)

    one_hot = (ids[:, None] == jnp.arange(vocab)).astype(BF)
    embedded = product(one_hot_rel(ids), table)

    own_ids = lax.dynamic_slice_in_dim(ids_grp, me * own_spots, own_spots, 2)
    partial = 0.0
    for spot in range(own_spots):
        rows = product(one_hot_rel(own_ids[:, :, spot]).reshape(-1, vocab), table).astype(BF)
        partial += product(rows, patch_weight[spot * width : (spot + 1) * width])
    partial = partial.reshape(groups, patch_count, width)
    summary = partial[0] + patch_bias
    for rel in range(1, groups):
        summary = summary + swap(partial[rel].astype(BF), "grp", rel).astype(F32)

    def block_weights(at):
        return (
            norm_gain[at],
            norm_bias[at],
            gather_weight(qkv_weight[at], 1),
            gather_weight(out_weight[at], 0),
            gather_weight(up_weight[at], 0),
            up_bias[at],
            gather_weight(down_weight[at], 0),
            down_bias[at],
        )

    global_weights = block_weights(0)
    local_weights = block_weights(1)
    patch_full = gather_weight(patch_weight, 0)
    ids_all = gather_butterfly(own_ids[None], "wide", range(wide_bits))

    global_out, global_kept = block_forward(summary, global_weights, patch_count)
    local_in = (
        (embedded.reshape(patch_count, PATCH, width) + global_out[:, None, :])
        .reshape(byte_count, width)
        .astype(BF)
    )
    local_low, local_kept = block_forward(local_in.astype(F32), local_weights, PATCH)
    local_out = (local_low.astype(BF).astype(F32) * byte_keep).astype(BF)
    cot_masked = out_cot.astype(F32) * byte_keep
    grad_rows, l_up, l_down, l_attend, l_vectors = block_backward(
        cot_masked, local_weights, local_kept, PATCH, chips, wides
    )

    chip_steps = [("grp", b) for b in range(1, grp_bits)]
    rest = [("wide", b) for b in range(1, wide_bits)]
    order_a = chip_steps + [("wide", 0)] + rest
    order_b = [("wide", 0)] + chip_steps + rest
    l_up = reduce_blocks(l_up, order_a)
    l_down = reduce_blocks(l_down, order_b)
    l_attend = reduce_blocks(l_attend, order_a)

    grad_local = grad_rows.astype(BF)
    grad_global = jnp.sum(grad_local.astype(F32).reshape(patch_count, PATCH, width), axis=1)
    grad_summary, g_up, g_down, g_attend, g_vectors = block_backward(
        grad_global, global_weights, global_kept, patch_count, chips, wides
    )
    g_up = reduce_blocks(g_up, order_a)
    g_down = reduce_blocks(g_down, order_b)
    g_attend = reduce_blocks(g_attend, order_b)
    grad_summary = grad_summary.astype(BF)
    patch_bias_term = jnp.sum(grad_summary.astype(F32), axis=0)

    collected = grad_summary.T.reshape((2,) * wide_bits + (1, width // wides, patch_count))
    for bit in range(wide_bits):
        mine = bit_at("wide", bit)
        at = wide_bits - 1 - bit
        collected = jnp.concatenate(
            [pick(collected, mine, at), swap(pick(collected, 1 - mine, at), "wide", 1 << bit)],
            axis=wide_bits - 1 - bit,
        )
    collected = gather_butterfly(collected[None], "grp", range(grp_bits))
    patch_terms = []
    for spot in range(own_spots):
        hot = one_hot_rel(ids_all[:, :, :, spot])
        counts = jnp.einsum("gwnp,wgpv->nv", collected, hot, preferred_element_type=F32).astype(BF)
        patch_terms.append(product(counts, table).T)
    patch_weight_grad = jnp.concatenate(patch_terms, axis=0)

    grad_patches = back_product(grad_summary, patch_full).reshape(byte_count, width)
    embed_rows_grad = (grad_local.astype(F32) + grad_patches).astype(BF)
    table_term = by_chips(one_hot, embed_rows_grad, chips, wides)
    table_term = join_cores(reduce_blocks(table_term, order_a), True)

    flat = [patch_bias_term]
    for g_entry, l_entry in zip(g_vectors, l_vectors):
        flat.append(jnp.stack([g_entry, l_entry]).reshape(-1))
    vector = jnp.concatenate(flat)
    for axis, count in (("grp", grp_bits), ("wide", wide_bits)):
        for bit in range(count):
            vector = vector + swap(vector, axis, 1 << bit)
    vectors = []
    base = 0
    for shape in ((width,), (2, 2, width), (2, 2, width), up_bias.shape, down_bias.shape):
        size = 1
        for extent in shape:
            size *= extent
        vectors.append(vector[base : base + size].reshape(shape))
        base += size

    def finish_up(half):
        return join_cores(half, True).T

    def finish_down(half):
        rows = width // wides
        kept = half.reshape(-1, rows, half.shape[1])
        return jnp.swapaxes(kept, 1, 2).reshape(-1, rows)

    def finish_attend(half):
        rows = width // wides
        joined = join_cores(half, True).reshape(4, rows, -1)
        return jnp.swapaxes(joined, 1, 2)

    g_attend = finish_attend(g_attend)
    l_attend = finish_attend(l_attend)
    return (
        local_out,
        embed_rows_grad,
        table_term.T,
        patch_weight_grad,
        vectors[0],
        vectors[1],
        vectors[2],
        jnp.stack([g_attend[:3], l_attend[:3]]),
        jnp.stack([g_attend[3], l_attend[3]]),
        jnp.stack([finish_up(g_up), finish_up(l_up)]),
        vectors[3],
        jnp.stack([finish_down(g_down), finish_down(l_down)]),
        vectors[4],
    )


def solution(mesh):
    placed = (
        P(("grp", "wide")),
        P(("grp", "wide")),
        P("grp", None),
        P("grp", None),
        P(),
        P(),
        P(),
        P(None, None, "grp", None),
        P(None, "grp", None),
        P(None, "grp", None),
        P(),
        P(None, "grp", None),
        P(),
        P(("grp", "wide"), None),
    )
    return jax.shard_map(
        body,
        mesh=mesh,
        in_specs=placed,
        out_specs=(
            P(("grp", "wide"), None),
            P(("grp", "wide"), None),
            P("grp", "wide"),
            P("grp", "wide"),
            P(),
            P(),
            P(),
            P(None, None, "grp", "wide"),
            P(None, "grp", "wide"),
            P(None, "grp", "wide"),
            P(),
            P(None, "grp", "wide"),
            P(),
        ),
        check_vma=False,
    )
```

time: 1940 us -> 751 us (0.39)
  waiting for transfers between devices: 1320 us -> 240 us
  local copies, waits for them, and re-layouts: 297 us -> 195 us
  blocking collectives: 65.2 us -> 0 us
  starting transfers between devices: 19.2 us -> 69.2 us
  other arithmetic: 48.5 us -> 75.6 us
    unnamed x7 -> x0, waiting for transfers between devices: 1060 us -> none
    ppermute x0 -> x105, waiting for transfers between devices: none -> 240 us  [swap(): lax.ppermute(value, axis, [(i, i ^ mask) for i in range(lax.axis_size(axi...]
    all_gather x5 -> x0, waiting for transfers between devices: 223 us -> none  [the longest x1 63.6 us: body(): lax.all_gather(up_weight, 'grp', axis=1, tiled=True)]
    reshape x20 -> x10, local copies, waits for them, and re-layouts: 118 us -> 7.22 us  [the longest x1 3.06 us: body(): back_product(grad_summary, patch_full).reshape(byte_count, width)]
    ppermute x0 -> x105, starting transfers between devices: none -> 69.2 us  [swap(): lax.ppermute(value, axis, [(i, i ^ mask) for i in range(lax.axis_size(axi...]
    dynamic_update_slice x0 -> x52, local copies, waits for them, and re-layouts: none -> 60.7 us  [the longest x16 22.8 us: gather_weight(): lax.dynamic_update_slice_in_dim(out, second, base + (1 - side) * half, dim)]
    transpose x4 -> x2, local copies, waits for them, and re-layouts: 54.4 us -> 0.46 us  [finish_down(): return jnp.swapaxes(kept, 1, 2).reshape(-1, rows)]
    all_to_all x4 -> x0, waiting for transfers between devices: 44.3 us -> none  [the longest x1 19.9 us: body(): lax.all_to_all(sent_in, 'wide', split_axis=1, concat_axis=1, tiled=True)]
  transfers between devices with their start and end apart: 10 -> 105, of which waited for: 9 -> 40; matrix products, arithmetic and copies ran while one was open for 4% -> 53% of each run, Pallas kernels for 0% -> 0%
where the time goes in v1:
time: 751 us; the launch traced here: 739 us
  waiting for transfers between devices  240 us (32%)
  local copies, waits for them, and re-layouts  195 us (26%)
  matrix products  154 us (21%)
  other arithmetic  75.6 us (10%)
  starting transfers between devices  69.2 us (9%)
    ppermute x105, waiting for transfers between devices, swap(): lax.ppermute(value, axis, [(i, i ^ mask) for i in range(lax.axis_size(axi...  240 us
    ppermute x105, starting transfers between devices, swap(): lax.ppermute(value, axis, [(i, i ^ mask) for i in range(lax.axis_size(axi...  69.2 us
    dot_general x38, matrix products, weight_term(): lax.dot_general(left, right, (((0,), (0,)), ((), ())), preferred_element_...  47.9 us
    dot_general x13, matrix products, back_product(): lax.dot_general(left, right, (((1,), (1,)), ((), ())), preferred_element_...  44.1 us
    dot_general x17, matrix products, product(): return jnp.dot(left, right, preferred_element_type=F32)  42.5 us
    unnamed x365, local copies, waits for them, and re-layouts  28 us
    dynamic_update_slice x16, local copies, waits for them, and re-layouts, gather_weight(): lax.dynamic_update_slice_in_dim(out, second, base + (1 - side) * half, dim)  22.8 us
    dynamic_update_slice x18, local copies, waits for them, and re-layouts, gather_weight(): out = lax.dynamic_update_slice_in_dim(out, first, base, dim)  19.9 us
  transfers between devices with their start and end apart: 105, of which 40 were waited for; matrix products, arithmetic and copies ran while one was open for 53% of the time, Pallas kernels for 0%

profile of v1, /device:TPU:0, one launch (start us, length us, event | category | flops | bytes accessed | tf_op | source)
XLA Modules:
  0.0 739.0 jit_solution(13337946913630989185)
XLA Ops:
  86.4 6.0 collective-permute-done.1
  138.5 7.2 collective-permute-done.29
  153.7 10.1 %collective-permute-done.39 = bf16[96,3072]{1,0:T(8,128)(2,1)} collective-permute-done((bf16[96,3072]{1,0:T(8,128)(2,1)S(1)}, bf16[96,3072]{1,0:T(8,128)(2,1)}, u32[]{:S(2)}, u32[]{:S(2)}) %collective-permute-start.39) | collective-permute-done | bytes 589856 | tf_op jit(solution)/shard_map/ppermute | solution.py:33
  173.4 6.8 collective-permute-done.18
  180.2 12.6 %collective-permute-done.43 = bf16[384,768]{1,0:T(8,128)(2,1)S(1)} collective-permute-done((bf16[384,768]{1,0:T(8,128)(2,1)S(1)}, bf16[384,768]{1,0:T(8,128)(2,1)S(1)}, u32[]{:S(2)}, u32[]{:S(2)}) %collective-permute-start.43) | collective-permute-done | bytes 589856 | tf_op jit(solution)/shard_map/ppermute | solution.py:33
  199.7 9.5 %collective-permute-done.44 = bf16[384,768]{1,0:T(8,128)(2,1)} collective-permute-done((bf16[384,768]{1,0:T(8,128)(2,1)S(1)}, bf16[384,768]{1,0:T(8,128)(2,1)}, u32[]{:S(2)}, u32[]{:S(2)}) %collective-permute-start.44) | collective-permute-done | bytes 589856 | tf_op jit(solution)/shard_map/ppermute | solution.py:33
  212.5 7.1 collective-permute-done.19
  270.3 10.7 %fusion.253 = (f32[64,12,8]{2,1,0:T(8,128)S(1)}, f32[64,12,8,8]{2,3,1,0:T(8,128)S(1)}) fusion(f32[64,12,8,8]{2,3,1,0:T(8,128)S(1)} %fusion.93, pred[8,8]{0,1:T(8,128)(4,1)S(1)} %copy-done.157), kind=kOutput, calls=%fused_computation.622 | output fusion | flops 294919 | bytes 417856 | tf_op jit(solution)/shard_map/jvp()/sub | solution.py:119
  288.9 8.1 %multiply_convert_fusion = (bf16[512,3072]{1,0:T(8,128)(2,1)}, f32[512,3072]{1,0:T(8,128)S(1)}) fusion(f32[3072]{0:T(1024)S(1)} %bitcast.698, bf16[512,768]{1,0:T(8,128)(2,1)S(1)} %add_convert_fusion.2, bf16[768,3072]{1,0:T(8,128)(2,1)} %get-tuple-element.188), kind=kOutput, calls=%fused_computation.12 | convolution fusion | flops 2431647744 | bytes 14954496 | tf_op jit(solution)/shard_map/dot_general | solution.py:17
  298.9 8.9 %convert_reduce_fusion = (f32[3072]{0:T(1024)}, bf16[512,3072]{1,0:T(8,128)(2,1)S(1)}) fusion(f32[512,3072]{1,0:T(8,128)S(1)} %get-tuple-element.177, f32[3072]{0:T(1024)S(1)} %bitcast.699, bf16[3072,768]{1,0:T(8,128)(2,1)} %constant_dynamic-update-slice_fusion.6, bf16[512,768]{1,0:T(8,128)(2,1)S(1)} %copy-done.40, f32[512]{0:T(512)S(1)} %copy-done.123), kind=kOutput, calls=%fused_computation.11 | convolution fusion | flops 2453271552 | bytes 14968832 | tf_op jit(solution)/shard_map/dot_general | solution.py:25
  462.8 5.9 multiply_convert_fusion.3
  489.0 7.9 %fusion.255 = f32[64,6144]{1,0:T(8,128)} fusion(bf16[64,768]{1,0:T(8,128)(2,1)S(1)} %get-tuple-element.95, bf16[6144,768]{1,0:T(8,128)(2,1)} %constant_dynamic-update-slice_fusion), kind=kOutput, calls=%fused_computation.624 | convolution fusion | flops 603979776 | bytes 11108352 | tf_op jit(solution)/shard_map/dot_general | solution.py:25
  530.3 6.9 collective-permute-done.62
  568.3 9.9 %collective-permute-done.96 = bf16[2,2,2,192,384]{4,3,2,1,0:T(8,128)(2,1)S(1)} collective-permute-done((bf16[2,2,2,192,384]{4,3,2,1,0:T(8,128)(2,1)S(1)}, bf16[2,2,2,192,384]{4,3,2,1,0:T(8,128)(2,1)S(1)}, u32[]{:S(2)}, u32[]{:S(2)}) %collective-permute-start.96) | collective-permute-done | bytes 1179680 | tf_op jit(solution)/shard_map/ppermute | solution.py:33
  579.6 23.9 %collective-permute-done.101 = bf16[2,2,2,192,384]{4,3,2,1,0:T(8,128)(2,1)S(1)} collective-permute-done((bf16[2,2,2,192,384]{4,3,2,1,0:T(8,128)(2,1)S(1)}, bf16[2,2,2,192,384]{4,3,2,1,0:T(8,128)(2,1)S(1)}, u32[]{:S(2)}, u32[]{:S(2)}) %collective-permute-start.101) | collective-permute-done | bytes 1179680 | tf_op jit(solution)/shard_map/ppermute | solution.py:33
  612.7 16.0 %collective-permute-done.72 = bf16[2,2,2,192,384]{4,3,2,1,0:T(8,128)(2,1)S(1)} collective-permute-done((bf16[2,2,2,192,384]{4,3,2,1,0:T(8,128)(2,1)S(1)}, bf16[2,2,2,192,384]{4,3,2,1,0:T(8,128)(2,1)S(1)}, u32[]{:S(2)}, u32[]{:S(2)}) %collective-permute-start.72) | collective-permute-done | bytes 1179680 | tf_op jit(solution)/shard_map/ppermute | solution.py:33
  629.7 7.3 collective-permute-done.78
  638.4 11.2 %collective-permute-done.97 = bf16[2,2,192,384]{3,2,1,0:T(8,128)(2,1)S(1)} collective-permute-done((bf16[2,2,192,384]{3,2,1,0:T(8,128)(2,1)S(1)}, bf16[2,2,192,384]{3,2,1,0:T(8,128)(2,1)S(1)}, u32[]{:S(2)}, u32[]{:S(2)}) %collective-permute-start.97) | collective-permute-done | bytes 589856 | tf_op jit(solution)/shard_map/ppermute | solution.py:33
  650.5 11.8 %collective-permute-done.102 = bf16[2,2,192,384]{3,2,1,0:T(8,128)(2,1)S(1)} collective-permute-done((bf16[2,2,192,384]{3,2,1,0:T(8,128)(2,1)S(1)}, bf16[2,2,192,384]{3,2,1,0:T(8,128)(2,1)S(1)}, u32[]{:S(2)}, u32[]{:S(2)}) %collective-permute-start.102) | collective-permute-done | bytes 589856 | tf_op jit(solution)/shard_map/ppermute | solution.py:33
  666.8 7.7 %collective-permute-done.73 = bf16[2,2,192,384]{3,2,1,0:T(8,128)(2,1)S(1)} collective-permute-done((bf16[2,2,192,384]{3,2,1,0:T(8,128)(2,1)S(1)}, bf16[2,2,192,384]{3,2,1,0:T(8,128)(2,1)S(1)}, u32[]{:S(2)}, u32[]{:S(2)}) %collective-permute-start.73) | collective-permute-done | bytes 589856 | tf_op jit(solution)/shard_map/ppermute | solution.py:33
  679.4 10.2 %collective-permute-done.86 = bf16[2,192,384]{2,1,0:T(8,128)(2,1)S(1)} collective-permute-done((bf16[2,192,384]{2,1,0:T(8,128)(2,1)S(1)}, bf16[2,192,384]{2,1,0:T(8,128)(2,1)S(1)}, u32[]{:S(2)}, u32[]{:S(2)}) %collective-permute-start.86) | collective-permute-done | bytes 294944 | tf_op jit(solution)/shard_map/ppermute | solution.py:33
  689.8 9.4 %collective-permute-done.92 = bf16[2,192,384]{2,1,0:T(8,128)(2,1)S(1)} collective-permute-done((bf16[2,192,384]{2,1,0:T(8,128)(2,1)S(1)}, bf16[2,192,384]{2,1,0:T(8,128)(2,1)S(1)}, u32[]{:S(2)}, u32[]{:S(2)}) %collective-permute-start.92) | collective-permute-done | bytes 294944 | tf_op jit(solution)/shard_map/ppermute | solution.py:33
  699.2 6.3 collective-permute-done.74
  714.3 9.5 %collective-permute-done.87 = bf16[192,384]{1,0:T(8,128)(2,1)S(1)} collective-permute-done((bf16[192,384]{1,0:T(8,128)(2,1)S(1)}, bf16[192,384]{1,0:T(8,128)(2,1)S(1)}, u32[]{:S(2)}, u32[]{:S(2)}) %collective-permute-start.87) | collective-permute-done | bytes 147488 | tf_op jit(solution)/shard_map/ppermute | solution.py:33
  (948 shorter events, 503.3 us)
Async XLA Ops:
  3.3 55.2 %collective-permute-start.2 = (s32[1,64,8]{2,1,0:T(8,128)}, s32[1,64,8]{2,1,0:T(8,128)}, u32[]{:S(2)}, u32[]{:S(2)}) collective-permute-start(s32[1,64,8]{2,1,0:T(8,128)} %reshape.697), channel_id=1, source_target_pairs={{0,8},{8,0},{16,24},{24,16},{1,9},{9,1},{17,25},{25,17},{2,10},{10... | collective-permute-start | bytes 6152 | tf_op jit(solution)/shard_map/ppermute | solution.py:33
  3.7 80.3 %collective-permute-start = (bf16[1,64,768]{2,1,0:T(8,128)(2,1)}, bf16[1,64,768]{2,1,0:T(8,128)(2,1)}, u32[]{:S(2)}, u32[]{:S(2)}) collective-permute-start(bf16[1,64,768]{2,1,0:T(8,128)(2,1)} %bitcast.687), channel_id=1, source_target_pairs={{0,8},{8,0},{16,24},{24,16},{1,9},{9,1},{17,25},{25,17},{2,10},{10... | collective-permute-start | bytes 294920 | tf_op jit(solution)/shard_map/ppermute | solution.py:33
  7.3 118.8 %collective-permute-start.7 = (bf16[3,192,768]{2,1,0:T(8,128)(2,1)}, bf16[3,192,768]{2,1,0:T(8,128)(2,1)}, u32[]{:S(2)}, u32[]{:S(2)}) collective-permute-start(bf16[3,192,768]{2,1,0:T(8,128)(2,1)} %get-tuple-element.123), channel_id=1, source_target_pairs={{0,8},{8,0},{16,24},{24,16},{1,9},{9,1},{17,25},{25,17},{2,10},{10... | collective-permute-start | bytes 2654216 | tf_op jit(solution)/shard_map/ppermute | solution.py:33
  8.7 95.0 %collective-permute-start.12 = (bf16[192,768]{1,0:T(8,128)(2,1)}, bf16[192,768]{1,0:T(8,128)(2,1)}, u32[]{:S(2)}, u32[]{:S(2)}) collective-permute-start(bf16[192,768]{1,0:T(8,128)(2,1)} %get-tuple-element.130), channel_id=1, source_target_pairs={{0,8},{8,0},{16,24},{24,16},{1,9},{9,1},{17,25},{25,17},{2,10},{10... | collective-permute-start | bytes 884744 | tf_op jit(solution)/shard_map/ppermute | solution.py:33
  9.5 92.9 %collective-permute-start.13 = (bf16[96,768]{1,0:T(8,128)(2,1)}, bf16[96,768]{1,0:T(8,128)(2,1)}, u32[]{:S(2)}, u32[]{:S(2)}) collective-permute-start(bf16[96,768]{1,0:T(8,128)(2,1)} %dynamic-slice_bitcast_fusion.30), channel_id=1, source_target_pairs={{0,16},{8,24},{16,0},{24,8},{1,17},{9,25},{17,1},{25,9},{2,18},{10... | collective-permute-start | bytes 442376 | tf_op jit(solution)/shard_map/ppermute | solution.py:33
  145.8 327.8 %collective-permute-start.47 = (bf16[1536,768]{1,0:T(8,128)(2,1)}, bf16[1536,768]{1,0:T(8,128)(2,1)}, u32[]{:S(2)}, u32[]{:S(2)}) collective-permute-start(bf16[1536,768]{1,0:T(8,128)(2,1)} %param.17), channel_id=1, source_target_pairs={{0,8},{8,0},{16,24},{24,16},{1,9},{9,1},{17,25},{25,17},{2,10},{10... | collective-permute-start | bytes 7077896 | tf_op jit(solution)/shard_map/ppermute | solution.py:33
  168.9 69.4 %collective-permute-start.48 = (bf16[768,768]{1,0:T(8,128)(2,1)}, bf16[768,768]{1,0:T(8,128)(2,1)}, u32[]{:S(2)}, u32[]{:S(2)}) collective-permute-start(bf16[768,768]{1,0:T(8,128)(2,1)} %constant_dynamic-slice_fusion.14), channel_id=1, source_target_pairs={{0,16},{8,24},{16,0},{24,8},{1,17},{9,25},{17,1},{25,9},{2,18},{10... | collective-permute-start | bytes 3538952 | tf_op jit(solution)/shard_map/ppermute | solution.py:33
  238.3 58.6 %collective-permute-start.46 = (bf16[384,768]{1,0:T(8,128)(2,1)}, bf16[384,768]{1,0:T(8,128)(2,1)}, u32[]{:S(2)}, u32[]{:S(2)}) collective-permute-start(bf16[384,768]{1,0:T(8,128)(2,1)} %collective-permute-done.44), channel_id=1, source_target_pairs={{0,8},{8,0},{16,24},{24,16},{1,9},{9,1},{17,25},{25,17},{2,10},{10... | collective-permute-start | bytes 1769480 | tf_op jit(solution)/shard_map/ppermute | solution.py:33
  238.7 230.0 %collective-permute-start.49 = (bf16[768,768]{1,0:T(8,128)(2,1)}, bf16[768,768]{1,0:T(8,128)(2,1)}, u32[]{:S(2)}, u32[]{:S(2)}) collective-permute-start(bf16[768,768]{1,0:T(8,128)(2,1)} %collective-permute-done.48), channel_id=1, source_target_pairs={{0,1},{1,0},{2,3},{3,2},{4,5},{5,4},{6,7},{7,6},{8,9},{9,8},{10,11... | collective-permute-start | bytes 3538952 | tf_op jit(solution)/shard_map/ppermute | solution.py:33
  239.2 244.1 %collective-permute-start.50 = (bf16[768,768]{1,0:T(8,128)(2,1)}, bf16[768,768]{1,0:T(8,128)(2,1)}, u32[]{:S(2)}, u32[]{:S(2)}) collective-permute-start(bf16[768,768]{1,0:T(8,128)(2,1)} %collective-permute-done.48), channel_id=1, source_target_pairs={{0,8},{8,0},{16,24},{24,16},{1,9},{9,1},{17,25},{25,17},{2,10},{10... | collective-permute-start | bytes 3538952 | tf_op jit(solution)/shard_map/ppermute | solution.py:33
  435.4 110.6 %collective-permute-start.95 = (bf16[2,8,192,384]{3,2,1,0:T(8,128)(2,1)}, bf16[2,8,192,384]{3,2,1,0:T(8,128)(2,1)}, u32[]{:S(2)}, u32[]{:S(2)}) collective-permute-start(bf16[2,8,192,384]{3,2,1,0:T(8,128)(2,1)} %fusion.21), channel_id=1, source_target_pairs={{0,8},{8,0},{16,24},{24,16},{1,9},{9,1},{17,25},{25,17},{2,10},{10... | collective-permute-start | bytes 7077896 | tf_op jit(solution)/shard_map/ppermute | solution.py:33
  473.2 76.1 %collective-permute-start.100 = (bf16[2,8,192,384]{3,2,1,0:T(8,128)(2,1)}, bf16[2,8,192,384]{3,2,1,0:T(8,128)(2,1)}, u32[]{:S(2)}, u32[]{:S(2)}) collective-permute-start(bf16[2,8,192,384]{3,2,1,0:T(8,128)(2,1)} %fusion.17), channel_id=1, source_target_pairs={{0,8},{8,0},{16,24},{24,16},{1,9},{9,1},{17,25},{25,17},{2,10},{10... | collective-permute-start | bytes 7077896 | tf_op jit(solution)/shard_map/ppermute | solution.py:33
  504.8 48.5 %collective-permute-start.83 = (bf16[2,8,192,384]{3,2,1,0:T(8,128)(2,1)}, bf16[2,8,192,384]{3,2,1,0:T(8,128)(2,1)}, u32[]{:S(2)}, u32[]{:S(2)}) collective-permute-start(bf16[2,8,192,384]{3,2,1,0:T(8,128)(2,1)} %fusion.29), channel_id=1, source_target_pairs={{0,8},{8,0},{16,24},{24,16},{1,9},{9,1},{17,25},{25,17},{2,10},{10... | collective-permute-start | bytes 7077896 | tf_op jit(solution)/shard_map/ppermute | solution.py:33
  553.3 50.1 %collective-permute-start.101 = (bf16[2,2,2,192,384]{4,3,2,1,0:T(8,128)(2,1)S(1)}, bf16[2,2,2,192,384]{4,3,2,1,0:T(8,128)(2,1)S(1)}, u32[]{:S(2)}, u32[]{:S(2)}) collective-permute-start(bf16[2,2,2,192,384]{4,3,2,1,0:T(8,128)(2,1)S(1)} %dynamic-slice_bitcast_fusion.2), channel_id=1, source_target_pairs={{0,1},{1,0},{2,3},{3,2},{4,5},{5,4},{6,7},{7,6},{8,9},{9,8},{10,11... | collective-permute-start | bytes 3538952 | tf_op jit(solution)/shard_map/ppermute | solution.py:33
  557.6 47.2 %collective-permute-start.84 = (bf16[2,2,2,192,384]{4,3,0,1,2:T(8,128)(2,1)S(1)}, bf16[2,2,2,192,384]{4,3,0,1,2:T(8,128)(2,1)S(1)}, u32[]{:S(2)}, u32[]{:S(2)}) collective-permute-start(bf16[2,2,2,192,384]{4,3,0,1,2:T(8,128)(2,1)S(1)} %bitcast.655), channel_id=1, source_target_pairs={{0,16},{8,24},{16,0},{24,8},{1,17},{9,25},{17,1},{25,9},{2,18},{10... | collective-permute-start | bytes 3538952 | tf_op jit(solution)/shard_map/ppermute | solution.py:33
  562.7 49.0 %collective-permute-start.90 = (bf16[2,2,2,192,384]{4,3,0,1,2:T(8,128)(2,1)S(1)}, bf16[2,2,2,192,384]{4,3,0,1,2:T(8,128)(2,1)S(1)}, u32[]{:S(2)}, u32[]{:S(2)}) collective-permute-start(bf16[2,2,2,192,384]{4,3,0,1,2:T(8,128)(2,1)S(1)} %bitcast.656), channel_id=1, source_target_pairs={{0,16},{8,24},{16,0},{24,8},{1,17},{9,25},{17,1},{25,9},{2,18},{10... | collective-permute-start | bytes 3538952 | tf_op jit(solution)/shard_map/ppermute | solution.py:33
  566.5 62.2 %collective-permute-start.72 = (bf16[2,2,2,192,384]{4,3,2,1,0:T(8,128)(2,1)S(1)}, bf16[2,2,2,192,384]{4,3,2,1,0:T(8,128)(2,1)S(1)}, u32[]{:S(2)}, u32[]{:S(2)}) collective-permute-start(bf16[2,2,2,192,384]{4,3,2,1,0:T(8,128)(2,1)S(1)} %dynamic-slice_bitcast_fusion.4), channel_id=1, source_target_pairs={{0,1},{1,0},{2,3},{3,2},{4,5},{5,4},{6,7},{7,6},{8,9},{9,8},{10,11... | collective-permute-start | bytes 3538952 | tf_op jit(solution)/shard_map/ppermute | solution.py:33
  578.2 58.9 %collective-permute-start.78 = (bf16[2,2,2,192,384]{4,3,0,1,2:T(8,128)(2,1)S(1)}, bf16[2,2,2,192,384]{4,3,0,1,2:T(8,128)(2,1)S(1)}, u32[]{:S(2)}, u32[]{:S(2)}) collective-permute-start(bf16[2,2,2,192,384]{4,3,0,1,2:T(8,128)(2,1)S(1)} %bitcast.657), channel_id=1, source_target_pairs={{0,16},{8,24},{16,0},{24,8},{1,17},{9,25},{17,1},{25,9},{2,18},{10... | collective-permute-start | bytes 3538952 | tf_op jit(solution)/shard_map/ppermute | solution.py:33
  603.4 46.2 %collective-permute-start.97 = (bf16[2,2,192,384]{3,2,1,0:T(8,128)(2,1)S(1)}, bf16[2,2,192,384]{3,2,1,0:T(8,128)(2,1)S(1)}, u32[]{:S(2)}, u32[]{:S(2)}) collective-permute-start(bf16[2,2,192,384]{3,2,1,0:T(8,128)(2,1)S(1)} %dynamic-slice_bitcast_fusion.6), channel_id=1, source_target_pairs={{0,16},{8,24},{16,0},{24,8},{1,17},{9,25},{17,1},{25,9},{2,18},{10... | collective-permute-start | bytes 1769480 | tf_op jit(solution)/shard_map/ppermute | solution.py:33
  604.9 57.5 %collective-permute-start.102 = (bf16[2,2,192,384]{3,2,1,0:T(8,128)(2,1)S(1)}, bf16[2,2,192,384]{3,2,1,0:T(8,128)(2,1)S(1)}, u32[]{:S(2)}, u32[]{:S(2)}) collective-permute-start(bf16[2,2,192,384]{3,2,1,0:T(8,128)(2,1)S(1)} %dynamic-slice_bitcast_fusion.5), channel_id=1, source_target_pairs={{0,16},{8,24},{16,0},{24,8},{1,17},{9,25},{17,1},{25,9},{2,18},{10... | collective-permute-start | bytes 1769480 | tf_op jit(solution)/shard_map/ppermute | solution.py:33
  611.8 52.5 %collective-permute-start.85 = (bf16[2,2,192,384]{3,2,0,1:T(8,128)(2,1)S(1)}, bf16[2,2,192,384]{3,2,0,1:T(8,128)(2,1)S(1)}, u32[]{:S(2)}, u32[]{:S(2)}) collective-permute-start(bf16[2,2,192,384]{3,2,0,1:T(8,128)(2,1)S(1)} %dynamic-slice_bitcast_fusion.8), channel_id=1, source_target_pairs={{0,1},{1,0},{2,3},{3,2},{4,5},{5,4},{6,7},{7,6},{8,9},{9,8},{10,11... | collective-permute-start | bytes 1769480 | tf_op jit(solution)/shard_map/ppermute | solution.py:33
  628.7 36.1 %collective-permute-start.91 = (bf16[2,2,192,384]{3,2,0,1:T(8,128)(2,1)S(1)}, bf16[2,2,192,384]{3,2,0,1:T(8,128)(2,1)S(1)}, u32[]{:S(2)}, u32[]{:S(2)}) collective-permute-start(bf16[2,2,192,384]{3,2,0,1:T(8,128)(2,1)S(1)} %dynamic-slice_bitcast_fusion.7), channel_id=1, source_target_pairs={{0,1},{1,0},{2,3},{3,2},{4,5},{5,4},{6,7},{7,6},{8,9},{9,8},{10,11... | collective-permute-start | bytes 1769480 | tf_op jit(solution)/shard_map/ppermute | solution.py:33
  637.0 37.5 %collective-permute-start.73 = (bf16[2,2,192,384]{3,2,1,0:T(8,128)(2,1)S(1)}, bf16[2,2,192,384]{3,2,1,0:T(8,128)(2,1)S(1)}, u32[]{:S(2)}, u32[]{:S(2)}) collective-permute-start(bf16[2,2,192,384]{3,2,1,0:T(8,128)(2,1)S(1)} %dynamic-slice_bitcast_fusion.10), channel_id=1, source_target_pairs={{0,16},{8,24},{16,0},{24,8},{1,17},{9,25},{17,1},{25,9},{2,18},{10... | collective-permute-start | bytes 1769480 | tf_op jit(solution)/shard_map/ppermute | solution.py:33
  677.1 33.1 %collective-permute-start.80 = (bf16[2,192,384]{2,1,0:T(8,128)(2,1)S(1)}, bf16[2,192,384]{2,1,0:T(8,128)(2,1)S(1)}, u32[]{:S(2)}, u32[]{:S(2)}) collective-permute-start(bf16[2,192,384]{2,1,0:T(8,128)(2,1)S(1)} %dynamic-slice_bitcast_fusion.21), channel_id=1, source_target_pairs={{0,2},{1,3},{2,0},{3,1},{4,6},{5,7},{6,4},{7,5},{8,10},{9,11},{10,... | collective-permute-start | bytes 884744 | tf_op jit(solution)/shard_map/ppermute | solution.py:33
  (259 other events, 2172.9 us)

commit v2 on v1

v2 whole, which is shorter than its diff:
```python
import functools

import jax
import jax.numpy as jnp
from jax import lax
from jax.experimental import pallas as pl
from jax.experimental.pallas import tpu as pltpu
from jax.sharding import PartitionSpec as P

HEAD_DIM = 64
PATCH = 8
CHUNK = 128

NORM_EPS = 1e-05
MASK_FILL = -1e30
BF = jnp.bfloat16
F32 = jnp.float32
GELU_A = 0.7978845608028654
GELU_B = 0.044715

ANY = pl.BlockSpec(memory_space=pl.ANY)
VMEM = pl.BlockSpec(memory_space=pltpu.VMEM)
SMEM = pl.BlockSpec(memory_space=pltpu.SMEM)


def dot_nn(left, right):
    return lax.dot_general(left, right, (((1,), (0,)), ((), ())), preferred_element_type=F32)


def dot_tn(left, right):
    return lax.dot_general(left, right, (((0,), (0,)), ((), ())), preferred_element_type=F32)


def dot_nt(left, right):
    return lax.dot_general(left, right, (((1,), (1,)), ((), ())), preferred_element_type=F32)


def bits_of(count):
    return count.bit_length() - 1


def swap(value, axis, mask):
    return lax.ppermute(value, axis, [(i, i ^ mask) for i in range(lax.axis_size(axis))])


def bit_at(axis, bit):
    return (lax.axis_index(axis) >> bit) & 1


def pick(value, index, axis):
    return lax.dynamic_index_in_dim(value, index, axis, keepdims=False)


def far_pieces(half):
    found = {0: half}
    pieces = {}
    for bit in reversed(range(1, bits_of(lax.axis_size("grp")))):
        for rel in list(found):
            first = swap(found[rel], "grp", 1 << bit)
            second = swap(first, "wide", 1)
            found[rel ^ (1 << bit)] = first
            pieces[rel ^ (1 << bit)] = (first, second)
    flat = []
    for rel in sorted(pieces):
        first, second = pieces[rel]
        flat += [first, second, swap(first, "grp", 1), swap(second, "grp", 1)]
    return flat


def start_all(copies, sem, base=0):
    made = []
    for at, (source, target) in enumerate(copies):
        made.append(pltpu.make_async_copy(source, target, sem.at[base + at]))
        made[-1].start()
    return made


def wait_all(made):
    for copy in made:
        copy.wait()


def piece_rows(place, chips, rows):
    me, side = place[0], place[1]
    half = rows // 2
    near = [(pl.multiple_of((me ^ rel) * rows, 16), rows) for rel in (0, 1)]
    far = []
    for chip in range(1, chips):
        for core in (0, 1):
            for other in (0, 1):
                base = (me ^ (2 * chip + core)) * rows + (side ^ other) * half
                far.append((pl.multiple_of(base, 16), half))
    return near, far


def attend_copies(place, block, chips, refs, weights):
    own_qkv, own_out, near_qkv, near_out = refs[:4]
    rows = own_out.shape[1]
    near, far = piece_rows(place, chips, rows)
    copies = []
    for (base, count), qkv, out in zip(near, (own_qkv, near_qkv), (own_out, near_out)):
        copies.append((qkv.at[block], weights.at[pl.ds(0, 3), pl.ds(base, count)]))
        copies.append((out.at[block], weights.at[3, pl.ds(base, count)]))
    for (base, count), piece in zip(far, refs[4:]):
        copies.append((piece, weights.at[:, pl.ds(base, count)]))
    return copies


def wide_copies(place, block, chips, refs, weights):
    own, near_one = refs[:2]
    pieces, _, columns = weights.shape
    near, far = piece_rows(place, chips, own.shape[1])
    copies = []
    for (base, count), source in zip(near + far, (own.at[block], near_one.at[block]) + tuple(refs[2:])):
        for at in range(pieces):
            copies.append((source.at[:, pl.ds(at * columns, columns)], weights.at[at, pl.ds(base, count)]))
    return copies


def tall_copies(place, block, chips, refs, weights):
    own, near_one = refs[:2]
    if block is not None:
        own, near_one = own.at[block], near_one.at[block]
    near, far = piece_rows(place, chips, own.shape[0])
    return [
        (source, weights.at[pl.ds(base, count)])
        for (base, count), source in zip(near + far, (own, near_one) + tuple(refs[2:]))
    ]


def far_count(chips):
    return 4 * (chips - 1)


def normalize(hidden):
    centered = hidden - jnp.mean(hidden, axis=-1, keepdims=True)
    spread = jnp.mean(centered * centered, axis=-1, keepdims=True)
    scale = lax.rsqrt(spread + NORM_EPS)
    return centered * scale, scale


def normalize_back(grad, unit, scale, gain):
    inner = grad * gain
    mean_one = jnp.mean(inner, axis=-1, keepdims=True)
    mean_two = jnp.mean(inner * unit, axis=-1, keepdims=True)
    return scale * (inner - mean_one - unit * mean_two)


def column_sum(value):
    return jnp.sum(value, axis=0, keepdims=True)


def pair_masks():
    lanes = lax.broadcasted_iota(jnp.int32, (1, 2 * HEAD_DIM), 1)
    low = (lanes < HEAD_DIM).astype(F32)
    return low, 1.0 - low


def group_mask(rows, span):
    at = lax.broadcasted_iota(jnp.int32, (2 * rows, rows), 0) & (rows - 1)
    to = lax.broadcasted_iota(jnp.int32, (2 * rows, rows), 1)
    return (to <= at) & ((to | (span - 1)) == (at | (span - 1)))


def stack_heads(pair, low, high):
    return jnp.concatenate([pair * low, pair * high], axis=0)


def join_heads(stacked, low, high):
    rows = stacked.shape[0] // 2
    return stacked[:rows] * low + stacked[rows:] * high


def soft(scores, allowed):
    scores = jnp.where(allowed, scores * (HEAD_DIM**-0.5), MASK_FILL)
    top = jnp.max(scores, axis=-1, keepdims=True)
    grown = jnp.exp(scores - top)
    return grown / jnp.sum(grown, axis=-1, keepdims=True)


def attend_forward_kernel(block, chips, span, summed, *refs):
    place = refs[0]
    count = 4 + far_count(chips)
    weight_refs = refs[1 : 1 + count]
    at = 1 + count
    if summed:
        hidden_refs = refs[at : at + 2 * chips + 1]
        at += 2 * chips + 1
    else:
        hidden_refs = refs[at : at + 1]
        at += 1
    gain_ref, bias_ref = refs[at : at + 2]
    at += 2
    outs = refs[at:-2]
    weights, sem = refs[-2:]
    copies = start_all(attend_copies(place, block, chips, weight_refs, weights), sem)
    if summed:
        hidden = hidden_refs[0][...] + hidden_refs[1][...]
        for ref in hidden_refs[2:]:
            hidden = hidden + ref[...].astype(F32)
        outs[3][...] = hidden
    else:
        hidden = hidden_refs[0][...].astype(F32)
    middle_ref, qkv_ref, mixed_ref = outs[:3]
    unit, _ = normalize(hidden)
    normed = (unit * gain_ref[block, 0:1, :] + bias_ref[block, 0:1, :]).astype(BF)
    wait_all(copies)
    for which in range(3):
        qkv_ref[which] = dot_nn(normed, weights[which]).astype(BF)
    total, width = hidden.shape
    rows = min(total, CHUNK)
    low, high = pair_masks()
    low_bf, high_bf = low.astype(BF), high.astype(BF)
    allowed = group_mask(rows, span)

    def one_chunk(number, carry):
        spot = pl.ds(pl.multiple_of(number * rows, rows), rows)
        for pair in range(width // (2 * HEAD_DIM)):
            lanes = slice(pair * 2 * HEAD_DIM, (pair + 1) * 2 * HEAD_DIM)
            query = stack_heads(qkv_ref[0, spot, lanes], low_bf, high_bf)
            probs = soft(dot_nt(query, qkv_ref[1, spot, lanes]), allowed).astype(BF)
            mixed = dot_nn(probs, qkv_ref[2, spot, lanes])
            mixed_ref[spot, lanes] = join_heads(mixed, low, high).astype(BF)
        return carry

    lax.fori_loop(0, total // rows, one_chunk, 0)
    middle_ref[...] = hidden + dot_nn(mixed_ref[...], weights[3])


def attend_forward(block, chips, span, place, weight_pieces, hidden, gains, biases, rows, width):
    summed = len(hidden) > 1
    outs = [
        jax.ShapeDtypeStruct((rows, width), F32),
        jax.ShapeDtypeStruct((3, rows, width), BF),
        jax.ShapeDtypeStruct((rows, width), BF),
    ]
    if summed:
        outs.append(jax.ShapeDtypeStruct((rows, width), F32))
    count = 4 + far_count(chips)
    return pl.pallas_call(
        functools.partial(attend_forward_kernel, block, chips, span, summed),
        out_shape=outs,
        in_specs=[SMEM] + [ANY] * count + [VMEM] * (len(hidden) + 2),
        out_specs=[VMEM] * len(outs),
        scratch_shapes=[pltpu.VMEM((4, width, width), BF), pltpu.SemaphoreType.DMA((count,))],
        compiler_params=pltpu.CompilerParams(vmem_limit_bytes=52 << 20),
        cost_estimate=pl.CostEstimate(
            flops=8 * rows * width * width, bytes_accessed=8 * width * width + 20 * rows * width, transcendentals=0
        ),
        name=f"attend_forward_{block}",
    )(place, *weight_pieces, *hidden, gains, biases)


def gelu_tanh(upper):
    inner = jnp.tanh(GELU_A * (upper + GELU_B * (upper * upper * upper)))
    return 0.5 * upper * (1.0 + inner)


def gelu_both(upper):
    square = upper * upper
    inner = jnp.tanh(GELU_A * (upper + GELU_B * (upper * square)))
    half = 0.5 * (1.0 + inner)
    slope = half + 0.5 * upper * (1.0 - inner * inner) * (GELU_A * (1.0 + 3.0 * GELU_B * square))
    return upper * half, slope


def feed_forward_kernel(block, chips, *refs):
    place = refs[0]
    count = 2 + far_count(chips)
    up_refs = refs[1 : 1 + count]
    down_refs = refs[1 + count : 1 + 2 * count]
    middle_ref, embedded_ref, gain_ref, bias_ref, up_bias_ref, down_bias_ref = refs[1 + 2 * count : 7 + 2 * count]
    local_ref, up, down, sem = refs[7 + 2 * count :]
    pieces, width, _ = up.shape
    up_copies = start_all(wide_copies(place, block, chips, up_refs, up), sem)
    down_copies = start_all(tall_copies(place, block, chips, down_refs, down), sem, count * pieces)
    middle = middle_ref[...]
    unit, _ = normalize(middle)
    normed = (unit * gain_ref[block, 1:2, :] + bias_ref[block, 1:2, :]).astype(BF)
    out = middle + down_bias_ref[block : block + 1, :]
    wait_all(up_copies)
    wait_all(down_copies)
    for at in range(pieces):
        columns = slice(at * width, (at + 1) * width)
        upper = dot_nn(normed, up[at]) + up_bias_ref[block : block + 1, columns]
        out = out + dot_nn(gelu_tanh(upper).astype(BF), down[columns, :])
    patches = middle.shape[0]
    spread = jnp.broadcast_to(out[:, None, :], (patches, PATCH, width)).reshape(patches * PATCH, width)
    local_ref[...] = (embedded_ref[...].astype(F32) + spread).astype(BF)


def feed_forward(block, chips, place, up_pieces, down_pieces, middle, embedded, gains, biases, up_bias, down_bias):
    rows, width = middle.shape
    hidden_width = up_bias.shape[1]
    pieces = hidden_width // width
    count = 2 + far_count(chips)
    return pl.pallas_call(
        functools.partial(feed_forward_kernel, block, chips),
        out_shape=jax.ShapeDtypeStruct(embedded.shape, BF),
        in_specs=[SMEM] + [ANY] * (2 * count) + [VMEM] * 6,
        out_specs=VMEM,
        scratch_shapes=[
            pltpu.VMEM((pieces, width, width), BF),
            pltpu.VMEM((hidden_width, width), BF),
            pltpu.SemaphoreType.DMA((count * pieces + count,)),
        ],
        compiler_params=pltpu.CompilerParams(vmem_limit_bytes=52 << 20),
        cost_estimate=pl.CostEstimate(
            flops=4 * rows * width * hidden_width, bytes_accessed=4 * width * hidden_width, transcendentals=0
        ),
        name=f"feed_forward_{block}",
    )(place, *up_pieces, *down_pieces, middle, embedded, gains, biases, up_bias, down_bias)


def feed_backward_kernel(block, chips, local, *refs):
    place = refs[0]
    count = 2 + far_count(chips)
    up_refs = refs[1 : 1 + count]
    down_refs = refs[1 + count : 1 + 2 * count]
    middle_ref, grad_ref, gain_ref, bias_ref, up_bias_ref, down_bias_ref = refs[1 + 2 * count : 7 + 2 * count]
    outs = refs[7 + 2 * count : -7]
    up, down, normed_ref, grad_low, grad_turned, total, sem = refs[-7:]
    up_term, down_term, middle_grad_ref, vector_ref = outs[:4]
    pieces, width, _ = up.shape
    lanes = up_term.shape[2]
    up_copies = start_all(wide_copies(place, block, chips, up_refs, up), sem)
    down_copies = start_all(tall_copies(place, block, chips, down_refs, down), sem, count * pieces)
    middle = middle_ref[...]
    rows = middle.shape[0]
    unit, _ = normalize(middle)
    normed_ref[...] = (unit * gain_ref[block, 1:2, :] + bias_ref[block, 1:2, :]).astype(BF)
    if local:
        positions = lax.broadcasted_iota(jnp.int32, (rows, 1), 0)
        keep = (positions < place[2]).astype(F32)
        low_grad = (grad_ref[...].astype(F32) * keep).astype(BF)
    else:
        low_grad = grad_ref[...].astype(BF)
    grad_low[...] = low_grad
    grad_turned[...] = low_grad.T
    total[...] = jnp.zeros_like(total)
    vector_ref[...] = jnp.zeros_like(vector_ref)
    vector_ref[pieces + 2 : pieces + 3, :] = column_sum(low_grad.astype(F32))
    wait_all(up_copies)
    wait_all(down_copies)
    out_total = refs[-8] if local else None
    if local:
        out_total[...] = middle + down_bias_ref[block : block + 1, :]

    def one_piece(at, carry):
        columns = pl.ds(pl.multiple_of(at * width, width), width)
        normed = normed_ref[...]
        upper = dot_nn(normed, up[at]) + up_bias_ref[block : block + 1, columns]
        active, slope = gelu_both(upper)
        active = active.astype(BF)
        if local:
            out_total[...] += dot_nn(active, down[columns, :])
        grad_upper_full = dot_nt(grad_low[...], down[columns, :]) * slope
        grad_upper = grad_upper_full.astype(BF)
        vector_ref[pl.ds(at, 1), :] = column_sum(grad_upper.astype(F32))
        down_part = dot_nn(grad_turned[...], active).astype(BF)
        for part in range(width // lanes):
            down_term[at * (width // lanes) + part] = down_part[:, part * lanes : (part + 1) * lanes]
        up_part = dot_tn(grad_upper, normed).astype(BF)
        for part in range(width // lanes):
            up_term[part, columns, :] = up_part[:, part * lanes : (part + 1) * lanes]
        total[...] += dot_nt(grad_upper, up[at])
        return carry

    lax.fori_loop(0, pieces, one_piece, 0)
    unit, scale = normalize(middle_ref[...])
    grad = total[...]
    vector_ref[pieces : pieces + 1, :] = column_sum(grad * unit)
    vector_ref[pieces + 1 : pieces + 2, :] = column_sum(grad)
    back = normalize_back(grad, unit, scale, gain_ref[block, 1:2, :])
    if local:
        middle_grad_ref[...] = grad_low[...].astype(F32) + back
        outs[4][...] = (out_total[...].astype(BF).astype(F32) * keep).astype(BF)
    else:
        middle_grad_ref[...] = grad_ref[...] + back


def feed_backward(block, chips, local, place, up_pieces, down_pieces, middle, grad, gains, biases, up_bias, down_bias):
    rows, width = middle.shape
    hidden_width = up_bias.shape[1]
    pieces = hidden_width // width
    lanes = width // chips
    count = 2 + far_count(chips)
    outs = [
        jax.ShapeDtypeStruct((chips, hidden_width, lanes), BF),
        jax.ShapeDtypeStruct((hidden_width // lanes, width, lanes), BF),
        jax.ShapeDtypeStruct((rows, width), F32),
        jax.ShapeDtypeStruct((8, width), F32),
    ]
    scratch = []
    if local:
        outs.append(jax.ShapeDtypeStruct((rows, width), BF))
        scratch.append(pltpu.VMEM((rows, width), F32))
    scratch += [
        pltpu.VMEM((pieces, width, width), BF),
        pltpu.VMEM((hidden_width, width), BF),
        pltpu.VMEM((rows, width), BF),
        pltpu.VMEM((rows, width), BF),
        pltpu.VMEM((width, rows), BF),
        pltpu.VMEM((rows, width), F32),
        pltpu.SemaphoreType.DMA((count * pieces + count,)),
    ]
    kernel = feed_backward_local if local else feed_backward_global
    return pl.pallas_call(
        functools.partial(kernel, block, chips),
        out_shape=outs,
        in_specs=[SMEM] + [ANY] * (2 * count) + [VMEM] * 6,
        out_specs=[VMEM] * len(outs),
        scratch_shapes=scratch,
        compiler_params=pltpu.CompilerParams(vmem_limit_bytes=56 << 20),
        cost_estimate=pl.CostEstimate(
            flops=12 * rows * width * hidden_width, bytes_accessed=8 * width * hidden_width, transcendentals=0
        ),
        name=f"feed_backward_{block}",
    )(place, *up_pieces, *down_pieces, middle, grad, gains, biases, up_bias, down_bias)


def feed_backward_local(block, chips, *refs):
    return feed_backward_kernel(block, chips, True, *refs)


def feed_backward_global(block, chips, *refs):
    return feed_backward_kernel(block, chips, False, *refs)


def attend_backward_kernel(block, chips, span, local, *refs):
    place = refs[0]
    count = 4 + far_count(chips)
    weight_refs = refs[1 : 1 + count]
    hidden_ref, grad_ref, qkv_ref, mixed_ref, gain_ref, bias_ref = refs[1 + count : 7 + count]
    outs = refs[7 + count : -4]
    weights, mixed_grad, grads, sem = refs[-4:]
    term_ref, vector_ref, low_ref, extra_ref = outs
    copies = start_all(attend_copies(place, block, chips, weight_refs, weights), sem)
    hidden = hidden_ref[...].astype(F32)
    total, width = hidden.shape
    lanes_out = term_ref.shape[3]
    unit, scale = normalize(hidden)
    normed = (unit * gain_ref[block, 0:1, :] + bias_ref[block, 0:1, :]).astype(BF)
    branch = grad_ref[...].astype(BF)
    out_term = dot_tn(branch, mixed_ref[...]).astype(BF)
    for part in range(chips):
        term_ref[part, 3] = out_term[:, part * lanes_out : (part + 1) * lanes_out]
    wait_all(copies)
    mixed_grad[...] = dot_nt(branch, weights[3]).astype(BF)
    rows = min(total, CHUNK)
    low, high = pair_masks()
    low_bf, high_bf = low.astype(BF), high.astype(BF)
    allowed = group_mask(rows, span)
    shrink = HEAD_DIM**-0.5

    def one_chunk(number, carry):
        spot = pl.ds(pl.multiple_of(number * rows, rows), rows)
        for pair in range(width // (2 * HEAD_DIM)):
            lanes = slice(pair * 2 * HEAD_DIM, (pair + 1) * 2 * HEAD_DIM)
            query = stack_heads(qkv_ref[0, spot, lanes], low_bf, high_bf)
            keyed = qkv_ref[1, spot, lanes]
            valued = qkv_ref[2, spot, lanes]
            above = stack_heads(mixed_grad[spot, lanes], low_bf, high_bf)
            probs = soft(dot_nt(query, keyed), allowed)
            grad_probs = dot_nt(above, valued)
            grads[2, spot, lanes] = dot_tn(probs.astype(BF), above).astype(BF)
            inner = jnp.sum(probs * grad_probs, axis=-1, keepdims=True)
            grad_scores = (probs * (grad_probs - inner)).astype(BF)
            grad_query = join_heads(dot_nn(grad_scores, keyed), low, high)
            grads[0, spot, lanes] = (grad_query * shrink).astype(BF)
            grads[1, spot, lanes] = (dot_tn(grad_scores, query) * shrink).astype(BF)
        return carry

    lax.fori_loop(0, total // rows, one_chunk, 0)
    grad = jnp.zeros((total, width), F32)
    for which in range(3):
        entry = grads[which]
        part_term = dot_tn(entry, normed).astype(BF)
        for part in range(chips):
            term_ref[part, which] = part_term[:, part * lanes_out : (part + 1) * lanes_out]
        grad = grad + dot_nt(entry, weights[which])
    vector_ref[...] = jnp.zeros_like(vector_ref)
    vector_ref[0:1, :] = column_sum(grad * unit)
    vector_ref[1:2, :] = column_sum(grad)
    result = grad_ref[...] + normalize_back(grad, unit, scale, gain_ref[block, 0:1, :])
    result_low = result.astype(BF)
    low_ref[...] = result_low
    rounded = result_low.astype(F32)
    if local:
        extra_ref[...] = jnp.sum(rounded.reshape(total // PATCH, PATCH, width), axis=1)
    else:
        vector_ref[2:3, :] = column_sum(rounded)
        wides = extra_ref.shape[0]
        columns = width // wides
        for at in range(wides):
            block_out = rounded[:, at * columns : (at + 1) * columns]
            if extra_ref.shape[2] > columns:
                block_out = jnp.pad(block_out, ((0, 0), (0, extra_ref.shape[2] - columns)))
            extra_ref[at] = block_out.astype(BF)


def attend_backward(block, chips, wides, span, local, place, weight_pieces, hidden, grad, qkv, mixed, gains, biases):
    rows, width = hidden.shape
    lanes = width // chips
    padded = -(-(width // wides) // 128) * 128
    outs = [
        jax.ShapeDtypeStruct((chips, 4, width, lanes), BF),
        jax.ShapeDtypeStruct((8, width), F32),
        jax.ShapeDtypeStruct((rows, width), BF),
        jax.ShapeDtypeStruct((rows // PATCH, width), F32) if local else jax.ShapeDtypeStruct((wides, rows, padded), BF),
    ]
    count = 4 + far_count(chips)
    return pl.pallas_call(
        functools.partial(attend_backward_kernel, block, chips, span, local),
        out_shape=outs,
        in_specs=[SMEM] + [ANY] * count + [VMEM] * 6,
        out_specs=[VMEM] * 4,
        scratch_shapes=[
            pltpu.VMEM((4, width, width), BF),
            pltpu.VMEM((rows, width), BF),
            pltpu.VMEM((3, rows, width), BF),
            pltpu.SemaphoreType.DMA((count,)),
        ],
        compiler_params=pltpu.CompilerParams(vmem_limit_bytes=52 << 20),
        cost_estimate=pl.CostEstimate(
            flops=16 * rows * width * width, bytes_accessed=16 * width * width, transcendentals=0
        ),
        name=f"attend_backward_{block}",
    )(place, *weight_pieces, hidden, grad, qkv, mixed, gains, biases)


def embed_kernel(spots, groups, *refs):
    ids_ref, spot_ids_ref = refs[:2]
    table_refs = refs[2 : 2 + groups]
    weight_ref, embedded_ref, own_ref, part_ref = refs[2 + groups :]
    table = jnp.concatenate([ref[...] for ref in table_refs], axis=0)
    vocab, width = table.shape

    def hot(ids):
        at = lax.broadcasted_iota(jnp.int32, (vocab, ids.shape[1]), 0)
        return (at == ids).astype(F32).astype(BF)

    total = None
    for spot in range(spots):
        rows = dot_tn(hot(spot_ids_ref[spot : spot + 1, :]), table).astype(BF)
        term = dot_nn(rows, weight_ref[spot * width : (spot + 1) * width, :])
        total = term if total is None else total + term
    patches = own_ref.shape[0]
    own_ref[...] = total[:patches]
    for rel in range(1, groups):
        part_ref[rel - 1] = total[rel * patches : (rel + 1) * patches].astype(BF)
    embedded_ref[...] = dot_tn(hot(ids_ref[...]), table).astype(BF)


def embed(ids, spot_ids, tables, patch_weight, patches):
    groups = len(tables)
    width = tables[0].shape[1]
    spots = spot_ids.shape[0]
    return pl.pallas_call(
        functools.partial(embed_kernel, spots, groups),
        out_shape=[
            jax.ShapeDtypeStruct((ids.shape[1], width), BF),
            jax.ShapeDtypeStruct((patches, width), F32),
            jax.ShapeDtypeStruct((groups - 1, patches, width), BF),
        ],
        in_specs=[VMEM] * (3 + groups),
        out_specs=[VMEM] * 3,
        compiler_params=pltpu.CompilerParams(vmem_limit_bytes=40 << 20),
        name="embed",
    )(ids, spot_ids, *tables, patch_weight)


def patch_backward_kernel(chips, *refs):
    place = refs[0]
    count = 2 + far_count(chips)
    weight_refs = refs[1 : 1 + count]
    ids_ref, grad_ref, local_ref, rows_ref, table_ref, weights, spread, sem = refs[1 + count :]
    copies = start_all(tall_copies(place, None, chips, weight_refs, weights), sem)
    grad = grad_ref[...]
    patches, width = grad.shape
    vocab = table_ref.shape[0] * table_ref.shape[2]
    wait_all(copies)
    for spot in range(PATCH):
        part = dot_nt(grad, weights[spot * width : (spot + 1) * width, :])
        for tile in range(width // 128):
            lanes = slice(tile * 128, (tile + 1) * 128)
            spread[tile, pl.ds(spot, patches, stride=PATCH), :] = part[:, lanes]
    whole = jnp.concatenate([spread[tile] for tile in range(width // 128)], axis=1)
    rows = (local_ref[...].astype(F32) + whole).astype(BF)
    rows_ref[...] = rows
    at = lax.broadcasted_iota(jnp.int32, (vocab, ids_ref.shape[1]), 0)
    hot = (at == ids_ref[...]).astype(F32).astype(BF)
    term = dot_nn(hot, rows).T.astype(BF)
    lanes = table_ref.shape[2]
    for part in range(chips):
        table_ref[part] = term[:, part * lanes : (part + 1) * lanes]


def patch_backward(chips, vocab, place, pieces, ids, grad_summary, grad_local):
    patches, width = grad_summary.shape
    count = 2 + far_count(chips)
    return pl.pallas_call(
        functools.partial(patch_backward_kernel, chips),
        out_shape=[
            jax.ShapeDtypeStruct(grad_local.shape, BF),
            jax.ShapeDtypeStruct((chips, width, vocab // chips), BF),
        ],
        in_specs=[SMEM] + [ANY] * count + [VMEM] * 3,
        out_specs=[VMEM] * 2,
        scratch_shapes=[
            pltpu.VMEM((PATCH * width, width), BF),
            pltpu.VMEM((width // 128, grad_local.shape[0], 128), F32),
            pltpu.SemaphoreType.DMA((count,)),
        ],
        compiler_params=pltpu.CompilerParams(vmem_limit_bytes=52 << 20),
        name="patch_backward",
    )(place, *pieces, ids, grad_summary, grad_local)


def patch_weight_kernel(spots, groups, *refs):
    ids_ref, grads_ref = refs[:2]
    table_refs = refs[2 : 2 + groups]
    out_ref = refs[-1]
    table = jnp.concatenate([ref[...] for ref in table_refs], axis=0)
    vocab, width = table.shape
    grads = grads_ref[...]
    for spot in range(spots):
        at = lax.broadcasted_iota(jnp.int32, (vocab, ids_ref.shape[1]), 0)
        hot = (at == ids_ref[spot : spot + 1, :]).astype(F32).astype(BF)
        counts = dot_nn(hot, grads).astype(BF)
        out_ref[spot * width : (spot + 1) * width, :] = dot_tn(table, counts)[:, : out_ref.shape[1]]


def patch_weight_term(ids, grads, tables, columns):
    spots = ids.shape[0]
    width = tables[0].shape[1]
    return pl.pallas_call(
        functools.partial(patch_weight_kernel, spots, len(tables)),
        out_shape=jax.ShapeDtypeStruct((spots * width, columns), F32),
        in_specs=[VMEM] * (2 + len(tables)),
        out_specs=VMEM,
        compiler_params=pltpu.CompilerParams(vmem_limit_bytes=40 << 20),
        name="patch_weight_term",
    )(ids, grads, *tables)


def reduce_steps(terms, core_at, steps):
    alive = list(range(terms.ndim))
    acc = terms
    for number, (axis, bit, dimension) in enumerate([("grp", 0, core_at)] + steps):
        at = alive.index(dimension)
        alive.pop(at)
        mine = bit_at(axis, bit)
        got = swap(pick(acc, 1 - mine, at), axis, 1 << bit)
        acc = pick(acc, mine, at).astype(F32) + got.astype(F32)
        if number < len(steps):
            acc = acc.astype(BF)
    return acc


def body(
    byte_ids,
    item_lengths,
    embed_table,
    patch_weight,
    patch_bias,
    norm_gain,
    norm_bias,
    qkv_weight,
    out_weight,
    up_weight,
    up_bias,
    down_weight,
    down_bias,
    out_cot,
):
    groups = lax.axis_size("grp")
    wides = lax.axis_size("wide")
    chips = groups // 2
    chip_bits = bits_of(chips)
    grp_bits = bits_of(groups)
    wide_bits = bits_of(wides)
    me = lax.axis_index("grp")
    core = bit_at("grp", 0)
    side = bit_at("wide", 0)
    width = embed_table.shape[1]
    vocab_rows = embed_table.shape[0]
    vocab = vocab_rows * groups
    byte_count = byte_ids.shape[0]
    patch_count = byte_count // PATCH
    own_spots = PATCH // groups
    hidden_width = up_bias.shape[1]
    place = jnp.stack([me, side, item_lengths[0]]).astype(jnp.int32)

    def own_half(value, dim):
        rows = value.shape[dim] // 2
        return lax.dynamic_slice_in_dim(value, side * rows, rows, dim)

    valid = jnp.arange(byte_count, dtype=jnp.int32) < item_lengths[0]
    ids = jnp.where(valid, byte_ids, -1)
    spots_first = ids.reshape(patch_count, PATCH).T
    tables = [embed_table] + [swap(embed_table, "grp", rel) for rel in range(1, groups)]
    ids_grp = jnp.stack([spots_first] + [swap(spots_first, "grp", rel) for rel in range(1, groups)], axis=1)
    spot_ids = lax.dynamic_slice_in_dim(ids_grp, me * own_spots, own_spots, 0)

    def moved(numbers):
        return jnp.where(numbers < 0, -1, numbers ^ (me * vocab_rows))

    near_qkv, near_out, near_up, near_down = (
        swap(entry, "grp", 1) for entry in (qkv_weight, out_weight, up_weight, down_weight)
    )

    def block_pieces(at):
        attend_half = jnp.concatenate([own_half(qkv_weight[at], 1), own_half(out_weight[at], 0)[None]])
        return (
            [qkv_weight, out_weight, near_qkv, near_out] + far_pieces(attend_half),
            [up_weight, near_up] + far_pieces(own_half(up_weight[at], 0)),
            [down_weight, near_down] + far_pieces(own_half(down_weight[at], 0)),
        )

    g_attend_w, g_up_w, g_down_w = block_pieces(0)
    embedded, summary_own, summary_parts = embed(
        moved(ids)[None], moved(spot_ids).reshape(own_spots, -1), tables, patch_weight, patch_count
    )
    arrived = [swap(summary_parts[rel - 1], "grp", rel) for rel in range(1, groups)]
    l_attend_w, l_up_w, l_down_w = block_pieces(1)
    patch_w = [patch_weight, swap(patch_weight, "grp", 1)] + far_pieces(own_half(patch_weight, 0))

    ids_all = spot_ids[:, :, None, :]
    for bit in range(wide_bits):
        ids_all = jnp.concatenate([ids_all, swap(ids_all, "wide", 1 << bit)], axis=2)

    norm = (norm_gain, norm_bias)
    feed = (norm_gain, norm_bias, up_bias, down_bias)
    g_middle, g_qkv, g_mixed, summary = attend_forward(
        0, chips, patch_count, place, g_attend_w, [summary_own, patch_bias[None]] + arrived, *norm, patch_count, width
    )
    local_in = feed_forward(0, chips, place, g_up_w, g_down_w, g_middle, embedded, *feed)
    l_middle, l_qkv, l_mixed = attend_forward(
        1, chips, PATCH, place, l_attend_w, [local_in], *norm, byte_count, width
    )
    l_up, l_down, l_grad, l_feed_vector, local_out = feed_backward(
        1, chips, True, place, l_up_w, l_down_w, l_middle, out_cot, *feed
    )
    l_attend, l_attend_vector, grad_local, grad_global = attend_backward(
        1, chips, wides, PATCH, True, place, l_attend_w, local_in, l_grad, l_qkv, l_mixed, *norm
    )

    pair = (2,)
    columns = width // wides
    lanes = width // chips

    def orders(chip_base, wide_base):
        chip = [("grp", b + 1, chip_base + chip_bits - 1 - b) for b in range(chip_bits)]
        wide = [("wide", b, wide_base + wide_bits - 1 - b) for b in range(wide_bits)]
        return chip, wide

    def reduce_up(term):
        shaped = term.reshape(pair * (chip_bits + wide_bits) + (2, hidden_width // wides // 2, lanes))
        chip, wide = orders(0, chip_bits)
        return reduce_steps(shaped, chip_bits + wide_bits, chip + wide)

    def reduce_down(term):
        many = hidden_width // lanes // chips // 2
        shaped = term.reshape(pair * (chip_bits + 1) + (many,) + pair * wide_bits + (columns, lanes))
        chip, wide = orders(0, chip_bits + 2)
        return reduce_steps(shaped, chip_bits, wide[:1] + chip + wide[1:])

    def reduce_attend(term, chip_first):
        shaped = term.reshape(pair * (chip_bits + 2) + pair * wide_bits + (columns, lanes))
        chip, wide = orders(0, chip_bits + 2)
        return reduce_steps(shaped, chip_bits, chip + wide if chip_first else wide[:1] + chip + wide[1:])

    l_up = reduce_up(l_up)
    l_down = reduce_down(l_down)
    l_attend = reduce_attend(l_attend, True)

    g_up, g_down, g_grad, g_feed_vector = feed_backward(
        0, chips, False, place, g_up_w, g_down_w, g_middle, grad_global, *feed
    )
    g_attend, g_attend_vector, grad_summary, summary_columns = attend_backward(
        0, chips, wides, patch_count, False, place, g_attend_w, summary, g_grad, g_qkv, g_mixed, *norm
    )
    g_up = reduce_up(g_up)
    g_down = reduce_down(g_down)
    g_attend = reduce_attend(g_attend, False)

    padded = summary_columns.shape[2]
    collected = summary_columns.reshape(pair * wide_bits + (patch_count, padded))
    for bit in range(wide_bits):
        at = wide_bits - 1 - bit
        mine = bit_at("wide", bit)
        collected = jnp.concatenate(
            [pick(collected, mine, at), swap(pick(collected, 1 - mine, at), "wide", 1 << bit)], axis=at
        )
    for bit in range(grp_bits):
        collected = jnp.concatenate([collected, swap(collected, "grp", 1 << bit)], axis=0)
    patch_weight_grad = patch_weight_term(moved(ids_all).reshape(own_spots, -1), collected, tables, columns)

    embed_rows_grad, table_term = patch_backward(chips, vocab, place, patch_w, ids[None], grad_summary, grad_local)
    shaped = table_term.reshape(pair * (chip_bits + wide_bits) + (2, columns // 2, vocab // chips))
    chip, wide = orders(0, chip_bits)
    table_half = reduce_steps(shaped, chip_bits + wide_bits, chip + wide)

    vector = jnp.stack([g_feed_vector, l_feed_vector, g_attend_vector, l_attend_vector])
    for axis, count in (("grp", grp_bits), ("wide", wide_bits)):
        for bit in range(count):
            vector = vector + swap(vector, axis, 1 << bit)
    pieces = hidden_width // width
    feed_vector, attend_vector = vector[:2], vector[2:]
    patch_bias_grad = attend_vector[0, 2]
    norm_gain_grad = jnp.stack([attend_vector[:, 0], feed_vector[:, pieces]], axis=1)
    norm_bias_grad = jnp.stack([attend_vector[:, 1], feed_vector[:, pieces + 1]], axis=1)
    up_bias_grad = feed_vector[:, :pieces].reshape(2, hidden_width)
    down_bias_grad = feed_vector[:, pieces + 2]

    def split_lanes(half):
        lanes_half = half.shape[-1] // 2
        low, high = half[..., :lanes_half], half[..., lanes_half:]
        mine = jnp.where(core == 0, low, high)
        return mine, swap(jnp.where(core == 0, high, low), "grp", 1)

    def join(half, axis):
        mine, other = split_lanes(half)
        return jnp.where(core == 0, jnp.concatenate([mine, other], axis), jnp.concatenate([other, mine], axis))

    def finish_down(half):
        return jnp.swapaxes(half, 1, 2).reshape(-1, columns)

    g_attend = jnp.swapaxes(join(g_attend, 0), 1, 2)
    l_attend = jnp.swapaxes(join(l_attend, 0), 1, 2)
    return (
        local_out,
        embed_rows_grad,
        join(table_half, 0).T,
        patch_weight_grad,
        patch_bias_grad,
        norm_gain_grad,
        norm_bias_grad,
        jnp.stack([g_attend[:3], l_attend[:3]]),
        jnp.stack([g_attend[3], l_attend[3]]),
        jnp.stack([join(g_up, 0).T, join(l_up, 0).T]),
        up_bias_grad,
        jnp.stack([finish_down(g_down), finish_down(l_down)]),
        down_bias_grad,
    )


def solution(mesh):
    placed = (
        P(("grp", "wide")),
        P(("grp", "wide")),
        P("grp", None),
        P("grp", None),
        P(),
        P(),
        P(),
        P(None, None, "grp", None),
        P(None, "grp", None),
        P(None, "grp", None),
        P(),
        P(None, "grp", None),
        P(),
        P(("grp", "wide"), None),
    )
    return jax.shard_map(
        body,
        mesh=mesh,
        in_specs=placed,
        out_specs=(
            P(("grp", "wide"), None),
            P(("grp", "wide"), None),
            P("grp", "wide"),
            P("grp", "wide"),
            P(),
            P(),
            P(),
            P(None, None, "grp", "wide"),
            P(None, "grp", "wide"),
            P(None, "grp", "wide"),
            P(),
            P(None, "grp", "wide"),
            P(),
        ),
        check_vma=False,
    )
```

time: 751 us -> 555 us (0.74)
  matrix products: 154 us -> 0 us
  local copies, waits for them, and re-layouts: 195 us -> 64.8 us
  Pallas kernels: 0 us -> 111 us
  other arithmetic: 75.6 us -> 23.1 us
  waiting for transfers between devices: 240 us -> 270 us
  starting transfers between devices: 69.2 us -> 77 us
    dot_general x80 -> x0, matrix products: 154 us -> none  [the longest x38 47.9 us: weight_term(): lax.dot_general(left, right, (((0,), (0,)), ((), ())), preferred_element_...]
    pallas_call x0 -> x10, Pallas kernels: none -> 111 us  [the longest x2 40.4 us: feed_backward(): pl.pallas_call(functools.partial(kernel, block, chips), out_shape=outs, i...]
    dynamic_update_slice x52 -> x0, local copies, waits for them, and re-layouts: 60.7 us -> none  [the longest x16 22.8 us: gather_weight(): lax.dynamic_update_slice_in_dim(out, second, base + (1 - side) * half, dim)]
    ppermute x105 -> x95, waiting for transfers between devices: 240 us -> 270 us  [swap(): lax.ppermute(value, axis, [(i, i ^ mask) for i in range(lax.axis_size(axi...]
    convert_element_type x12 -> x0, local copies, waits for them, and re-layouts: 24 us -> none  [the longest x4 8 us: block_backward(): grad_query = grad_query.reshape(rows_total, -1).astype(BF)]
    reshape x22 -> x2, local copies, waits for them, and re-layouts: 21.9 us -> 0.17 us  [the longest x1 0.08 us: body(): moved(spot_ids).reshape(own_spots, -1)]
    squeeze x27 -> x35, local copies, waits for them, and re-layouts: 4.96 us -> 21.4 us  [pick(): return lax.dynamic_index_in_dim(value, index, axis, keepdims=False)]
    another operation x14 -> x4, local copies, waits for them, and re-layouts: 15.8 us -> 2.52 us  [body(): jnp.stack([spots_first] + [swap(spots_first, 'grp', rel) for rel in range...]
  transfers between devices with their start and end apart: 105 -> 95, of which waited for: 40 -> 41; matrix products, arithmetic and copies ran while one was open for 53% -> 13% of each run, Pallas kernels for 0% -> 20%
where the time goes in v2:
time: 555 us; the launch traced here: 549 us
  waiting for transfers between devices  270 us (49%)
  Pallas kernels  111 us (20%)
  starting transfers between devices  77 us (14%)
  local copies, waits for them, and re-layouts  64.8 us (12%)
  other arithmetic  23.1 us (4%)
    ppermute x95, waiting for transfers between devices, swap(): lax.ppermute(value, axis, [(i, i ^ mask) for i in range(lax.axis_size(axi...  270 us
    ppermute x95, starting transfers between devices, swap(): lax.ppermute(value, axis, [(i, i ^ mask) for i in range(lax.axis_size(axi...  77 us
    pallas_call x2, Pallas kernels, feed_backward(): pl.pallas_call(functools.partial(kernel, block, chips), out_shape=outs, i...  40.4 us
    pallas_call x2, Pallas kernels, attend_backward(): pl.pallas_call(functools.partial(attend_backward_kernel, block, chips, sp...  33.2 us
    squeeze x35, local copies, waits for them, and re-layouts, pick(): return lax.dynamic_index_in_dim(value, index, axis, keepdims=False)  21.4 us
    unnamed x156, local copies, waits for them, and re-layouts  20 us
    convert_element_type x28, other arithmetic, reduce_steps(): acc = acc.astype(BF)  17.4 us
    pallas_call x2, Pallas kernels, attend_forward(): pl.pallas_call(functools.partial(attend_forward_kernel, block, chips, spa...  16.9 us
  transfers between devices with their start and end apart: 95, of which 41 were waited for; matrix products, arithmetic and copies ran while one was open for 13% of the time, Pallas kernels for 20%

profile of v2, /device:TPU:0, one launch (start us, length us, event | category | flops | bytes accessed | tf_op | source)
XLA Modules:
  0.0 549.3 jit_solution(14995251293522253267)
XLA Ops:
  40.7 18.7 %collective-permute-done.35.refs_12_ = bf16[64,768]{1,0:T(8,128)(2,1)S(1)} collective-permute-done((bf16[64,768]{1,0:T(8,128)(2,1)S(1)}, bf16[64,768]{1,0:T(8,128)(2,1)S(1)}, u32[]{:S(2)}, u32[]{:S(2)}) %collective-permute-start.35) | collective-permute-done | bytes 98336 | tf_op jit(solution)/shard_map/ppermute | solution.py:43
  65.2 10.4 %collective-permute-done.20.refs_9_ = bf16[384,768]{1,0:T(8,128)(2,1)S(1)} collective-permute-done((bf16[384,768]{1,0:T(8,128)(2,1)S(1)}, bf16[384,768]{1,0:T(8,128)(2,1)S(1)}, u32[]{:S(2)}, u32[]{:S(2)}) %collective-permute-start.20) | collective-permute-done | bytes 589856 | tf_op jit(solution)/shard_map/ppermute | solution.py:43
  75.6 12.6 %collective-permute-done.12.refs_5_ = bf16[4,96,768]{2,1,0:T(8,128)(2,1)S(1)} collective-permute-done((bf16[4,96,768]{2,1,0:T(8,128)(2,1)S(1)}, bf16[4,96,768]{2,1,0:T(8,128)(2,1)S(1)}, u32[]{:S(2)}, u32[]{:S(2)}) %collective-permute-start.12) | collective-permute-done | bytes 589856 | tf_op jit(solution)/shard_map/ppermute | solution.py:43
  89.9 11.1 %collective-permute-done.1.refs_3_ = bf16[96,3072]{1,0:T(8,128)(2,1)} collective-permute-done((bf16[96,3072]{1,0:T(8,128)(2,1)S(1)}, bf16[96,3072]{1,0:T(8,128)(2,1)}, u32[]{:S(2)}, u32[]{:S(2)}) %collective-permute-start.1) | collective-permute-done | bytes 589856 | tf_op jit(solution)/shard_map/ppermute | solution.py:43
  101.0 10.0 %collective-permute-done.6.refs_9_ = bf16[384,768]{1,0:T(8,128)(2,1)} collective-permute-done((bf16[384,768]{1,0:T(8,128)(2,1)S(1)}, bf16[384,768]{1,0:T(8,128)(2,1)}, u32[]{:S(2)}, u32[]{:S(2)}) %collective-permute-start.6) | collective-permute-done | bytes 589856 | tf_op jit(solution)/shard_map/ppermute | solution.py:43
  115.4 12.0 %collective-permute-done.21.refs_10_ = bf16[384,768]{1,0:T(8,128)(2,1)S(1)} collective-permute-done((bf16[384,768]{1,0:T(8,128)(2,1)S(1)}, bf16[384,768]{1,0:T(8,128)(2,1)S(1)}, u32[]{:S(2)}, u32[]{:S(2)}) %collective-permute-start.21) | collective-permute-done | bytes 589856 | tf_op jit(solution)/shard_map/ppermute | solution.py:43
  127.9 9.1 %collective-permute-done.13.refs_6_ = bf16[4,96,768]{2,1,0:T(8,128)(2,1)S(1)} collective-permute-done((bf16[4,96,768]{2,1,0:T(8,128)(2,1)S(1)}, bf16[4,96,768]{2,1,0:T(8,128)(2,1)S(1)}, u32[]{:S(2)}, u32[]{:S(2)}) %collective-permute-start.13) | collective-permute-done | bytes 589856 | tf_op jit(solution)/shard_map/ppermute | solution.py:43
  139.1 14.5 %collective-permute-done.2.refs_4_ = bf16[96,3072]{1,0:T(8,128)(2,1)} collective-permute-done((bf16[96,3072]{1,0:T(8,128)(2,1)}, bf16[96,3072]{1,0:T(8,128)(2,1)}, u32[]{:S(2)}, u32[]{:S(2)}) %collective-permute-start.2) | collective-permute-done | bytes 589856 | tf_op jit(solution)/shard_map/ppermute | solution.py:43
  153.6 8.2 %collective-permute-done.7.refs_10_ = bf16[384,768]{1,0:T(8,128)(2,1)} collective-permute-done((bf16[384,768]{1,0:T(8,128)(2,1)}, bf16[384,768]{1,0:T(8,128)(2,1)}, u32[]{:S(2)}, u32[]{:S(2)}) %collective-permute-start.7) | collective-permute-done | bytes 589856 | tf_op jit(solution)/shard_map/ppermute | solution.py:43
  182.6 8.1 %feed_forward_0.1.refs_9_ = bf16[512,768]{1,0:T(8,128)(2,1)} custom-call(s32[3]{0:T(128)S(1)} %pad_add_fusion.3.refs_0_, bf16[2,192,3072]{2,1,0:T(8,128)(2,1)} %refs_1_.13, bf16[2,192,3072]{2,1,0:T(8,128)(2,1)} %collective-permute-done.refs_2_, bf16[96,3072]{1,0:T(8,128)(2,1)S(1)} %collective-permute-done.16.refs_3_, ...), custom_call_target="tpu_custom_call" | custom-call | flops 603979776 | bytes 9437184 | tf_op jit(solution)/shard_map/feed_forward_0/pallas_call | solution.py:297
  190.7 11.4 %attend_forward_1.1 = (f32[512,768]{1,0:T(8,128)}, bf16[3,512,768]{2,1,0:T(8,128)(2,1)}, bf16[512,768]{1,0:T(8,128)(2,1)}) custom-call(s32[3]{0:T(128)S(1)} %pad_add_fusion.3.refs_0_, bf16[2,3,192,768]{3,2,1,0:T(8,128)(2,1)} %refs_1_.14, bf16[2,192,768]{2,1,0:T(8,128)(2,1)S(1)} %copy-done.1, bf16[2,3,192,768]{3,2,1,0:T(8,128)(2,1)} %collective-permute-done.10.refs_3_, ...), custom_call_target="tpu_custom_call" | custom-call | flops 2415919104 | bytes 12582912 | tf_op jit(solution)/shard_map/attend_forward_1/pallas_call | solution.py:240
  202.8 26.0 %feed_backward_1.1 = (bf16[2,3072,384]{2,1,0:T(8,128)(2,1)}, bf16[8,768,384]{2,1,0:T(8,128)(2,1)}, f32[512,768]{1,0:T(8,128)}, f32[8,768]{1,0:T(8,128)}, bf16[512,768]{1,0:T(8,128)(2,1)}) custom-call(s32[3]{0:T(128)} %copy-done.31, bf16[2,192,3072]{2,1,0:T(8,128)(2,1)} %refs_1_.13, bf16[2,192,3072]{2,1,0:T(8,128)(2,1)} %collective-permute-done.refs_2_, ...), custom_call_target="tpu_custom_call" | custom-call | flops 14495514624 | bytes 18874368 | tf_op jit(solution)/shard_map/feed_backward_1/pallas_call | solution.py:408
  228.9 22.4 %attend_backward_1.1 = (bf16[2,4,768,384]{3,2,1,0:T(8,128)(2,1)}, f32[8,768]{1,0:T(8,128)S(1)}, bf16[512,768]{1,0:T(8,128)(2,1)}, f32[64,768]{1,0:T(8,128)S(1)}) custom-call(s32[3]{0:T(128)S(1)} %copy-done.32, bf16[2,3,192,768]{3,2,1,0:T(8,128)(2,1)} %refs_1_.14, bf16[2,192,768]{2,1,0:T(8,128)(2,1)S(1)} %copy-done.1, ...), custom_call_target="tpu_custom_call" | custom-call | flops 4831838208 | bytes 9437184 | tf_op jit(solution)/shard_map/attend_backward_1/pallas_call | solution.py:513
  252.0 14.4 %feed_backward_0.1 = (bf16[2,3072,384]{2,1,0:T(8,128)(2,1)}, bf16[8,768,384]{2,1,0:T(8,128)(2,1)}, f32[64,768]{1,0:T(8,128)}, f32[8,768]{1,0:T(8,128)}) custom-call(s32[3]{0:T(128)} %copy-done.31, bf16[2,192,3072]{2,1,0:T(8,128)(2,1)} %refs_1_.13, bf16[2,192,3072]{2,1,0:T(8,128)(2,1)} %collective-permute-done.refs_2_, bf16[96,3072]{1,0:T(8,128)(2,1)} %copy-done.2, ...), custom_call_target="tpu_custom_call" | custom-call | flops 1811939328 | bytes 18874368 | tf_op jit(solution)/shard_map/feed_backward_0/pallas_call | solution.py:408
  270.4 10.8 %attend_backward_0.1 = (bf16[2,4,768,384]{3,2,1,0:T(8,128)(2,1)}, f32[8,768]{1,0:T(8,128)S(1)}, bf16[64,768]{1,0:T(8,128)(2,1)S(1)}, bf16[8,64,128]{2,1,0:T(8,128)(2,1)S(1)}) custom-call(s32[3]{0:T(128)S(1)} %copy-done.33, bf16[2,3,192,768]{3,2,1,0:T(8,128)(2,1)} %refs_1_.14, bf16[2,192,768]{2,1,0:T(8,128)(2,1)S(1)} %copy-done.1, ...), custom_call_target="tpu_custom_call" | custom-call | flops 603979776 | bytes 9437184 | tf_op jit(solution)/shard_map/attend_backward_0/pallas_call | solution.py:513
  303.8 8.3 %patch_backward.1 = (bf16[512,768]{1,0:T(8,128)(2,1)}, bf16[2,768,128]{2,1,0:T(8,128)(2,1)S(1)}) custom-call(s32[3]{0:T(128)S(1)} %copy-done.33, bf16[1536,768]{1,0:T(8,128)(2,1)} %refs_1_.15, bf16[1536,768]{1,0:T(8,128)(2,1)} %copy-done.49, bf16[768,768]{1,0:T(8,128)(2,1)} %collective-permute-done.38.refs_3_, ...), custom_call_target="tpu_custom_call" | custom-call | tf_op jit(solution)/shard_map/patch_backward/pallas_call | solution.py:602
  382.3 11.2 %collective-permute-done.86 = bf16[2,2,2,2,96,384]{5,4,3,2,1,0:T(8,128)(2,1)S(1)} collective-permute-done((bf16[2,2,2,2,96,384]{5,4,3,2,1,0:T(8,128)(2,1)S(1)}, bf16[2,2,2,2,96,384]{5,4,3,2,1,0:T(8,128)(2,1)S(1)}, u32[]{:S(2)}, u32[]{:S(2)}) %collective-permute-start.86) | collective-permute-done | bytes 1179680 | tf_op jit(solution)/shard_map/ppermute | solution.py:43
  394.6 24.2 %collective-permute-done.91 = bf16[2,2,2,2,96,384]{5,4,3,2,1,0:T(8,128)(2,1)S(1)} collective-permute-done((bf16[2,2,2,2,96,384]{5,4,3,2,1,0:T(8,128)(2,1)S(1)}, bf16[2,2,2,2,96,384]{5,4,3,2,1,0:T(8,128)(2,1)S(1)}, u32[]{:S(2)}, u32[]{:S(2)}) %collective-permute-start.91) | collective-permute-done | bytes 1179680 | tf_op jit(solution)/shard_map/ppermute | solution.py:43
  427.0 17.0 %collective-permute-done.62 = bf16[2,2,2,2,96,384]{5,4,3,2,1,0:T(8,128)(2,1)S(1)} collective-permute-done((bf16[2,2,2,2,96,384]{5,4,3,2,1,0:T(8,128)(2,1)S(1)}, bf16[2,2,2,2,96,384]{5,4,3,2,1,0:T(8,128)(2,1)S(1)}, u32[]{:S(2)}, u32[]{:S(2)}) %collective-permute-start.62) | collective-permute-done | bytes 1179680 | tf_op jit(solution)/shard_map/ppermute | solution.py:43
  452.5 11.5 %collective-permute-done.87 = bf16[2,2,2,96,384]{4,3,2,1,0:T(8,128)(2,1)S(1)} collective-permute-done((bf16[2,2,2,96,384]{4,3,2,1,0:T(8,128)(2,1)S(1)}, bf16[2,2,2,96,384]{4,3,2,1,0:T(8,128)(2,1)S(1)}, u32[]{:S(2)}, u32[]{:S(2)}) %collective-permute-start.87) | collective-permute-done | bytes 589856 | tf_op jit(solution)/shard_map/ppermute | solution.py:43
  464.8 11.9 %collective-permute-done.92 = bf16[2,2,2,96,384]{4,3,2,1,0:T(8,128)(2,1)S(1)} collective-permute-done((bf16[2,2,2,96,384]{4,3,2,1,0:T(8,128)(2,1)S(1)}, bf16[2,2,2,96,384]{4,3,2,1,0:T(8,128)(2,1)S(1)}, u32[]{:S(2)}, u32[]{:S(2)}) %collective-permute-start.92) | collective-permute-done | bytes 589856 | tf_op jit(solution)/shard_map/ppermute | solution.py:43
  495.8 8.1 %collective-permute-done.76 = bf16[2,192,384]{2,1,0:T(8,128)(2,1)S(1)} collective-permute-done((bf16[2,192,384]{2,1,0:T(8,128)(2,1)S(1)}, bf16[2,192,384]{2,1,0:T(8,128)(2,1)S(1)}, u32[]{:S(2)}, u32[]{:S(2)}) %collective-permute-start.76) | collective-permute-done | bytes 294944 | tf_op jit(solution)/shard_map/ppermute | solution.py:43
  505.5 8.0 %collective-permute-done.82 = bf16[2,192,384]{2,1,0:T(8,128)(2,1)S(1)} collective-permute-done((bf16[2,192,384]{2,1,0:T(8,128)(2,1)S(1)}, bf16[2,192,384]{2,1,0:T(8,128)(2,1)S(1)}, u32[]{:S(2)}, u32[]{:S(2)}) %collective-permute-start.82) | collective-permute-done | bytes 294944 | tf_op jit(solution)/shard_map/ppermute | solution.py:43
  528.5 8.7 %collective-permute-done.77 = bf16[192,384]{1,0:T(8,128)(2,1)S(1)} collective-permute-done((bf16[192,384]{1,0:T(8,128)(2,1)S(1)}, bf16[192,384]{1,0:T(8,128)(2,1)S(1)}, u32[]{:S(2)}, u32[]{:S(2)}) %collective-permute-start.77) | collective-permute-done | bytes 147488 | tf_op jit(solution)/shard_map/ppermute | solution.py:43
  (477 shorter events, 237.6 us)
Async XLA Ops:
  19.2 43.9 %collective-permute-start.11 = (bf16[2,192,768]{2,1,0:T(8,128)(2,1)S(1)}, bf16[2,192,768]{2,1,0:T(8,128)(2,1)}, u32[]{:S(2)}, u32[]{:S(2)}) collective-permute-start(bf16[2,192,768]{2,1,0:T(8,128)(2,1)S(1)} %copy-done.1), channel_id=1, source_target_pairs={{0,8},{8,0},{16,24},{24,16},{1,9},{9,1},{17,25},{25,17},{2,10},{10... | collective-permute-start | bytes 1769480 | tf_op jit(solution)/shard_map/ppermute | solution.py:43
  61.4 39.6 %collective-permute-start.1 = (bf16[96,3072]{1,0:T(8,128)(2,1)S(1)}, bf16[96,3072]{1,0:T(8,128)(2,1)}, u32[]{:S(2)}, u32[]{:S(2)}) collective-permute-start(bf16[96,3072]{1,0:T(8,128)(2,1)S(1)} %copy-done.53), channel_id=1, source_target_pairs={{0,16},{8,24},{16,0},{24,8},{1,17},{9,25},{17,1},{25,9},{2,18},{10... | collective-permute-start | bytes 1769480 | tf_op jit(solution)/shard_map/ppermute | solution.py:43
  63.2 47.9 %collective-permute-start.6 = (bf16[384,768]{1,0:T(8,128)(2,1)S(1)}, bf16[384,768]{1,0:T(8,128)(2,1)}, u32[]{:S(2)}, u32[]{:S(2)}) collective-permute-start(bf16[384,768]{1,0:T(8,128)(2,1)S(1)} %dynamic-slice_bitcast_fusion.16), channel_id=1, source_target_pairs={{0,16},{8,24},{16,0},{24,8},{1,17},{9,25},{17,1},{25,9},{2,18},{10... | collective-permute-start | bytes 1769480 | tf_op jit(solution)/shard_map/ppermute | solution.py:43
  63.6 48.2 %collective-permute-start.25 = (bf16[4,96,768]{2,1,0:T(8,128)(2,1)S(1)}, bf16[4,96,768]{2,1,0:T(8,128)(2,1)}, u32[]{:S(2)}, u32[]{:S(2)}) collective-permute-start(bf16[4,96,768]{2,1,0:T(8,128)(2,1)S(1)} %collective-permute-done.24.refs_5_), channel_id=1, source_target_pairs={{0,1},{1,0},{2,3},{3,2},{4,5},{5,4},{6,7},{7,6},{8,9},{9,8},{10,11... | collective-permute-start | bytes 1769480 | tf_op jit(solution)/shard_map/ppermute | solution.py:43
  113.2 50.5 %collective-permute-start.10 = (bf16[2,3,192,768]{3,2,1,0:T(8,128)(2,1)}, bf16[2,3,192,768]{3,2,1,0:T(8,128)(2,1)}, u32[]{:S(2)}, u32[]{:S(2)}) collective-permute-start(bf16[2,3,192,768]{3,2,1,0:T(8,128)(2,1)} %refs_1_.14), channel_id=1, source_target_pairs={{0,8},{8,0},{16,24},{24,16},{1,9},{9,1},{17,25},{25,17},{2,10},{10... | collective-permute-start | bytes 5308424 | tf_op jit(solution)/shard_map/ppermute | solution.py:43
  127.3 40.6 %collective-permute-start = (bf16[2,192,3072]{2,1,0:T(8,128)(2,1)}, bf16[2,192,3072]{2,1,0:T(8,128)(2,1)}, u32[]{:S(2)}, u32[]{:S(2)}) collective-permute-start(bf16[2,192,3072]{2,1,0:T(8,128)(2,1)} %refs_1_.13), channel_id=1, source_target_pairs={{0,8},{8,0},{16,24},{24,16},{1,9},{9,1},{17,25},{25,17},{2,10},{10... | collective-permute-start | bytes 7077896 | tf_op jit(solution)/shard_map/ppermute | solution.py:43
  127.4 41.0 %collective-permute-start.5 = (bf16[2,768,768]{2,1,0:T(8,128)(2,1)}, bf16[2,768,768]{2,1,0:T(8,128)(2,1)}, u32[]{:S(2)}, u32[]{:S(2)}) collective-permute-start(bf16[2,768,768]{2,1,0:T(8,128)(2,1)} %refs_7_.5), channel_id=1, source_target_pairs={{0,8},{8,0},{16,24},{24,16},{1,9},{9,1},{17,25},{25,17},{2,10},{10... | collective-permute-start | bytes 7077896 | tf_op jit(solution)/shard_map/ppermute | solution.py:43
  163.7 38.8 %collective-permute-start.38 = (bf16[768,768]{1,0:T(8,128)(2,1)}, bf16[768,768]{1,0:T(8,128)(2,1)}, u32[]{:S(2)}, u32[]{:S(2)}) collective-permute-start(bf16[768,768]{1,0:T(8,128)(2,1)} %constant_dynamic-slice_fusion.12), channel_id=1, source_target_pairs={{0,16},{8,24},{16,0},{24,8},{1,17},{9,25},{17,1},{25,9},{2,18},{10... | collective-permute-start | bytes 3538952 | tf_op jit(solution)/shard_map/ppermute | solution.py:43
  202.1 100.2 %collective-permute-start.37 = (bf16[1536,768]{1,0:T(8,128)(2,1)S(1)}, bf16[1536,768]{1,0:T(8,128)(2,1)S(1)}, u32[]{:S(2)}, u32[]{:S(2)}) collective-permute-start(bf16[1536,768]{1,0:T(8,128)(2,1)S(1)} %copy-done), channel_id=1, source_target_pairs={{0,8},{8,0},{16,24},{24,16},{1,9},{9,1},{17,25},{25,17},{2,10},{10... | collective-permute-start | bytes 7077896 | tf_op jit(solution)/shard_map/ppermute | solution.py:43
  202.5 67.9 %collective-permute-start.39 = (bf16[768,768]{1,0:T(8,128)(2,1)}, bf16[768,768]{1,0:T(8,128)(2,1)}, u32[]{:S(2)}, u32[]{:S(2)}) collective-permute-start(bf16[768,768]{1,0:T(8,128)(2,1)} %collective-permute-done.38.refs_3_), channel_id=1, source_target_pairs={{0,1},{1,0},{2,3},{3,2},{4,5},{5,4},{6,7},{7,6},{8,9},{9,8},{10,11... | collective-permute-start | bytes 3538952 | tf_op jit(solution)/shard_map/ppermute | solution.py:43
  202.8 99.2 %collective-permute-start.40 = (bf16[768,768]{1,0:T(8,128)(2,1)}, bf16[768,768]{1,0:T(8,128)(2,1)}, u32[]{:S(2)}, u32[]{:S(2)}) collective-permute-start(bf16[768,768]{1,0:T(8,128)(2,1)} %collective-permute-done.38.refs_3_), channel_id=1, source_target_pairs={{0,8},{8,0},{16,24},{24,16},{1,9},{9,1},{17,25},{25,17},{2,10},{10... | collective-permute-start | bytes 3538952 | tf_op jit(solution)/shard_map/ppermute | solution.py:43
  269.9 90.7 %collective-permute-start.85 = (bf16[2,2,2,2,2,96,384]{6,5,4,3,2,1,0:T(8,128)(2,1)}, bf16[2,2,2,2,2,96,384]{6,5,4,3,2,1,0:T(8,128)(2,1)}, u32[]{:S(2)}, u32[]{:S(2)}) collective-permute-start(bf16[2,2,2,2,2,96,384]{6,5,4,3,2,1,0:T(8,128)(2,1)} %dynamic-slice_bitcast_fusion.1), channel_id=1, source_target_pairs={{0,8},{8,0},{16,24},{24,16},{1,9},{9,1},{17,25},{25,17},{2,10},{10... | collective-permute-start | bytes 7077896 | tf_op jit(solution)/shard_map/ppermute | solution.py:43
  301.7 62.9 %collective-permute-start.90 = (bf16[2,2,2,2,2,96,384]{6,5,4,3,2,1,0:T(8,128)(2,1)}, bf16[2,2,2,2,2,96,384]{6,5,4,3,2,1,0:T(8,128)(2,1)}, u32[]{:S(2)}, u32[]{:S(2)}) collective-permute-start(bf16[2,2,2,2,2,96,384]{6,5,4,3,2,1,0:T(8,128)(2,1)} %dynamic-slice_bitcast_fusion), channel_id=1, source_target_pairs={{0,8},{8,0},{16,24},{24,16},{1,9},{9,1},{17,25},{25,17},{2,10},{10... | collective-permute-start | bytes 7077896 | tf_op jit(solution)/shard_map/ppermute | solution.py:43
  302.0 65.8 %collective-permute-start.73 = (bf16[2,2,2,2,192,384]{5,4,3,2,1,0:T(8,128)(2,1)}, bf16[2,2,2,2,192,384]{5,4,3,2,1,0:T(8,128)(2,1)}, u32[]{:S(2)}, u32[]{:S(2)}) collective-permute-start(bf16[2,2,2,2,192,384]{5,4,3,2,1,0:T(8,128)(2,1)} %dynamic-slice_bitcast_fusion.3), channel_id=1, source_target_pairs={{0,8},{8,0},{16,24},{24,16},{1,9},{9,1},{17,25},{25,17},{2,10},{10... | collective-permute-start | bytes 7077896 | tf_op jit(solution)/shard_map/ppermute | solution.py:43
  335.3 36.6 %collective-permute-start.79 = (bf16[2,2,2,2,192,384]{5,4,3,2,1,0:T(8,128)(2,1)}, bf16[2,2,2,2,192,384]{5,4,3,2,1,0:T(8,128)(2,1)}, u32[]{:S(2)}, u32[]{:S(2)}) collective-permute-start(bf16[2,2,2,2,192,384]{5,4,3,2,1,0:T(8,128)(2,1)} %get-tuple-element.153), channel_id=1, source_target_pairs={{0,8},{8,0},{16,24},{24,16},{1,9},{9,1},{17,25},{25,17},{2,10},{10... | collective-permute-start | bytes 7077896 | tf_op jit(solution)/shard_map/ppermute | solution.py:43
  367.8 51.0 %collective-permute-start.91 = (bf16[2,2,2,2,96,384]{5,4,3,2,1,0:T(8,128)(2,1)S(1)}, bf16[2,2,2,2,96,384]{5,4,3,2,1,0:T(8,128)(2,1)S(1)}, u32[]{:S(2)}, u32[]{:S(2)}) collective-permute-start(bf16[2,2,2,2,96,384]{5,4,3,2,1,0:T(8,128)(2,1)S(1)} %dynamic-slice_bitcast_fusion.6), channel_id=1, source_target_pairs={{0,1},{1,0},{2,3},{3,2},{4,5},{5,4},{6,7},{7,6},{8,9},{9,8},{10,11... | collective-permute-start | bytes 3538952 | tf_op jit(solution)/shard_map/ppermute | solution.py:43
  371.9 48.0 %collective-permute-start.74 = (bf16[2,2,2,192,384]{4,3,2,1,0:T(8,128)(2,1)S(1)}, bf16[2,2,2,192,384]{4,3,2,1,0:T(8,128)(2,1)S(1)}, u32[]{:S(2)}, u32[]{:S(2)}) collective-permute-start(bf16[2,2,2,192,384]{4,3,2,1,0:T(8,128)(2,1)S(1)} %dynamic-slice_bitcast_fusion.8), channel_id=1, source_target_pairs={{0,16},{8,24},{16,0},{24,8},{1,17},{9,25},{17,1},{25,9},{2,18},{10... | collective-permute-start | bytes 3538952 | tf_op jit(solution)/shard_map/ppermute | solution.py:43
  375.9 50.2 %collective-permute-start.80 = (bf16[2,2,2,192,384]{4,3,2,1,0:T(8,128)(2,1)S(1)}, bf16[2,2,2,192,384]{4,3,2,1,0:T(8,128)(2,1)S(1)}, u32[]{:S(2)}, u32[]{:S(2)}) collective-permute-start(bf16[2,2,2,192,384]{4,3,2,1,0:T(8,128)(2,1)S(1)} %copy_bitcast_fusion.3), channel_id=1, source_target_pairs={{0,16},{8,24},{16,0},{24,8},{1,17},{9,25},{17,1},{25,9},{2,18},{10... | collective-permute-start | bytes 3538952 | tf_op jit(solution)/shard_map/ppermute | solution.py:43
  379.9 64.1 %collective-permute-start.62 = (bf16[2,2,2,2,96,384]{5,4,3,2,1,0:T(8,128)(2,1)S(1)}, bf16[2,2,2,2,96,384]{5,4,3,2,1,0:T(8,128)(2,1)S(1)}, u32[]{:S(2)}, u32[]{:S(2)}) collective-permute-start(bf16[2,2,2,2,96,384]{5,4,3,2,1,0:T(8,128)(2,1)S(1)} %dynamic-slice_bitcast_fusion.9), channel_id=1, source_target_pairs={{0,1},{1,0},{2,3},{3,2},{4,5},{5,4},{6,7},{7,6},{8,9},{9,8},{10,11... | collective-permute-start | bytes 3538952 | tf_op jit(solution)/shard_map/ppermute | solution.py:43
  393.5 57.9 %collective-permute-start.68 = (bf16[2,2,2,2,96,384]{5,4,3,2,1,0:T(8,128)(2,1)S(1)}, bf16[2,2,2,2,96,384]{5,4,3,2,1,0:T(8,128)(2,1)S(1)}, u32[]{:S(2)}, u32[]{:S(2)}) collective-permute-start(bf16[2,2,2,2,96,384]{5,4,3,2,1,0:T(8,128)(2,1)S(1)} %copy_bitcast_fusion.4), channel_id=1, source_target_pairs={{0,16},{8,24},{16,0},{24,8},{1,17},{9,25},{17,1},{25,9},{2,18},{10... | collective-permute-start | bytes 3538952 | tf_op jit(solution)/shard_map/ppermute | solution.py:43
  418.8 45.2 %collective-permute-start.87 = (bf16[2,2,2,96,384]{4,3,2,1,0:T(8,128)(2,1)S(1)}, bf16[2,2,2,96,384]{4,3,2,1,0:T(8,128)(2,1)S(1)}, u32[]{:S(2)}, u32[]{:S(2)}) collective-permute-start(bf16[2,2,2,96,384]{4,3,2,1,0:T(8,128)(2,1)S(1)} %dynamic-slice_bitcast_fusion.11), channel_id=1, source_target_pairs={{0,16},{8,24},{16,0},{24,8},{1,17},{9,25},{17,1},{25,9},{2,18},{10... | collective-permute-start | bytes 1769480 | tf_op jit(solution)/shard_map/ppermute | solution.py:43
  419.9 56.7 %collective-permute-start.92 = (bf16[2,2,2,96,384]{4,3,2,1,0:T(8,128)(2,1)S(1)}, bf16[2,2,2,96,384]{4,3,2,1,0:T(8,128)(2,1)S(1)}, u32[]{:S(2)}, u32[]{:S(2)}) collective-permute-start(bf16[2,2,2,96,384]{4,3,2,1,0:T(8,128)(2,1)S(1)} %dynamic-slice_bitcast_fusion.10), channel_id=1, source_target_pairs={{0,16},{8,24},{16,0},{24,8},{1,17},{9,25},{17,1},{25,9},{2,18},{10... | collective-permute-start | bytes 1769480 | tf_op jit(solution)/shard_map/ppermute | solution.py:43
  426.1 52.7 %collective-permute-start.75 = (bf16[2,2,192,384]{3,2,1,0:T(8,128)(2,1)S(1)}, bf16[2,2,192,384]{3,2,1,0:T(8,128)(2,1)S(1)}, u32[]{:S(2)}, u32[]{:S(2)}) collective-permute-start(bf16[2,2,192,384]{3,2,1,0:T(8,128)(2,1)S(1)} %dynamic-slice_bitcast_fusion.12), channel_id=1, source_target_pairs={{0,1},{1,0},{2,3},{3,2},{4,5},{5,4},{6,7},{7,6},{8,9},{9,8},{10,11... | collective-permute-start | bytes 1769480 | tf_op jit(solution)/shard_map/ppermute | solution.py:43
  451.4 36.5 %collective-permute-start.63 = (bf16[2,2,2,96,384]{4,3,2,1,0:T(8,128)(2,1)S(1)}, bf16[2,2,2,96,384]{4,3,2,1,0:T(8,128)(2,1)S(1)}, u32[]{:S(2)}, u32[]{:S(2)}) collective-permute-start(bf16[2,2,2,96,384]{4,3,2,1,0:T(8,128)(2,1)S(1)} %dynamic-slice_bitcast_fusion.13), channel_id=1, source_target_pairs={{0,16},{8,24},{16,0},{24,8},{1,17},{9,25},{17,1},{25,9},{2,18},{10... | collective-permute-start | bytes 1769480 | tf_op jit(solution)/shard_map/ppermute | solution.py:43
  (145 other events, 2679.0 us)

commit v3 on v2

--- a/solution.py
+++ b/solution.py
@@ -18,6 +18,11 @@
 GELU_A = 0.7978845608028654
 GELU_B = 0.044715
 
+
+def hint(microseconds):
+    return pl.CostEstimate(flops=1, bytes_accessed=int(microseconds * 3.69e6), transcendentals=0)
+
+
 ANY = pl.BlockSpec(memory_space=pl.ANY)
 VMEM = pl.BlockSpec(memory_space=pltpu.VMEM)
 SMEM = pl.BlockSpec(memory_space=pltpu.SMEM)
@@ -51,18 +56,25 @@
     return lax.dynamic_index_in_dim(value, index, axis, keepdims=False)
 
 
-def far_pieces(half):
+def after(value, *others):
+    return lax.optimization_barrier((value,) + others)[0]
+
+
+def over_chips(half):
     found = {0: half}
-    pieces = {}
     for bit in reversed(range(1, bits_of(lax.axis_size("grp")))):
         for rel in list(found):
-            first = swap(found[rel], "grp", 1 << bit)
-            second = swap(first, "wide", 1)
-            found[rel ^ (1 << bit)] = first
-            pieces[rel ^ (1 << bit)] = (first, second)
+            found[rel ^ (1 << bit)] = swap(found[rel], "grp", 1 << bit)
+    return [found[rel] for rel in sorted(found) if rel]
+
+
+def over_sides(firsts):
+    return [swap(first, "wide", 1) for first in firsts]
+
+
+def over_cores(firsts, seconds):
     flat = []
-    for rel in sorted(pieces):
-        first, second = pieces[rel]
+    for first, second in zip(firsts, seconds):
         flat += [first, second, swap(first, "grp", 1), swap(second, "grp", 1)]
     return flat
 
@@ -184,8 +196,8 @@
     weight_refs = refs[1 : 1 + count]
     at = 1 + count
     if summed:
-        hidden_refs = refs[at : at + 2 * chips + 1]
-        at += 2 * chips + 1
+        hidden_refs = refs[at : at + 3]
+        at += 3
     else:
         hidden_refs = refs[at : at + 1]
         at += 1
@@ -244,9 +256,7 @@
         out_specs=[VMEM] * len(outs),
         scratch_shapes=[pltpu.VMEM((4, width, width), BF), pltpu.SemaphoreType.DMA((count,))],
         compiler_params=pltpu.CompilerParams(vmem_limit_bytes=52 << 20),
-        cost_estimate=pl.CostEstimate(
-            flops=8 * rows * width * width, bytes_accessed=8 * width * width + 20 * rows * width, transcendentals=0
-        ),
+        cost_estimate=hint(5 if summed else 11),
         name=f"attend_forward_{block}",
     )(place, *weight_pieces, *hidden, gains, biases)
 
@@ -305,24 +315,30 @@
             pltpu.SemaphoreType.DMA((count * pieces + count,)),
         ],
         compiler_params=pltpu.CompilerParams(vmem_limit_bytes=52 << 20),
-        cost_estimate=pl.CostEstimate(
-            flops=4 * rows * width * hidden_width, bytes_accessed=4 * width * hidden_width, transcendentals=0
-        ),
+        cost_estimate=hint(8),
         name=f"feed_forward_{block}",
     )(place, *up_pieces, *down_pieces, middle, embedded, gains, biases, up_bias, down_bias)
 
 
-def feed_backward_kernel(block, chips, local, *refs):
+def send_out(terms, outs, sem, base):
+    return start_all([(term.at[half], out) for term, pair in zip(terms, outs) for half, out in enumerate(pair)], sem, base)
+
+
+def feed_backward_kernel(block, chips, wides, local, *refs):
     place = refs[0]
     count = 2 + far_count(chips)
     up_refs = refs[1 : 1 + count]
     down_refs = refs[1 + count : 1 + 2 * count]
     middle_ref, grad_ref, gain_ref, bias_ref, up_bias_ref, down_bias_ref = refs[1 + 2 * count : 7 + 2 * count]
-    outs = refs[7 + 2 * count : -7]
-    up, down, normed_ref, grad_low, grad_turned, total, sem = refs[-7:]
-    up_term, down_term, middle_grad_ref, vector_ref = outs[:4]
+    outs = refs[7 + 2 * count : -8]
+    term, up, down, normed_ref, grad_low, grad_turned, total, sem = refs[-8:]
+    middle_grad_ref, vector_ref = outs[4:6]
     pieces, width, _ = up.shape
-    lanes = up_term.shape[2]
+    lanes = term.shape[4]
+    mine = place[0] & 1
+    wide_rows = pieces * width // wides
+    half = wide_rows // 2
+    columns_wide = width // wides
     up_copies = start_all(wide_copies(place, block, chips, up_refs, up), sem)
     down_copies = start_all(tall_copies(place, block, chips, down_refs, down), sem, count * pieces)
     middle = middle_ref[...]
@@ -342,7 +358,7 @@
     vector_ref[pieces + 2 : pieces + 3, :] = column_sum(low_grad.astype(F32))
     wait_all(up_copies)
     wait_all(down_copies)
-    out_total = refs[-8] if local else None
+    out_total = refs[-9] if local else None
     if local:
         out_total[...] = middle + down_bias_ref[block : block + 1, :]
 
@@ -359,14 +375,28 @@
         vector_ref[pl.ds(at, 1), :] = column_sum(grad_upper.astype(F32))
         down_part = dot_nn(grad_turned[...], active).astype(BF)
         for part in range(width // lanes):
-            down_term[at * (width // lanes) + part] = down_part[:, part * lanes : (part + 1) * lanes]
+            spot = at * (width // lanes) + part
+            chip, spot = spot // pieces, spot % pieces
+            core, spot = spot // (pieces // 2), spot % (pieces // 2)
+            for to in range(wides):
+                base = pl.multiple_of(to * half + spot * columns_wide, columns_wide)
+                term[core ^ mine, 1, chip, pl.ds(base, columns_wide), :] = down_part[
+                    to * columns_wide : (to + 1) * columns_wide, part * lanes : (part + 1) * lanes
+                ]
         up_part = dot_tn(grad_upper, normed).astype(BF)
-        for part in range(width // lanes):
-            up_term[part, columns, :] = up_part[:, part * lanes : (part + 1) * lanes]
+        for to in range(width // wide_rows):
+            base = pl.multiple_of((at * (width // wide_rows) + to) * half, half)
+            for core in (0, 1):
+                rows_at = to * wide_rows + core * half
+                for part in range(chips):
+                    term[core ^ mine, 0, part, pl.ds(base, half), :] = up_part[
+                        rows_at : rows_at + half, part * lanes : (part + 1) * lanes
+                    ]
         total[...] += dot_nt(grad_upper, up[at])
         return carry
 
     lax.fori_loop(0, pieces, one_piece, 0)
+    sent = send_out((term.at[:, 0], term.at[:, 1]), (outs[0:2], outs[2:4]), sem, count * pieces + count)
     unit, scale = normalize(middle_ref[...])
     grad = total[...]
     vector_ref[pieces : pieces + 1, :] = column_sum(grad * unit)
@@ -374,20 +404,20 @@
     back = normalize_back(grad, unit, scale, gain_ref[block, 1:2, :])
     if local:
         middle_grad_ref[...] = grad_low[...].astype(F32) + back
-        outs[4][...] = (out_total[...].astype(BF).astype(F32) * keep).astype(BF)
+        outs[6][...] = (out_total[...].astype(BF).astype(F32) * keep).astype(BF)
     else:
         middle_grad_ref[...] = grad_ref[...] + back
-
-
-def feed_backward(block, chips, local, place, up_pieces, down_pieces, middle, grad, gains, biases, up_bias, down_bias):
+    wait_all(sent)
+
+
+def feed_backward(block, chips, wides, local, place, up_pieces, down_pieces, middle, grad, gains, biases, up_bias, down_bias):
     rows, width = middle.shape
     hidden_width = up_bias.shape[1]
     pieces = hidden_width // width
     lanes = width // chips
     count = 2 + far_count(chips)
     outs = [
-        jax.ShapeDtypeStruct((chips, hidden_width, lanes), BF),
-        jax.ShapeDtypeStruct((hidden_width // lanes, width, lanes), BF),
+        *[jax.ShapeDtypeStruct((chips, hidden_width // 2, lanes), BF)] * 4,
         jax.ShapeDtypeStruct((rows, width), F32),
         jax.ShapeDtypeStruct((8, width), F32),
     ]
@@ -396,55 +426,55 @@
         outs.append(jax.ShapeDtypeStruct((rows, width), BF))
         scratch.append(pltpu.VMEM((rows, width), F32))
     scratch += [
+        pltpu.VMEM((2, 2, chips, hidden_width // 2, lanes), BF),
         pltpu.VMEM((pieces, width, width), BF),
         pltpu.VMEM((hidden_width, width), BF),
         pltpu.VMEM((rows, width), BF),
         pltpu.VMEM((rows, width), BF),
         pltpu.VMEM((width, rows), BF),
         pltpu.VMEM((rows, width), F32),
-        pltpu.SemaphoreType.DMA((count * pieces + count,)),
+        pltpu.SemaphoreType.DMA((count * pieces + count + 4,)),
     ]
-    kernel = feed_backward_local if local else feed_backward_global
     return pl.pallas_call(
-        functools.partial(kernel, block, chips),
+        functools.partial(feed_backward_kernel, block, chips, wides, local),
         out_shape=outs,
         in_specs=[SMEM] + [ANY] * (2 * count) + [VMEM] * 6,
-        out_specs=[VMEM] * len(outs),
+        out_specs=[ANY] * 4 + [VMEM] * (len(outs) - 4),
         scratch_shapes=scratch,
         compiler_params=pltpu.CompilerParams(vmem_limit_bytes=56 << 20),
-        cost_estimate=pl.CostEstimate(
-            flops=12 * rows * width * hidden_width, bytes_accessed=8 * width * hidden_width, transcendentals=0
-        ),
+        cost_estimate=hint(26 if local else 15),
         name=f"feed_backward_{block}",
     )(place, *up_pieces, *down_pieces, middle, grad, gains, biases, up_bias, down_bias)
 
 
-def feed_backward_local(block, chips, *refs):
-    return feed_backward_kernel(block, chips, True, *refs)
-
-
-def feed_backward_global(block, chips, *refs):
-    return feed_backward_kernel(block, chips, False, *refs)
-
-
-def attend_backward_kernel(block, chips, span, local, *refs):
+def attend_backward_kernel(block, chips, wides, span, local, *refs):
     place = refs[0]
     count = 4 + far_count(chips)
     weight_refs = refs[1 : 1 + count]
-    hidden_ref, grad_ref, qkv_ref, mixed_ref, gain_ref, bias_ref = refs[1 + count : 7 + count]
-    outs = refs[7 + count : -4]
-    weights, mixed_grad, grads, sem = refs[-4:]
-    term_ref, vector_ref, low_ref, extra_ref = outs
+    hidden_ref, grad_ref, qkv_ref, mixed_ref, gain_ref, bias_ref, ids_ref = refs[1 + count : 8 + count]
+    outs = refs[8 + count : -5]
+    term, weights, mixed_grad, grads, sem = refs[-5:]
+    keep_ref, send_ref, vector_ref, low_ref, extra_ref = outs
+    mine = place[0] & 1
     copies = start_all(attend_copies(place, block, chips, weight_refs, weights), sem)
     hidden = hidden_ref[...].astype(F32)
     total, width = hidden.shape
-    lanes_out = term_ref.shape[3]
+    lanes_out = term.shape[3]
+    columns = width // wides
+
+    def put(which, value):
+        core, slot = which // 2, which % 2
+        for part in range(chips):
+            for to in range(wides):
+                base = (2 * to + slot) * columns
+                term[core ^ mine, part, base : base + columns, :] = value[
+                    to * columns : (to + 1) * columns, part * lanes_out : (part + 1) * lanes_out
+                ]
+
     unit, scale = normalize(hidden)
     normed = (unit * gain_ref[block, 0:1, :] + bias_ref[block, 0:1, :]).astype(BF)
     branch = grad_ref[...].astype(BF)
-    out_term = dot_tn(branch, mixed_ref[...]).astype(BF)
-    for part in range(chips):
-        term_ref[part, 3] = out_term[:, part * lanes_out : (part + 1) * lanes_out]
+    put(3, dot_tn(branch, mixed_ref[...]).astype(BF))
     wait_all(copies)
     mixed_grad[...] = dot_nt(branch, weights[3]).astype(BF)
     rows = min(total, CHUNK)
@@ -475,10 +505,9 @@
     grad = jnp.zeros((total, width), F32)
     for which in range(3):
         entry = grads[which]
-        part_term = dot_tn(entry, normed).astype(BF)
-        for part in range(chips):
-            term_ref[part, which] = part_term[:, part * lanes_out : (part + 1) * lanes_out]
+        put(which, dot_tn(entry, normed).astype(BF))
         grad = grad + dot_nt(entry, weights[which])
+    sent = send_out((term,), ((keep_ref, send_ref),), sem, count)
     vector_ref[...] = jnp.zeros_like(vector_ref)
     vector_ref[0:1, :] = column_sum(grad * unit)
     vector_ref[1:2, :] = column_sum(grad)
@@ -490,84 +519,93 @@
         extra_ref[...] = jnp.sum(rounded.reshape(total // PATCH, PATCH, width), axis=1)
     else:
         vector_ref[2:3, :] = column_sum(rounded)
-        wides = extra_ref.shape[0]
-        columns = width // wides
         for at in range(wides):
             block_out = rounded[:, at * columns : (at + 1) * columns]
             if extra_ref.shape[2] > columns:
                 block_out = jnp.pad(block_out, ((0, 0), (0, extra_ref.shape[2] - columns)))
-            extra_ref[at] = block_out.astype(BF)
-
-
-def attend_backward(block, chips, wides, span, local, place, weight_pieces, hidden, grad, qkv, mixed, gains, biases):
+            extra_ref[at, :total, :] = block_out.astype(BF)
+            extra_ref[at, total:, :] = ids_ref[...]
+    wait_all(sent)
+
+
+def attend_backward(block, chips, wides, span, local, place, weight_pieces, hidden, grad, qkv, mixed, gains, biases, ids):
     rows, width = hidden.shape
     lanes = width // chips
     padded = -(-(width // wides) // 128) * 128
     outs = [
-        jax.ShapeDtypeStruct((chips, 4, width, lanes), BF),
+        jax.ShapeDtypeStruct((chips, 2 * width, lanes), BF),
+        jax.ShapeDtypeStruct((chips, 2 * width, lanes), BF),
         jax.ShapeDtypeStruct((8, width), F32),
         jax.ShapeDtypeStruct((rows, width), BF),
-        jax.ShapeDtypeStruct((rows // PATCH, width), F32) if local else jax.ShapeDtypeStruct((wides, rows, padded), BF),
+        jax.ShapeDtypeStruct((rows // PATCH, width), F32) if local else jax.ShapeDtypeStruct((wides, rows + 16, padded), BF),
     ]
     count = 4 + far_count(chips)
     return pl.pallas_call(
-        functools.partial(attend_backward_kernel, block, chips, span, local),
+        functools.partial(attend_backward_kernel, block, chips, wides, span, local),
         out_shape=outs,
-        in_specs=[SMEM] + [ANY] * count + [VMEM] * 6,
-        out_specs=[VMEM] * 4,
+        in_specs=[SMEM] + [ANY] * count + [VMEM] * 7,
+        out_specs=[ANY] * 2 + [VMEM] * 3,
         scratch_shapes=[
+            pltpu.VMEM((2, chips, 2 * width, lanes), BF),
             pltpu.VMEM((4, width, width), BF),
             pltpu.VMEM((rows, width), BF),
             pltpu.VMEM((3, rows, width), BF),
-            pltpu.SemaphoreType.DMA((count,)),
+            pltpu.SemaphoreType.DMA((count + 2,)),
         ],
         compiler_params=pltpu.CompilerParams(vmem_limit_bytes=52 << 20),
-        cost_estimate=pl.CostEstimate(
-            flops=16 * rows * width * width, bytes_accessed=16 * width * width, transcendentals=0
-        ),
+        cost_estimate=hint(22 if local else 10),
         name=f"attend_backward_{block}",
-    )(place, *weight_pieces, hidden, grad, qkv, mixed, gains, biases)
+    )(place, *weight_pieces, hidden, grad, qkv, mixed, gains, biases, ids)
 
 
 def embed_kernel(spots, groups, *refs):
-    ids_ref, spot_ids_ref = refs[:2]
-    table_refs = refs[2 : 2 + groups]
-    weight_ref, embedded_ref, own_ref, part_ref = refs[2 + groups :]
-    table = jnp.concatenate([ref[...] for ref in table_refs], axis=0)
-    vocab, width = table.shape
-
-    def hot(ids):
-        at = lax.broadcasted_iota(jnp.int32, (vocab, ids.shape[1]), 0)
-        return (at == ids).astype(F32).astype(BF)
-
-    total = None
-    for spot in range(spots):
-        rows = dot_tn(hot(spot_ids_ref[spot : spot + 1, :]), table).astype(BF)
-        term = dot_nn(rows, weight_ref[spot * width : (spot + 1) * width, :])
-        total = term if total is None else total + term
-    patches = own_ref.shape[0]
-    own_ref[...] = total[:patches]
-    for rel in range(1, groups):
-        part_ref[rel - 1] = total[rel * patches : (rel + 1) * patches].astype(BF)
-    embedded_ref[...] = dot_tn(hot(ids_ref[...]), table).astype(BF)
-
-
-def embed(ids, spot_ids, tables, patch_weight, patches):
+    place = refs[0]
+    table_refs = refs[1 : 1 + groups]
+    weight_ref, embedded_ref, part_ref, rows_ref = refs[1 + groups :]
+    me = place[0]
+    count, width = embedded_ref.shape
+    vocab_rows = table_refs[0].shape[0] - 16
+    vocab = vocab_rows * groups
+    patches = part_ref.shape[1]
+    table = jnp.concatenate([ref[:vocab_rows, :] for ref in table_refs], axis=0)
+    tiles = width // 128
+    at = lax.broadcasted_iota(jnp.int32, (vocab, count), 0)
+    for rel in range(groups):
+        ids = table_refs[rel][vocab_rows:, :count].astype(F32).astype(jnp.int32)[0:1, :]
+        ids = jnp.where(ids < 0, -1, ids ^ (me * vocab_rows))
+        rows = dot_tn((at == ids).astype(F32).astype(BF), table)
+        if rel == 0:
+            embedded_ref[...] = rows.astype(BF)
+        for tile in range(tiles):
+            rows_ref[tile] = rows[:, tile * 128 : (tile + 1) * 128]
+        total = None
+        for spot in range(spots):
+            first = me * spots + spot
+            taken = [rows_ref[tile, pl.ds(first, patches, stride=PATCH), :] for tile in range(tiles)]
+            taken = jnp.concatenate(taken, axis=1).astype(BF)
+            term = dot_nn(taken, weight_ref[spot * width : (spot + 1) * width, :])
+            total = term if total is None else total + term
+        part_ref[rel] = total
+
+
+def embed(place, tables, patch_weight, count):
     groups = len(tables)
     width = tables[0].shape[1]
-    spots = spot_ids.shape[0]
+    spots = PATCH // groups
+    patches = count // PATCH
     return pl.pallas_call(
         functools.partial(embed_kernel, spots, groups),
         out_shape=[
-            jax.ShapeDtypeStruct((ids.shape[1], width), BF),
-            jax.ShapeDtypeStruct((patches, width), F32),
-            jax.ShapeDtypeStruct((groups - 1, patches, width), BF),
+            jax.ShapeDtypeStruct((count, width), BF),
+            jax.ShapeDtypeStruct((groups, patches, width), F32),
         ],
-        in_specs=[VMEM] * (3 + groups),
-        out_specs=[VMEM] * 3,
+        in_specs=[SMEM] + [VMEM] * (1 + groups),
+        out_specs=[VMEM] * 2,
+        scratch_shapes=[pltpu.VMEM((width // 128, count, 128), F32)],
         compiler_params=pltpu.CompilerParams(vmem_limit_bytes=40 << 20),
+        cost_estimate=hint(4),
         name="embed",
-    )(ids, spot_ids, *tables, patch_weight)
+    )(place, *tables, patch_weight)
 
 
 def patch_backward_kernel(chips, *refs):
@@ -613,49 +651,111 @@
             pltpu.SemaphoreType.DMA((count,)),
         ],
         compiler_params=pltpu.CompilerParams(vmem_limit_bytes=52 << 20),
+        cost_estimate=hint(8),
         name="patch_backward",
     )(place, *pieces, ids, grad_summary, grad_local)
 
 
-def patch_weight_kernel(spots, groups, *refs):
-    ids_ref, grads_ref = refs[:2]
-    table_refs = refs[2 : 2 + groups]
-    out_ref = refs[-1]
-    table = jnp.concatenate([ref[...] for ref in table_refs], axis=0)
+def patch_weight_kernel(spots, patches, *refs):
+    place, grads_ref = refs[:2]
+    table_refs = refs[2:-2]
+    out_ref, counts_ref = refs[-2:]
+    me = place[0]
+    vocab_rows = table_refs[0].shape[0] - 16
+    table = jnp.concatenate([ref[:vocab_rows, :] for ref in table_refs], axis=0)
     vocab, width = table.shape
-    grads = grads_ref[...]
+    padded = grads_ref.shape[2]
+    at = lax.broadcasted_iota(jnp.int32, (vocab, 2 * patches), 0)
+    lane_half = lax.broadcasted_iota(jnp.int32, (vocab, 2 * patches), 1) // patches
+    counts_ref[...] = jnp.zeros_like(counts_ref)
+
+    def one_item(item, carry):
+        grads = grads_ref[item, :patches, :]
+        twice = jnp.concatenate([grads, grads], axis=0)
+        rows = grads_ref[item, patches:, : 2 * patches].astype(F32)
+        which = lax.broadcasted_iota(jnp.int32, rows.shape, 0)
+        for spot in range(spots):
+            number = me * spots + spot
+            ids = jnp.sum(jnp.where(which == number // 2, rows, 0.0), axis=0, keepdims=True).astype(jnp.int32)
+            ids = jnp.where(ids < 0, -1, ids ^ (me * vocab_rows))
+            hot = ((at == ids) & (lane_half == number % 2)).astype(F32).astype(BF)
+            counts_ref[spot] += dot_nn(hot, twice)
+        return carry
+
+    lax.fori_loop(0, grads_ref.shape[0], one_item, 0)
     for spot in range(spots):
-        at = lax.broadcasted_iota(jnp.int32, (vocab, ids_ref.shape[1]), 0)
-        hot = (at == ids_ref[spot : spot + 1, :]).astype(F32).astype(BF)
-        counts = dot_nn(hot, grads).astype(BF)
+        counts = counts_ref[spot].astype(BF)
         out_ref[spot * width : (spot + 1) * width, :] = dot_tn(table, counts)[:, : out_ref.shape[1]]
 
 
-def patch_weight_term(ids, grads, tables, columns):
-    spots = ids.shape[0]
+def patch_weight_term(place, spots, patches, grads, tables, columns):
     width = tables[0].shape[1]
+    vocab = (tables[0].shape[0] - 16) * len(tables)
     return pl.pallas_call(
-        functools.partial(patch_weight_kernel, spots, len(tables)),
+        functools.partial(patch_weight_kernel, spots, patches),
         out_shape=jax.ShapeDtypeStruct((spots * width, columns), F32),
-        in_specs=[VMEM] * (2 + len(tables)),
+        in_specs=[SMEM] + [VMEM] * (1 + len(tables)),
         out_specs=VMEM,
+        scratch_shapes=[pltpu.VMEM((spots, vocab, grads.shape[2]), F32)],
         compiler_params=pltpu.CompilerParams(vmem_limit_bytes=40 << 20),
+        cost_estimate=hint(4),
         name="patch_weight_term",
-    )(ids, grads, *tables)
-
-
-def reduce_steps(terms, core_at, steps):
-    alive = list(range(terms.ndim))
-    acc = terms
-    for number, (axis, bit, dimension) in enumerate([("grp", 0, core_at)] + steps):
-        at = alive.index(dimension)
-        alive.pop(at)
+    )(place, grads, *tables)
+
+
+class Route:
+    def __init__(self, chain, parts, left):
+        self.chain = chain
+        self.parts = parts
+        self.left = left
+
+    def total(self, part):
+        value = part[0].astype(F32)
+        for term in part[1:]:
+            value = value + term.astype(F32)
+        return value
+
+    def start(self, axis, bit):
+        at = self.left.index((axis, bit))
+        self.left = self.left[:at] + self.left[at + 1 :]
         mine = bit_at(axis, bit)
-        got = swap(pick(acc, 1 - mine, at), axis, 1 << bit)
-        acc = pick(acc, mine, at).astype(F32) + got.astype(F32)
-        if number < len(steps):
-            acc = acc.astype(BF)
-    return acc
+        anchor = self.chain.pin(self.parts[0][0])
+        self.parts[0] = [anchor] + self.parts[0][1:]
+        sent = [self.total([pick(term, 1 - mine, at) for term in part]).astype(BF) for part in self.parts]
+        sent = sent[0] if len(sent) == 1 else jnp.concatenate(sent, axis=-2)
+        self.chain.mark(sent)
+        self.got = swap(sent, axis, 1 << bit)
+        self.parts = [[pick(term, mine, at) for term in part] for part in self.parts]
+        return self
+
+    def finish(self):
+        base = 0
+        for part in self.parts:
+            rows = part[0].shape[-2]
+            part.append(self.got[..., base : base + rows, :])
+            base += rows
+        return self
+
+    def then(self, axis, bit):
+        return self.finish().start(axis, bit)
+
+    def join(self, other):
+        return Route(self.chain, self.parts + other.parts, self.left)
+
+    def totals(self):
+        return [self.total(part) for part in self.parts]
+
+
+class Chain:
+    def __init__(self, value):
+        self.last = value
+
+    def pin(self, value):
+        return after(value, self.last)
+
+    def mark(self, value):
+        self.last = value
+        return value
 
 
 def body(
@@ -698,114 +798,204 @@
 
     valid = jnp.arange(byte_count, dtype=jnp.int32) < item_lengths[0]
     ids = jnp.where(valid, byte_ids, -1)
-    spots_first = ids.reshape(patch_count, PATCH).T
-    tables = [embed_table] + [swap(embed_table, "grp", rel) for rel in range(1, groups)]
-    ids_grp = jnp.stack([spots_first] + [swap(spots_first, "grp", rel) for rel in range(1, groups)], axis=1)
-    spot_ids = lax.dynamic_slice_in_dim(ids_grp, me * own_spots, own_spots, 0)
-
-    def moved(numbers):
-        return jnp.where(numbers < 0, -1, numbers ^ (me * vocab_rows))
-
-    near_qkv, near_out, near_up, near_down = (
-        swap(entry, "grp", 1) for entry in (qkv_weight, out_weight, up_weight, down_weight)
-    )
-
-    def block_pieces(at):
-        attend_half = jnp.concatenate([own_half(qkv_weight[at], 1), own_half(out_weight[at], 0)[None]])
-        return (
-            [qkv_weight, out_weight, near_qkv, near_out] + far_pieces(attend_half),
-            [up_weight, near_up] + far_pieces(own_half(up_weight[at], 0)),
-            [down_weight, near_down] + far_pieces(own_half(down_weight[at], 0)),
-        )
-
-    g_attend_w, g_up_w, g_down_w = block_pieces(0)
-    embedded, summary_own, summary_parts = embed(
-        moved(ids)[None], moved(spot_ids).reshape(own_spots, -1), tables, patch_weight, patch_count
-    )
-    arrived = [swap(summary_parts[rel - 1], "grp", rel) for rel in range(1, groups)]
-    l_attend_w, l_up_w, l_down_w = block_pieces(1)
-    patch_w = [patch_weight, swap(patch_weight, "grp", 1)] + far_pieces(own_half(patch_weight, 0))
-
-    ids_all = spot_ids[:, :, None, :]
-    for bit in range(wide_bits):
-        ids_all = jnp.concatenate([ids_all, swap(ids_all, "wide", 1 << bit)], axis=2)
+    extra = jnp.zeros((16, width), BF).at[:, :byte_count].set(ids.astype(BF)[None])
+    load = jnp.concatenate([embed_table, extra])
+    tables = [load] + [swap(load, "grp", rel) for rel in range(1, groups)]
+
+    embedded, partial = embed(place, tables, patch_weight, byte_count)
+
+    def attend_half(at):
+        return jnp.concatenate([own_half(qkv_weight[at], 1), own_half(out_weight[at], 0)[None]])
+
+    g_attend_first = over_chips(attend_half(0))
+    summed = partial[0::2] + swap(partial[1::2], "grp", 1)
+    for bit in reversed(range(1, grp_bits)):
+        half = summed.shape[0] // 2
+        arrived = swap(summed[half:].astype(BF), "grp", 1 << bit).astype(F32)
+        if bit > 1:
+            summed = summed[:half] + arrived
+    near_qkv, near_out = (swap(after(entry, partial), "grp", 1) for entry in (qkv_weight, out_weight))
+    g_up_first = over_chips(after(own_half(up_weight[0], 0), arrived))
+    g_attend_second = over_sides(g_attend_first)
+    g_attend_w = [qkv_weight, out_weight, near_qkv, near_out] + over_cores(g_attend_first, g_attend_second)
+    g_down_first = over_chips(after(own_half(down_weight[0], 0), *g_attend_first, arrived))
+    near_up, near_down = (swap(after(entry, near_qkv), "grp", 1) for entry in (up_weight, down_weight))
+    l_attend_first = over_chips(after(attend_half(1), *g_up_first))
+    g_up_second = over_sides(g_up_first)
+    g_up_w = [up_weight, near_up] + over_cores(g_up_first, g_up_second)
+    l_up_first = over_chips(after(own_half(up_weight[1], 0), *g_down_first))
+    g_down_second = over_sides(g_down_first)
+    g_down_w = [down_weight, near_down] + over_cores(g_down_first, g_down_second)
 
     norm = (norm_gain, norm_bias)
     feed = (norm_gain, norm_bias, up_bias, down_bias)
+    early = after(summed[0], *g_down_first, *g_up_second)
     g_middle, g_qkv, g_mixed, summary = attend_forward(
-        0, chips, patch_count, place, g_attend_w, [summary_own, patch_bias[None]] + arrived, *norm, patch_count, width
-    )
-    local_in = feed_forward(0, chips, place, g_up_w, g_down_w, g_middle, embedded, *feed)
+        0, chips, patch_count, place, g_attend_w, [early, patch_bias[None], arrived[0]], *norm, patch_count, width
+    )
+    l_down_first = over_chips(after(own_half(down_weight[1], 0), *l_attend_first))
+    l_attend_second = over_sides([after(entry, g_middle, *g_down_second) for entry in l_attend_first])
+    l_attend_w = [qkv_weight, out_weight, near_qkv, near_out] + over_cores(l_attend_first, l_attend_second)
+    ids_rows = ids.reshape(patch_count, PATCH).T.reshape(-1, 2 * patch_count).astype(BF)
+    ids_rows = jnp.pad(ids_rows, ((0, 16 - ids_rows.shape[0]), (0, 0)))
+    local_in = feed_forward(
+        0, chips, place, g_up_w, g_down_w, after(g_middle, *l_up_first, *l_attend_second), embedded, *feed
+    )
+    patch_first = over_chips(after(own_half(patch_weight, 0), *l_up_first))
+    l_up_second = over_sides(l_up_first)
+    l_up_w = [up_weight, near_up] + over_cores(l_up_first, l_up_second)
     l_middle, l_qkv, l_mixed = attend_forward(
-        1, chips, PATCH, place, l_attend_w, [local_in], *norm, byte_count, width
-    )
-    l_up, l_down, l_grad, l_feed_vector, local_out = feed_backward(
-        1, chips, True, place, l_up_w, l_down_w, l_middle, out_cot, *feed
-    )
-    l_attend, l_attend_vector, grad_local, grad_global = attend_backward(
-        1, chips, wides, PATCH, True, place, l_attend_w, local_in, l_grad, l_qkv, l_mixed, *norm
-    )
-
+        1, chips, PATCH, place, l_attend_w, [after(local_in, *l_down_first, *l_up_second)], *norm, byte_count, width
+    )
+    l_down_second = over_sides([after(entry, local_in) for entry in l_down_first])
+    l_down_w = [down_weight, near_down] + over_cores(l_down_first, l_down_second)
+    near_patch = swap(after(patch_weight, l_middle), "grp", 1)
+    *l_feed, l_grad, l_feed_vector, local_out = feed_backward(
+        1, chips, wides, True, place, l_up_w, l_down_w, l_middle, out_cot, *feed
+    )
     pair = (2,)
     columns = width // wides
-    lanes = width // chips
-
-    def orders(chip_base, wide_base):
-        chip = [("grp", b + 1, chip_base + chip_bits - 1 - b) for b in range(chip_bits)]
-        wide = [("wide", b, wide_base + wide_bits - 1 - b) for b in range(wide_bits)]
-        return chip, wide
-
-    def reduce_up(term):
-        shaped = term.reshape(pair * (chip_bits + wide_bits) + (2, hidden_width // wides // 2, lanes))
-        chip, wide = orders(0, chip_bits)
-        return reduce_steps(shaped, chip_bits + wide_bits, chip + wide)
-
-    def reduce_down(term):
-        many = hidden_width // lanes // chips // 2
-        shaped = term.reshape(pair * (chip_bits + 1) + (many,) + pair * wide_bits + (columns, lanes))
-        chip, wide = orders(0, chip_bits + 2)
-        return reduce_steps(shaped, chip_bits, wide[:1] + chip + wide[1:])
-
-    def reduce_attend(term, chip_first):
-        shaped = term.reshape(pair * (chip_bits + 2) + pair * wide_bits + (columns, lanes))
-        chip, wide = orders(0, chip_bits + 2)
-        return reduce_steps(shaped, chip_bits, chip + wide if chip_first else wide[:1] + chip + wide[1:])
-
-    l_up = reduce_up(l_up)
-    l_down = reduce_down(l_down)
-    l_attend = reduce_attend(l_attend, True)
-
-    g_up, g_down, g_grad, g_feed_vector = feed_backward(
-        0, chips, False, place, g_up_w, g_down_w, g_middle, grad_global, *feed
-    )
-    g_attend, g_attend_vector, grad_summary, summary_columns = attend_backward(
-        0, chips, wides, patch_count, False, place, g_attend_w, summary, g_grad, g_qkv, g_mixed, *norm
-    )
-    g_up = reduce_up(g_up)
-    g_down = reduce_down(g_down)
-    g_attend = reduce_attend(g_attend, False)
+    chip_steps = [("grp", b) for b in reversed(range(1, grp_bits))]
+    wide_steps = [("wide", b) for b in reversed(range(wide_bits))]
+    near_steps = [("wide", 0)]
+    far_steps = [("wide", b) for b in range(1, wide_bits)]
+    chain = Chain(l_grad)
+
+    def routes(keeps, gots):
+        shape = pair * (chip_bits + wide_bits) + (-1, keeps[0].shape[-1])
+        return [
+            Route(chain, [[keep.reshape(shape), got.reshape(shape)]], chip_steps + wide_steps)
+            for keep, got in zip(keeps, gots)
+        ]
+
+    l_up_keep, l_up_send, l_down_keep, l_down_send = l_feed
+    l_up_got, l_down_got = swap(l_up_send, "grp", 1), swap(l_down_send, "grp", 1)
+    patch_second = over_sides([chain.mark(chain.pin(after(entry, l_middle))) for entry in patch_first])
+    l_attend_keep, l_attend_send, l_attend_vector, grad_local, grad_global = attend_backward(
+        1, chips, wides, PATCH, True, place, l_attend_w, local_in, chain.pin(l_grad), l_qkv, l_mixed, *norm, ids_rows
+    )
+    chain.mark(grad_global)
+
+    def over(route, steps):
+        for step in steps[:-1]:
+            route.start(*step).finish()
+        return route.start(*steps[-1])
+
+    l_up, l_down = routes([l_up_keep, l_down_keep], [l_up_got, l_down_got])
+    l_attend_got = swap(l_attend_send, "grp", 1)
+    over(l_up, chip_steps)
+    over(l_down, near_steps)
+    patch_w = [patch_weight, near_patch] + over_cores(patch_first, patch_second)
+    g_up_keep, g_up_send, g_down_keep, g_down_send, g_grad, g_feed_vector = feed_backward(
+        0, chips, wides, False, place, g_up_w, g_down_w, g_middle, chain.pin(grad_global), *feed
+    )
+    chain.mark(g_grad)
+    (l_attend,) = routes([l_attend_keep], [l_attend_got])
+    over(l_attend, far_steps[:1])
+    g_up_got, g_down_got = swap(g_up_send, "grp", 1), swap(g_down_send, "grp", 1)
+    g_attend_keep, g_attend_send, g_attend_vector, grad_summary, summary_columns = attend_backward(
+        0, chips, wides, patch_count, False, place, g_attend_w, summary, chain.pin(g_grad), g_qkv, g_mixed, *norm, ids_rows
+    )
+    chain.mark(grad_summary)
+    g_attend_got = swap(g_attend_send, "grp", 1)
+    over(l_up.finish(), near_steps)
+    over(l_down.finish(), chip_steps)
+    g_up, g_down = routes([g_up_keep, g_down_keep], [g_up_got, g_down_got])
+    over(l_attend.finish(), chip_steps)
+    over(g_up, chip_steps)
+    over(g_down, near_steps)
+    embed_rows_grad, table_term = patch_backward(
+        chips, vocab, place, patch_w, ids[None], chain.pin(grad_summary), grad_local
+    )
+    chain.mark(embed_rows_grad)
+    (g_attend,) = routes([g_attend_keep], [g_attend_got])
+    over(g_attend, far_steps[:1])
 
     padded = summary_columns.shape[2]
-    collected = summary_columns.reshape(pair * wide_bits + (patch_count, padded))
-    for bit in range(wide_bits):
-        at = wide_bits - 1 - bit
-        mine = bit_at("wide", bit)
-        collected = jnp.concatenate(
-            [pick(collected, mine, at), swap(pick(collected, 1 - mine, at), "wide", 1 << bit)], axis=at
-        )
-    for bit in range(grp_bits):
-        collected = jnp.concatenate([collected, swap(collected, "grp", 1 << bit)], axis=0)
-    patch_weight_grad = patch_weight_term(moved(ids_all).reshape(own_spots, -1), collected, tables, columns)
-
-    embed_rows_grad, table_term = patch_backward(chips, vocab, place, patch_w, ids[None], grad_summary, grad_local)
-    shaped = table_term.reshape(pair * (chip_bits + wide_bits) + (2, columns // 2, vocab // chips))
-    chip, wide = orders(0, chip_bits)
-    table_half = reduce_steps(shaped, chip_bits + wide_bits, chip + wide)
-
     vector = jnp.stack([g_feed_vector, l_feed_vector, g_attend_vector, l_attend_vector])
-    for axis, count in (("grp", grp_bits), ("wide", wide_bits)):
-        for bit in range(count):
-            vector = vector + swap(vector, axis, 1 << bit)
+    shaped = table_term.reshape(pair * (chip_bits + wide_bits + 1) + (columns // 2, vocab // chips))
+
+    class Small:
+        def __init__(self):
+            self.vector = vector
+            self.table = shaped
+            self.table_left = chip_steps + wide_steps + [("grp", 0)]
+            self.columns = summary_columns.reshape(pair * wide_bits + (1,) * (grp_bits + wide_bits) + summary_columns.shape[1:])
+            self.columns_left = list(wide_steps)
+            self.sources = [("grp", b) for b in reversed(range(grp_bits))] + wide_steps
+
+        def step(self, axis, bit):
+            mine = bit_at(axis, bit)
+            at = self.table_left.index((axis, bit))
+            self.table_left.pop(at)
+            table_sent, table_kept = pick(self.table, 1 - mine, at), pick(self.table, mine, at)
+            columns_sent = columns_kept = self.columns
+            if axis == "wide":
+                at = self.columns_left.index((axis, bit))
+                self.columns_left.pop(at)
+                columns_sent, columns_kept = pick(self.columns, 1 - mine, at), pick(self.columns, mine, at)
+            vector_sent = self.vector.astype(BF)
+            parts = (table_sent, vector_sent, columns_sent)
+            sent = jnp.concatenate([chain.pin(part).reshape(-1, 128) for part in parts])
+            chain.mark(sent)
+            got = swap(sent, axis, 1 << bit)
+
+            def finish():
+                arrived = chain.pin(got)
+                base, found = 0, []
+                for part in parts:
+                    count = part.size // 128
+                    found.append(arrived[base : base + count].reshape(part.shape))
+                    base += count
+                table = table_kept.astype(F32) + found[0].astype(F32)
+                self.table = table.astype(BF) if self.table_left else table
+                self.vector = vector_sent.astype(F32) + found[1].astype(F32)
+                at = len(self.columns_left) + self.sources.index((axis, bit))
+                self.columns = jnp.concatenate([columns_kept, found[2]], axis=at)
+                chain.mark(self.vector)
+
+            return finish
+
+    small = Small()
+    small_steps = [("grp", 0)] + list(reversed(far_steps)) + near_steps + list(reversed(chip_steps))
+    pending = small.step(*small_steps.pop(0))
+
+    def small_next():
+        nonlocal pending
+        if pending is not None:
+            pending()
+            pending = small.step(*small_steps.pop(0)) if small_steps else None
+
+    l_both = l_up.finish().join(l_down.finish())
+    over(l_both, far_steps[:1])
+    over(l_attend.finish(), near_steps)
+    small_next()
+    over(g_attend.finish(), chip_steps)
+    over(g_up.finish(), near_steps)
+    over(g_down.finish(), chip_steps)
+    small_next()
+    l_all = l_both.finish().join(l_attend.finish())
+    for step in far_steps[1:]:
+        over(l_all, [step])
+        l_all.finish()
+    over(g_attend.finish(), near_steps)
+    g_both = g_up.finish().join(g_down.finish())
+    over(g_both, far_steps[:1])
+    small_next()
+    small_next()
+    g_all = g_both.finish().join(g_attend.finish())
+    for step in far_steps[1:]:
+        over(g_all, [step])
+        g_all.finish()
+    while pending is not None:
+        small_next()
+    l_up, l_down, l_attend = l_all.totals()
+    g_up, g_down, g_attend = g_all.totals()
+    table_half = small.table
+    vector = small.vector
+    patch_weight_grad = patch_weight_term(
+        place, own_spots, patch_count, small.columns.reshape(groups * wides, -1, padded), tables, columns
+    )
     pieces = hidden_width // width
     feed_vector, attend_vector = vector[:2], vector[2:]
     patch_bias_grad = attend_vector[0, 2]
@@ -814,34 +1004,38 @@
     up_bias_grad = feed_vector[:, :pieces].reshape(2, hidden_width)
     down_bias_grad = feed_vector[:, pieces + 2]
 
-    def split_lanes(half):
+    def join(half):
         lanes_half = half.shape[-1] // 2
-        low, high = half[..., :lanes_half], half[..., lanes_half:]
+        low, high = half[:, :lanes_half], half[:, lanes_half:]
         mine = jnp.where(core == 0, low, high)
-        return mine, swap(jnp.where(core == 0, high, low), "grp", 1)
-
-    def join(half, axis):
-        mine, other = split_lanes(half)
-        return jnp.where(core == 0, jnp.concatenate([mine, other], axis), jnp.concatenate([other, mine], axis))
-
-    def finish_down(half):
-        return jnp.swapaxes(half, 1, 2).reshape(-1, columns)
-
-    g_attend = jnp.swapaxes(join(g_attend, 0), 1, 2)
-    l_attend = jnp.swapaxes(join(l_attend, 0), 1, 2)
+        other = swap(jnp.where(core == 0, high, low), "grp", 1)
+        return jnp.where(core == 0, jnp.stack([mine, other]), jnp.stack([other, mine]))
+
+    def finish(up, down, attend):
+        rows = up.shape[0]
+        joined = join(jnp.concatenate([up, attend]))
+        up = joined[:, :rows].reshape(2 * rows, -1).T
+        attend = jnp.swapaxes(joined[:, rows:].reshape(4, columns, -1), 1, 2)
+        down = jnp.swapaxes(down.reshape(-1, columns, down.shape[-1]), 1, 2).reshape(-1, columns)
+        return up, down, attend
+
+    l_up, l_down, l_attend = finish(l_up, l_down, l_attend)
+    g_up, g_down, g_attend = finish(g_up, g_down, g_attend)
+    table_grad = table_half.reshape(columns // 2, -1)
+    table_grad = join(table_grad).reshape(columns, -1).T
     return (
         local_out,
         embed_rows_grad,
-        join(table_half, 0).T,
+        table_grad,
         patch_weight_grad,
         patch_bias_grad,
         norm_gain_grad,
         norm_bias_grad,
         jnp.stack([g_attend[:3], l_attend[:3]]),
         jnp.stack([g_attend[3], l_attend[3]]),
-        jnp.stack([join(g_up, 0).T, join(l_up, 0).T]),
+        jnp.stack([g_up, l_up]),
         up_bias_grad,
-        jnp.stack([finish_down(g_down), finish_down(l_down)]),
+        jnp.stack([g_down, l_down]),
         down_bias_grad,
     )
 

time: 555 us -> 495 us (0.89)
  waiting for transfers between devices: 270 us -> 162 us
  other arithmetic: 23.1 us -> 76.8 us
  starting transfers between devices: 77 us -> 57.1 us
  Pallas kernels: 111 us -> 121 us
    ppermute x95 -> x70, waiting for transfers between devices: 270 us -> 162 us  [swap(): lax.ppermute(value, axis, [(i, i ^ mask) for i in range(lax.axis_size(axi...]
    convert_element_type x28 -> x31, other arithmetic: 17.4 us -> 48.7 us  [the longest x23 47.1 us: start(): self.total([pick(term, 1 - mine, at) for term in part]).astype(BF)]
    ppermute x95 -> x70, starting transfers between devices: 77 us -> 57.1 us  [swap(): lax.ppermute(value, axis, [(i, i ^ mask) for i in range(lax.axis_size(axi...]
    squeeze x35 -> x17, local copies, waits for them, and re-layouts: 21.4 us -> 7.03 us  [pick(): return lax.dynamic_index_in_dim(value, index, axis, keepdims=False)]
    pallas_call x5, Pallas kernels: 75.9 us -> 84.1 us  [the longest x2 43.8 us: feed_backward(): pl.pallas_call(functools.partial(feed_backward_kernel, block, chips, wide...]
    add x10 -> x11, other arithmetic: 0.21 us -> 8.35 us  [the longest x4 5.93 us: total(): value = value + term.astype(F32)]
    concatenate x7 -> x14, other arithmetic: 0.99 us -> 7.64 us  [the longest x4 3.37 us: start(): sent = sent[0] if len(sent) == 1 else jnp.concatenate(sent, axis=-2)]
    convert_element_type x0 -> x10, local copies, waits for them, and re-layouts: none -> 6.64 us  [the longest x3 4.07 us: body(): ids.reshape(patch_count, PATCH).T.reshape(-1, 2 * patch_count).astype(BF)]
  transfers between devices with their start and end apart: 95 -> 70, of which waited for: 41 -> 18; matrix products, arithmetic and copies ran while one was open for 13% -> 22% of each run, Pallas kernels for 20% -> 25%
where the time goes in v3:
time: 495 us; the launch traced here: 486 us
  waiting for transfers between devices  162 us (33%)
  Pallas kernels  121 us (24%)
  other arithmetic  76.8 us (16%)
  local copies, waits for them, and re-layouts  64.6 us (13%)
  starting transfers between devices  57.1 us (12%)
    ppermute x70, waiting for transfers between devices, swap(): lax.ppermute(value, axis, [(i, i ^ mask) for i in range(lax.axis_size(axi...  162 us
    ppermute x70, starting transfers between devices, swap(): lax.ppermute(value, axis, [(i, i ^ mask) for i in range(lax.axis_size(axi...  57.1 us
    convert_element_type x23, other arithmetic, start(): self.total([pick(term, 1 - mine, at) for term in part]).astype(BF)  47.1 us
    pallas_call x2, Pallas kernels, feed_backward(): pl.pallas_call(functools.partial(feed_backward_kernel, block, chips, wide...  43.8 us
    pallas_call x2, Pallas kernels, attend_backward(): pl.pallas_call(functools.partial(attend_backward_kernel, block, chips, wi...  33.5 us
    unnamed x233, local copies, waits for them, and re-layouts  21.6 us
    pallas_call x2, Pallas kernels, attend_forward(): pl.pallas_call(functools.partial(attend_forward_kernel, block, chips, spa...  16.8 us
  transfers between devices with their start and end apart: 70, of which 18 were waited for; matrix products, arithmetic and copies ran while one was open for 22% of the time, Pallas kernels for 25%

profile of v3, /device:TPU:0, one launch (start us, length us, event | category | flops | bytes accessed | tf_op | source)
XLA Modules:
  0.0 485.6 jit_solution(2261363587871830562)
XLA Ops:
  16.5 4.0 embed.1
  24.5 6.5 %collective-permute-done.5.refs_5_ = bf16[4,96,768]{2,1,0:T(8,128)(2,1)} collective-permute-done((bf16[4,96,768]{2,1,0:T(8,128)(2,1)}, bf16[4,96,768]{2,1,0:T(8,128)(2,1)}, u32[]{:S(2)}, u32[]{:S(2)}) %collective-permute-start.5) | collective-permute-done | bytes 589856 | tf_op jit(solution)/shard_map/ppermute | solution.py:48
  38.3 7.3 %collective-permute-done.24.refs_6_ = bf16[4,96,768]{2,1,0:T(8,128)(2,1)} collective-permute-done((bf16[4,96,768]{2,1,0:T(8,128)(2,1)}, bf16[4,96,768]{2,1,0:T(8,128)(2,1)}, u32[]{:S(2)}, u32[]{:S(2)}) %collective-permute-start.24) | collective-permute-done | bytes 589856 | tf_op jit(solution)/shard_map/ppermute | solution.py:48
  52.3 8.5 %collective-permute-done.8.refs_9_ = bf16[384,768]{1,0:T(8,128)(2,1)S(1)} collective-permute-done((bf16[384,768]{1,0:T(8,128)(2,1)S(1)}, bf16[384,768]{1,0:T(8,128)(2,1)S(1)}, u32[]{:S(2)}, u32[]{:S(2)}) %collective-permute-start.8) | collective-permute-done | bytes 589856 | tf_op jit(solution)/shard_map/ppermute | solution.py:48
  68.1 10.7 %collective-permute-done.20.refs_10_ = bf16[384,768]{1,0:T(8,128)(2,1)S(1)} collective-permute-done((bf16[384,768]{1,0:T(8,128)(2,1)S(1)}, bf16[384,768]{1,0:T(8,128)(2,1)S(1)}, u32[]{:S(2)}, u32[]{:S(2)}) %collective-permute-start.20) | collective-permute-done | bytes 589856 | tf_op jit(solution)/shard_map/ppermute | solution.py:48
  79.7 5.1 %attend_forward_0.1 = (f32[64,768]{1,0:T(8,128)S(1)}, bf16[3,64,768]{2,1,0:T(8,128)(2,1)S(1)}, bf16[64,768]{1,0:T(8,128)(2,1)S(1)}, f32[64,768]{1,0:T(8,128)S(1)}) custom-call(s32[3]{0:T(128)S(1)} %pad_add_fusion.refs_0_, bf16[2,3,192,768]{3,2,1,0:T(8,128)(2,1)} %refs_1_.14, bf16[2,192,768]{2,1,0:T(8,128)(2,1)S(1)} %copy-done.1, ...), custom_call_target="tpu_custom_call" | custom-call | flops 1 | bytes 18450000 | tf_op jit(solution)/shard_map/attend_forward_0/pallas_call | solution.py:252
  90.6 10.1 %collective-permute-done.27.refs_6_ = bf16[4,96,768]{2,1,0:T(8,128)(2,1)} collective-permute-done((bf16[4,96,768]{2,1,0:T(8,128)(2,1)}, bf16[4,96,768]{2,1,0:T(8,128)(2,1)}, u32[]{:S(2)}, u32[]{:S(2)}) %collective-permute-start.27) | collective-permute-done | bytes 589856 | tf_op jit(solution)/shard_map/ppermute | solution.py:48
  106.3 8.0 %feed_forward_0.1.refs_9_ = bf16[512,768]{1,0:T(8,128)(2,1)} custom-call(s32[3]{0:T(128)S(1)} %pad_add_fusion.refs_0_, bf16[2,192,3072]{2,1,0:T(8,128)(2,1)} %refs_1_.13, bf16[2,192,3072]{2,1,0:T(8,128)(2,1)} %copy-done.45, bf16[96,3072]{1,0:T(8,128)(2,1)} %collective-permute-done.14.refs_3_, bf16[96,3072]{1,0:T(8,128)(2,1)S(1)} %collective-permute-done.17.refs_4_, ...), custom_call_target="tpu_custom_call" | custom-call | flops 1 | bytes 29520000 | tf_op jit(solution)/shard_map/feed_forward_0/pallas_call | solution.py:307
  115.8 14.5 %collective-permute-done.28.refs_10_ = bf16[384,768]{1,0:T(8,128)(2,1)} collective-permute-done((bf16[384,768]{1,0:T(8,128)(2,1)}, bf16[384,768]{1,0:T(8,128)(2,1)}, u32[]{:S(2)}, u32[]{:S(2)}) %collective-permute-start.28) | collective-permute-done | bytes 589856 | tf_op jit(solution)/shard_map/ppermute | solution.py:48
  132.0 11.7 %attend_forward_1.1 = (f32[512,768]{1,0:T(8,128)}, bf16[3,512,768]{2,1,0:T(8,128)(2,1)}, bf16[512,768]{1,0:T(8,128)(2,1)}) custom-call(s32[3]{0:T(128)S(1)} %pad_add_fusion.refs_0_, bf16[2,3,192,768]{3,2,1,0:T(8,128)(2,1)} %refs_1_.14, bf16[2,192,768]{2,1,0:T(8,128)(2,1)S(1)} %copy-done.1, bf16[2,3,192,768]{3,2,1,0:T(8,128)(2,1)} %collective-permute-done.3.refs_3_, ...), custom_call_target="tpu_custom_call" | custom-call | flops 1 | bytes 40590000 | tf_op jit(solution)/shard_map/attend_forward_1/pallas_call | solution.py:252
  145.1 27.9 %feed_backward_1.1 = (bf16[2,1536,384]{2,1,0:T(8,128)(2,1)}, bf16[2,1536,384]{2,1,0:T(8,128)(2,1)}, bf16[2,1536,384]{2,1,0:T(8,128)(2,1)}, bf16[2,1536,384]{2,1,...) custom-call(s32[3]{0:T(128)} %copy-done.33, bf16[2,192,3072]{2,1,0:T(8,128)(2,1)} %refs_1_.13, ...), custom_call_target="tpu_custom_call" | custom-call | flops 1 | bytes 95940000 | tf_op jit(solution)/shard_map/feed_backward_1/pallas_call | solution.py:438
  179.0 23.0 %attend_backward_1.1 = (bf16[2,1536,384]{2,1,0:T(8,128)(2,1)}, bf16[2,1536,384]{2,1,0:T(8,128)(2,1)}, f32[8,768]{1,0:T(8,128)S(1)}, bf16[512,768]{1,0:T(8,128)(2,1)}, f32[64,768]{1,0:T(8,128)S(1)}) custom-call(s32[3]{0:T(128)S(1)} %copy-done.34, bf16[2,3,192,768]{3,2,1,0:T(8,128)(2,1)} %refs_1_.14, bf16[2,192,768]{2,1,0:T(8,128)(2,1)S(1)} %copy-done.1, ...), custom_call_target="tpu_custom_call" | custom-call | flops 1 | bytes 81180000 | tf_op jit(solution)/shard_map/attend_backward_1/pallas_call | solution.py:543
  203.8 3.1 fusion
  212.7 16.0 %feed_backward_0.1 = (bf16[2,1536,384]{2,1,0:T(8,128)(2,1)}, bf16[2,1536,384]{2,1,0:T(8,128)(2,1)}, bf16[2,1536,384]{2,1,0:T(8,128)(2,1)}, bf16[2,1536,384]{2,1,...) custom-call(s32[3]{0:T(128)} %copy-done.33, bf16[2,192,3072]{2,1,0:T(8,128)(2,1)} %refs_1_.13, ...), custom_call_target="tpu_custom_call" | custom-call | flops 1 | bytes 55350000 | tf_op jit(solution)/shard_map/feed_backward_0/pallas_call | solution.py:438
  235.6 10.5 %attend_backward_0.1 = (bf16[2,1536,384]{2,1,0:T(8,128)(2,1)}, bf16[2,1536,384]{2,1,0:T(8,128)(2,1)}, f32[8,768]{1,0:T(8,128)S(1)}, bf16[64,768]{1,0:T(8,128)(2,1)S(1)}, bf16[8,80,128]{2,1,0:T(8,128)(2,1)S(1)}) custom-call(s32[3]{0:T(128)S(1)} %copy-done.35, bf16[2,3,192,768]{3,2,1,0:T(8,128)(2,1)} %refs_1_.14, bf16[2,192,768]{2,1,0:T(8,128)(2,1)S(1)} %copy-done.1, ...), custom_call_target="tpu_custom_call" | custom-call | flops 1 | bytes 36900000 | tf_op jit(solution)/shard_map/attend_backward_0/pallas_call | solution.py:543
  246.4 10.9 %collective-permute-done.42 = bf16[2,2,2,192,384]{4,3,2,1,0:T(8,128)(2,1)} collective-permute-done((bf16[2,2,2,192,384]{4,3,2,1,0:T(8,128)(2,1)}, bf16[2,2,2,192,384]{4,3,2,1,0:T(8,128)(2,1)}, u32[]{:S(2)}, u32[]{:S(2)}) %collective-permute-start.42) | collective-permute-done | bytes 1179680 | tf_op jit(solution)/shard_map/ppermute | solution.py:48
  265.1 13.1 %collective-permute-done.49 = bf16[2,2,192,384]{3,2,0,1:T(8,128)(2,1)S(1)} collective-permute-done((bf16[2,2,192,384]{3,2,0,1:T(8,128)(2,1)S(1)}, bf16[2,2,192,384]{3,2,0,1:T(8,128)(2,1)S(1)}, u32[]{:S(2)}, u32[]{:S(2)}) %collective-permute-start.49) | collective-permute-done | bytes 589856 | tf_op jit(solution)/shard_map/ppermute | solution.py:48
  295.6 8.5 %patch_backward.1 = (bf16[512,768]{1,0:T(8,128)(2,1)}, bf16[2,768,128]{2,1,0:T(8,128)(2,1)S(1)}) custom-call(s32[3]{0:T(128)S(1)} %copy-done.35, bf16[1536,768]{1,0:T(8,128)(2,1)} %refs_1_.15, bf16[1536,768]{1,0:T(8,128)(2,1)} %copy-done.69, bf16[768,768]{1,0:T(8,128)(2,1)} %collective-permute-done.34.refs_3_, ...), custom_call_target="tpu_custom_call" | custom-call | flops 1 | bytes 29520000 | tf_op jit(solution)/shard_map/patch_backward/pallas_call | solution.py:640
  317.3 26.2 %collective-permute-done.57 = bf16[2,192,384]{2,1,0:T(8,128)(2,1)S(1)} collective-permute-done((bf16[2,192,384]{2,1,0:T(8,128)(2,1)S(1)}, bf16[2,192,384]{2,1,0:T(8,128)(2,1)S(1)}, u32[]{:S(2)}, u32[]{:S(2)}) %collective-permute-start.57) | collective-permute-done | bytes 294944 | tf_op jit(solution)/shard_map/ppermute | solution.py:48
  351.1 14.3 %collective-permute-done.56 = bf16[2,384,384]{2,1,0:T(8,128)(2,1)} collective-permute-done((bf16[2,384,384]{2,1,0:T(8,128)(2,1)}, bf16[2,384,384]{2,1,0:T(8,128)(2,1)}, u32[]{:S(2)}, u32[]{:S(2)}) %collective-permute-start.56) | collective-permute-done | bytes 589856 | tf_op jit(solution)/shard_map/ppermute | solution.py:48
  397.7 12.9 %collective-permute-done.68 = bf16[576,384]{1,0:T(8,128)(2,1)} collective-permute-done((bf16[576,384]{1,0:T(8,128)(2,1)}, bf16[576,384]{1,0:T(8,128)(2,1)}, u32[]{:S(2)}, u32[]{:S(2)}) %collective-permute-start.68) | collective-permute-done | bytes 442400 | tf_op jit(solution)/shard_map/ppermute | solution.py:48
  433.7 5.0 %collective-permute-done.61 = bf16[928,128]{1,0:T(8,128)(2,1)} collective-permute-done((bf16[928,128]{1,0:T(8,128)(2,1)}, bf16[928,128]{1,0:T(8,128)(2,1)}, u32[]{:S(2)}, u32[]{:S(2)}) %collective-permute-start.61) | collective-permute-done | bytes 237600 | tf_op jit(solution)/shard_map/ppermute | solution.py:48
  453.2 13.0 %collective-permute-done.66 = bf16[576,384]{1,0:T(8,128)(2,1)} collective-permute-done((bf16[576,384]{1,0:T(8,128)(2,1)}, bf16[576,384]{1,0:T(8,128)(2,1)}, u32[]{:S(2)}, u32[]{:S(2)}) %collective-permute-start.66) | collective-permute-done | bytes 442400 | tf_op jit(solution)/shard_map/ppermute | solution.py:48
  470.2 6.8 %patch_weight_term.1 = f32[1536,96]{1,0:T(8,128)S(1)} custom-call(s32[3]{0:T(128)S(1)} %copy-done.35, bf16[32,80,128]{2,1,0:T(8,128)(2,1)S(1)} %bitcast.546, bf16[80,768]{1,0:T(8,128)(2,1)S(1)} %copy-done.7, bf16[80,768]{1,0:T(8,128)(2,1)S(1)} %copy-done.19, bf16[80,768]{1,0:T(8,128)(2,1)S(1)} %copy-done.21, bf16[80,768]{1,0:T(8,128)(2,1)S(1)} %copy-done.23), custom_call_target="tpu_custom_call" | custom-call | flops 1 | bytes 14760000 | tf_op jit(solution)/shard_map/patch_weight_term/pallas_call | solution.py:694
  (516 shorter events, 204.6 us)
Async XLA Ops:
  20.7 29.4 %collective-permute-start.3 = (bf16[2,3,192,768]{3,2,1,0:T(8,128)(2,1)}, bf16[2,3,192,768]{3,2,1,0:T(8,128)(2,1)}, u32[]{:S(2)}, u32[]{:S(2)}) collective-permute-start(bf16[2,3,192,768]{3,2,1,0:T(8,128)(2,1)} %refs_1_.14), channel_id=1, source_target_pairs={{0,8},{8,0},{16,24},{24,16},{1,9},{9,1},{17,25},{25,17},{2,10},{10... | collective-permute-start | bytes 5308424 | tf_op jit(solution)/shard_map/ppermute | solution.py:48
  51.6 52.3 %collective-permute-start.13 = (bf16[2,768,768]{2,1,0:T(8,128)(2,1)}, bf16[2,768,768]{2,1,0:T(8,128)(2,1)S(1)}, u32[]{:S(2)}, u32[]{:S(2)}) collective-permute-start(bf16[2,768,768]{2,1,0:T(8,128)(2,1)} %refs_7_.5), channel_id=1, source_target_pairs={{0,8},{8,0},{16,24},{24,16},{1,9},{9,1},{17,25},{25,17},{2,10},{10... | collective-permute-start | bytes 7077896 | tf_op jit(solution)/shard_map/ppermute | solution.py:48
  51.9 52.1 %collective-permute-start.4 = (bf16[2,192,3072]{2,1,0:T(8,128)(2,1)}, bf16[2,192,3072]{2,1,0:T(8,128)(2,1)S(1)}, u32[]{:S(2)}, u32[]{:S(2)}) collective-permute-start(bf16[2,192,3072]{2,1,0:T(8,128)(2,1)} %refs_1_.13), channel_id=1, source_target_pairs={{0,8},{8,0},{16,24},{24,16},{1,9},{9,1},{17,25},{25,17},{2,10},{10... | collective-permute-start | bytes 7077896 | tf_op jit(solution)/shard_map/ppermute | solution.py:48
  114.9 28.8 %collective-permute-start.11 = (bf16[96,3072]{1,0:T(8,128)(2,1)}, bf16[96,3072]{1,0:T(8,128)(2,1)S(1)}, u32[]{:S(2)}, u32[]{:S(2)}) collective-permute-start(bf16[96,3072]{1,0:T(8,128)(2,1)} %collective-permute-done.9.refs_3_), channel_id=1, source_target_pairs={{0,8},{8,0},{16,24},{24,16},{1,9},{9,1},{17,25},{25,17},{2,10},{10... | collective-permute-start | bytes 1769480 | tf_op jit(solution)/shard_map/ppermute | solution.py:48
  115.3 28.4 %collective-permute-start.29 = (bf16[384,768]{1,0:T(8,128)(2,1)}, bf16[384,768]{1,0:T(8,128)(2,1)S(1)}, u32[]{:S(2)}, u32[]{:S(2)}) collective-permute-start(bf16[384,768]{1,0:T(8,128)(2,1)} %collective-permute-done.16.refs_9_), channel_id=1, source_target_pairs={{0,8},{8,0},{16,24},{24,16},{1,9},{9,1},{17,25},{25,17},{2,10},{10... | collective-permute-start | bytes 1769480 | tf_op jit(solution)/shard_map/ppermute | solution.py:48
  131.5 46.8 %collective-permute-start.34 = (bf16[768,768]{1,0:T(8,128)(2,1)}, bf16[768,768]{1,0:T(8,128)(2,1)}, u32[]{:S(2)}, u32[]{:S(2)}) collective-permute-start(bf16[768,768]{1,0:T(8,128)(2,1)} %constant_dynamic-slice_fusion.8), channel_id=1, source_target_pairs={{0,16},{8,24},{16,0},{24,8},{1,17},{9,25},{17,1},{25,9},{2,18},{10... | collective-permute-start | bytes 3538952 | tf_op jit(solution)/shard_map/ppermute | solution.py:48
  172.9 30.9 %collective-permute-start.38 = (bf16[2,1536,384]{2,1,0:T(8,128)(2,1)}, bf16[2,1536,384]{2,1,0:T(8,128)(2,1)}, u32[]{:S(2)}, u32[]{:S(2)}) collective-permute-start(bf16[2,1536,384]{2,1,0:T(8,128)(2,1)} %get-tuple-element.151), channel_id=1, source_target_pairs={{0,8},{8,0},{16,24},{24,16},{1,9},{9,1},{17,25},{25,17},{2,10},{10... | collective-permute-start | bytes 7077896 | tf_op jit(solution)/shard_map/ppermute | solution.py:48
  173.2 35.2 %collective-permute-start.39 = (bf16[2,1536,384]{2,1,0:T(8,128)(2,1)}, bf16[2,1536,384]{2,1,0:T(8,128)(2,1)}, u32[]{:S(2)}, u32[]{:S(2)}) collective-permute-start(bf16[2,1536,384]{2,1,0:T(8,128)(2,1)} %get-tuple-element.153), channel_id=1, source_target_pairs={{0,8},{8,0},{16,24},{24,16},{1,9},{9,1},{17,25},{25,17},{2,10},{10... | collective-permute-start | bytes 7077896 | tf_op jit(solution)/shard_map/ppermute | solution.py:48
  203.5 29.9 %collective-permute-start.35 = (bf16[768,768]{1,0:T(8,128)(2,1)}, bf16[768,768]{1,0:T(8,128)(2,1)}, u32[]{:S(2)}, u32[]{:S(2)}) collective-permute-start(bf16[768,768]{1,0:T(8,128)(2,1)} %collective-permute-done.34.refs_3_), channel_id=1, source_target_pairs={{0,1},{1,0},{2,3},{3,2},{4,5},{5,4},{6,7},{7,6},{8,9},{9,8},{10,11... | collective-permute-start | bytes 3538952 | tf_op jit(solution)/shard_map/ppermute | solution.py:48
  206.9 39.1 %collective-permute-start.41 = (bf16[2,2,2,192,384]{4,3,2,1,0:T(8,128)(2,1)}, bf16[2,2,2,192,384]{4,3,2,1,0:T(8,128)(2,1)}, u32[]{:S(2)}, u32[]{:S(2)}) collective-permute-start(bf16[2,2,2,192,384]{4,3,2,1,0:T(8,128)(2,1)} %fusion), channel_id=1, source_target_pairs={{0,16},{8,24},{16,0},{24,8},{1,17},{9,25},{17,1},{25,9},{2,18},{10... | collective-permute-start | bytes 3538952 | tf_op jit(solution)/shard_map/ppermute | solution.py:48
  211.0 46.3 %collective-permute-start.42 = (bf16[2,2,2,192,384]{4,3,2,1,0:T(8,128)(2,1)}, bf16[2,2,2,192,384]{4,3,2,1,0:T(8,128)(2,1)}, u32[]{:S(2)}, u32[]{:S(2)}) collective-permute-start(bf16[2,2,2,192,384]{4,3,2,1,0:T(8,128)(2,1)} %fusion.1), channel_id=1, source_target_pairs={{0,1},{1,0},{2,3},{3,2},{4,5},{5,4},{6,7},{7,6},{8,9},{9,8},{10,11... | collective-permute-start | bytes 3538952 | tf_op jit(solution)/shard_map/ppermute | solution.py:48
  228.7 49.6 %collective-permute-start.44 = (bf16[2,1536,384]{2,1,0:T(8,128)(2,1)}, bf16[2,1536,384]{2,1,0:T(8,128)(2,1)}, u32[]{:S(2)}, u32[]{:S(2)}) collective-permute-start(bf16[2,1536,384]{2,1,0:T(8,128)(2,1)} %get-tuple-element.169), channel_id=1, source_target_pairs={{0,8},{8,0},{16,24},{24,16},{1,9},{9,1},{17,25},{25,17},{2,10},{10... | collective-permute-start | bytes 7077896 | tf_op jit(solution)/shard_map/ppermute | solution.py:48
  231.9 31.6 %collective-permute-start.43 = (bf16[2,2,2,192,384]{4,3,2,1,0:T(8,128)(2,1)}, bf16[2,2,2,192,384]{4,3,2,1,0:T(8,128)(2,1)}, u32[]{:S(2)}, u32[]{:S(2)}) collective-permute-start(bf16[2,2,2,192,384]{4,3,2,1,0:T(8,128)(2,1)} %fusion.2), channel_id=1, source_target_pairs={{0,2},{1,3},{2,0},{3,1},{4,6},{5,7},{6,4},{7,5},{8,10},{9,11},{10,... | collective-permute-start | bytes 3538952 | tf_op jit(solution)/shard_map/ppermute | solution.py:48
  233.4 55.6 %collective-permute-start.45 = (bf16[2,1536,384]{2,1,0:T(8,128)(2,1)}, bf16[2,1536,384]{2,1,0:T(8,128)(2,1)}, u32[]{:S(2)}, u32[]{:S(2)}) collective-permute-start(bf16[2,1536,384]{2,1,0:T(8,128)(2,1)} %get-tuple-element.171), channel_id=1, source_target_pairs={{0,8},{8,0},{16,24},{24,16},{1,9},{9,1},{17,25},{25,17},{2,10},{10... | collective-permute-start | bytes 7077896 | tf_op jit(solution)/shard_map/ppermute | solution.py:48
  246.1 47.6 %collective-permute-start.33 = (bf16[1536,768]{1,0:T(8,128)(2,1)S(1)}, bf16[1536,768]{1,0:T(8,128)(2,1)S(1)}, u32[]{:S(2)}, u32[]{:S(2)}) collective-permute-start(bf16[1536,768]{1,0:T(8,128)(2,1)S(1)} %copy-done), channel_id=1, source_target_pairs={{0,8},{8,0},{16,24},{24,16},{1,9},{9,1},{17,25},{25,17},{2,10},{10... | collective-permute-start | bytes 7077896 | tf_op jit(solution)/shard_map/ppermute | solution.py:48
  257.3 46.7 %collective-permute-start.46 = (bf16[2,1536,384]{2,1,0:T(8,128)(2,1)}, bf16[2,1536,384]{2,1,0:T(8,128)(2,1)}, u32[]{:S(2)}, u32[]{:S(2)}) collective-permute-start(bf16[2,1536,384]{2,1,0:T(8,128)(2,1)} %get-tuple-element.178), channel_id=1, source_target_pairs={{0,8},{8,0},{16,24},{24,16},{1,9},{9,1},{17,25},{25,17},{2,10},{10... | collective-permute-start | bytes 7077896 | tf_op jit(solution)/shard_map/ppermute | solution.py:48
  293.7 78.6 %collective-permute-start.53 = (bf16[2,2,2,192,384]{4,3,2,1,0:T(8,128)(2,1)}, bf16[2,2,2,192,384]{4,3,2,1,0:T(8,128)(2,1)}, u32[]{:S(2)}, u32[]{:S(2)}) collective-permute-start(bf16[2,2,2,192,384]{4,3,2,1,0:T(8,128)(2,1)} %fusion.3), channel_id=1, source_target_pairs={{0,16},{8,24},{16,0},{24,8},{1,17},{9,25},{17,1},{25,9},{2,18},{10... | collective-permute-start | bytes 3538952 | tf_op jit(solution)/shard_map/ppermute | solution.py:48
  306.7 63.1 %collective-permute-start.52 = (bf16[2,2,2,192,384]{4,3,2,1,0:T(8,128)(2,1)}, bf16[2,2,2,192,384]{4,3,2,1,0:T(8,128)(2,1)}, u32[]{:S(2)}, u32[]{:S(2)}) collective-permute-start(bf16[2,2,2,192,384]{4,3,2,1,0:T(8,128)(2,1)} %fusion.5), channel_id=1, source_target_pairs={{0,2},{1,3},{2,0},{3,1},{4,6},{5,7},{6,4},{7,5},{8,10},{9,11},{10,... | collective-permute-start | bytes 3538952 | tf_op jit(solution)/shard_map/ppermute | solution.py:48
  308.5 37.3 %collective-permute-start.47 = (bf16[1600,128]{1,0:T(8,128)(2,1)S(1)}, bf16[1600,128]{1,0:T(8,128)(2,1)S(1)}, u32[]{:S(2)}, u32[]{:S(2)}) collective-permute-start(bf16[1600,128]{1,0:T(8,128)(2,1)S(1)} %pad_maximum_fusion.10), channel_id=1, source_target_pairs={{0,8},{8,0},{16,24},{24,16},{1,9},{9,1},{17,25},{25,17},{2,10},{10... | collective-permute-start | bytes 1228808 | tf_op jit(solution)/shard_map/ppermute | solution.py:48
  308.6 66.1 %collective-permute-start.54 = (bf16[2,2,2,192,384]{4,3,2,1,0:T(8,128)(2,1)}, bf16[2,2,2,192,384]{4,3,2,1,0:T(8,128)(2,1)}, u32[]{:S(2)}, u32[]{:S(2)}) collective-permute-start(bf16[2,2,2,192,384]{4,3,2,1,0:T(8,128)(2,1)} %fusion.4), channel_id=1, source_target_pairs={{0,1},{1,0},{2,3},{3,2},{4,5},{5,4},{6,7},{7,6},{8,9},{9,8},{10,11... | collective-permute-start | bytes 3538952 | tf_op jit(solution)/shard_map/ppermute | solution.py:48
  313.9 29.6 %collective-permute-start.57 = (bf16[2,192,384]{2,1,0:T(8,128)(2,1)S(1)}, bf16[2,192,384]{2,1,0:T(8,128)(2,1)S(1)}, u32[]{:S(2)}, u32[]{:S(2)}) collective-permute-start(bf16[2,192,384]{2,1,0:T(8,128)(2,1)S(1)} %fusion.15), channel_id=1, source_target_pairs={{0,1},{1,0},{2,3},{3,2},{4,5},{5,4},{6,7},{7,6},{8,9},{9,8},{10,11... | collective-permute-start | bytes 884744 | tf_op jit(solution)/shard_map/ppermute | solution.py:48
  348.4 28.6 %collective-permute-start.51 = (bf16[1216,128]{1,0:T(8,128)(2,1)S(1)}, bf16[1216,128]{1,0:T(8,128)(2,1)S(1)}, u32[]{:S(2)}, u32[]{:S(2)}) collective-permute-start(bf16[1216,128]{1,0:T(8,128)(2,1)S(1)} %pad_maximum_fusion.15), channel_id=1, source_target_pairs={{0,4},{1,5},{2,6},{3,7},{4,0},{5,1},{6,2},{7,3},{8,12},{9,13},{10,... | collective-permute-start | bytes 933896 | tf_op jit(solution)/shard_map/ppermute | solution.py:48
  392.0 29.1 %collective-permute-start.59 = (bf16[2,2,192,384]{3,2,1,0:T(8,128)(2,1)}, bf16[2,2,192,384]{3,2,1,0:T(8,128)(2,1)}, u32[]{:S(2)}, u32[]{:S(2)}) collective-permute-start(bf16[2,2,192,384]{3,2,1,0:T(8,128)(2,1)} %fusion.7), channel_id=1, source_target_pairs={{0,1},{1,0},{2,3},{3,2},{4,5},{5,4},{6,7},{7,6},{8,9},{9,8},{10,11... | collective-permute-start | bytes 1769480 | tf_op jit(solution)/shard_map/ppermute | solution.py:48
  394.6 28.7 %collective-permute-start.55 = (bf16[1024,128]{1,0:T(8,128)(2,1)}, bf16[1024,128]{1,0:T(8,128)(2,1)}, u32[]{:S(2)}, u32[]{:S(2)}) collective-permute-start(bf16[1024,128]{1,0:T(8,128)(2,1)} %pad_maximum_fusion.16), channel_id=1, source_target_pairs={{0,2},{1,3},{2,0},{3,1},{4,6},{5,7},{6,4},{7,5},{8,10},{9,11},{10,... | collective-permute-start | bytes 786440 | tf_op jit(solution)/shard_map/ppermute | solution.py:48
  (159 other events, 2019.9 us)
